TPU v7x, 512 devices: a whole 4x4x16 slice. The times are simulated.
512 devices in a mesh: lat: 16 (over x, y_lo, core), lon: 32 (over y_hi, z).
Axes of the slice: x: 4, y: 4 (y_hi: 2, y_lo: 2; y = y_hi * 2 + y_lo), z: 16, core: 2. Of those that a mesh axis runs over, the one named last changes fastest.
Arguments:
- tokens: bfloat16 [4, 96, 384, 384], P(None, 'lat', 'lon'), may hold values from -6 to 6
- position_index: int32 [144, 144], replicated, may hold values from 0 to 3311
- gain_first: float32 [384], replicated, may hold values from 0.1 to 1.9
- qkv_first: bfloat16 [384, 1152], replicated, may hold values from -0.3125 to 0.3125
- proj_first: bfloat16 [384, 384], replicated, may hold values from -0.8984375 to 0.8984375
- bias_first: bfloat16 [16, 2, 12, 3312], P('lat'), may hold values from -4 to 4
- gain_second: float32 [384], replicated, may hold values from 0.1 to 1.9
- qkv_second: bfloat16 [384, 1152], replicated, may hold values from -0.3125 to 0.3125
- proj_second: bfloat16 [384, 384], replicated, may hold values from -0.8984375 to 0.8984375
- bias_second: bfloat16 [16, 2, 12, 3312], P('lat'), may hold values from -4 to 4
Outputs:
- mixed: bfloat16 [4, 96, 384, 384], P(None, 'lat', 'lon')
All inputs are finite; a program needn't handle non-finite values.
Results may differ from a plain program's by a relative error of at most 0.015.
Values may be sent and summed in bfloat16 or wider, within the bound.
No kernel may reach another device: no remote copies, remote signals or barrier semaphores. Data moves between devices by JAX's collectives and lax.ppermute only.
A program may use at most 64 MiB of HBM per device.

v0:
```python
import jax
import jax.numpy as jnp
from jax import lax
from jax.sharding import PartitionSpec as P


def passed_along(block, axis, distance):
    devices = range(lax.axis_size(axis))
    route = [((i - distance) % len(devices), i) for i in devices]
    return lax.ppermute(block, axis, route)


def from_behind(array, axis, by):
    size = lax.axis_size(axis)
    pairs = [(i, i + by) for i in range(size) if 0 <= i + by < size]
    return lax.ppermute(array, axis, pairs)


def expand_bias(table, position_index):
    types, lwin, heads, entries = table.shape
    columns = table.reshape(types * lwin * heads, entries).T
    picked = jnp.take(columns, position_index.reshape(-1), axis=0)
    picked = picked.reshape(144, 144, types, lwin, heads)
    return picked.transpose(2, 3, 4, 0, 1)


def window_block(grid, valid, side, table, position_index, gain, w_qkv, w_proj):
    levels, rows, cols, width = grid.shape
    heads = table.shape[2]
    head_dim = width // heads
    rwin = rows // 6
    lwin = levels // 2
    cwin = cols // 12
    values = grid.astype(jnp.float32)
    center = jnp.mean(values, axis=-1, keepdims=True)
    spread = jnp.mean((values - center) ** 2, axis=-1, keepdims=True)
    normed = ((values - center) * lax.rsqrt(spread + 1e-05) * gain).astype(jnp.bfloat16)
    qkv = jnp.dot(normed.reshape(-1, width), w_qkv, preferred_element_type=jnp.float32).astype(
        jnp.bfloat16
    )
    qkv = qkv.reshape(lwin, 2, rwin, 6, cwin, 12, 3 * width).transpose(2, 0, 4, 1, 3, 5, 6)
    qkv = qkv.reshape(rwin, lwin, cwin, 144, 3 * width)
    val_win = jnp.broadcast_to(valid.reshape(rwin, 1, 1, 6, 1), (rwin, lwin, 2, 6, 12)).reshape(
        rwin, lwin, 144
    )
    side_win = jnp.broadcast_to(side.reshape(1, lwin, 2, 1, 1), (rwin, lwin, 2, 6, 12)).reshape(
        rwin, lwin, 144
    )
    same = side_win[..., :, None] == side_win[..., None, :]
    mask = same & val_win[..., None, :] | jnp.eye(144, dtype=bool)
    bias = expand_bias(table, position_index)
    query = qkv[..., :width].reshape(rwin, lwin, cwin, 144, heads, head_dim)
    key = qkv[..., width : 2 * width].reshape(rwin, lwin, cwin, 144, heads, head_dim)
    value = qkv[..., 2 * width :].reshape(rwin, lwin, cwin, 144, heads, head_dim)
    scores = jnp.einsum(
        "rlcqhd,rlckhd->rlchqk", query, key, preferred_element_type=jnp.float32
    ) * head_dim ** (-0.5)
    scores = scores + bias[:, :, None]
    expd = jnp.exp(jnp.where(mask[:, :, None, None], scores, -1e30))
    probs = (expd / jnp.sum(expd, axis=-1, keepdims=True)).astype(jnp.bfloat16)
    attended = jnp.einsum(
        "rlchqk,rlckhd->rlcqhd", probs, value, preferred_element_type=jnp.float32
    ).astype(jnp.bfloat16)
    attended = attended.reshape(rwin, lwin, cwin, 2, 6, 12, width).transpose(1, 3, 0, 4, 2, 5, 6)
    attended = attended.reshape(-1, width)
    update = jnp.dot(attended, w_proj, preferred_element_type=jnp.float32).reshape(values.shape)
    return (values + update).astype(jnp.bfloat16)


def shards(
    tokens,
    position_index,
    gain_first,
    qkv_first,
    proj_first,
    bias_first,
    gain_second,
    qkv_second,
    proj_second,
    bias_second,
):
    levels, rows, cols, width = tokens.shape
    first = window_block(
        tokens,
        jnp.ones((rows,), bool),
        jnp.zeros((levels,), bool),
        bias_first,
        position_index,
        gain_first,
        qkv_first,
        proj_first,
    )
    neighbour = passed_along(first, "lon", -1)
    lon_frame = jnp.concatenate([first[:, :, 6:], neighbour[:, :, :6]], axis=2)
    below = from_behind(lon_frame, "lat", -1)[:, :3]
    rolled = jnp.roll(jnp.concatenate([lon_frame[:, 3:], below], axis=1), -1, axis=0)
    lat_pos = lax.axis_index("lat")
    global_rows = lat_pos * rows + 3 + jnp.arange(rows)
    valid = global_rows < rows * lax.axis_size("lat")
    side = jnp.arange(levels) == levels - 1
    main = window_block(
        rolled, valid, side, bias_second, position_index, gain_second, qkv_second, proj_second
    )
    block = jnp.concatenate(
        [jnp.zeros((levels, 3, cols, width), jnp.bfloat16), lon_frame[:, :3]], axis=1
    )
    block = jnp.roll(block, -1, axis=0)
    polar_valid = jnp.arange(6) >= 3
    result = window_block(
        block, polar_valid, side, bias_second, position_index, gain_second, qkv_second, proj_second
    )
    northern = result[:, 3:]
    main = jnp.roll(main, 1, axis=0)
    northern = jnp.roll(northern, 1, axis=0)
    above = from_behind(main, "lat", 1)[:, rows - 3 :]
    top_rows = jnp.where(lat_pos == 0, northern, above)
    lon_back = jnp.concatenate([top_rows, main[:, : rows - 3]], axis=1)
    before = passed_along(lon_back, "lon", 1)[:, :, cols - 6 :]
    return jnp.concatenate([before, lon_back[:, :, : cols - 6]], axis=2)


def solution(mesh):
    return jax.shard_map(
        shards,
        mesh=mesh,
        in_specs=(
            P(None, "lat", "lon", None),
            P(),
            P(),
            P(),
            P(),
            P("lat", None, None, None),
            P(),
            P(),
            P(),
            P("lat", None, None, None),
        ),
        out_specs=P(None, "lat", "lon", None),
        check_vma=False,
    )
```

profile of v0, /device:TPU:11, one launch (start us, length us, event | category | flops | bytes accessed | tf_op | source)
XLA Modules:
  0.0 215.3 jit_solution(16479940504831260941)
XLA Ops:
  0.0 1.1 reshape.279
  1.2 0.9 copy.56
  2.2 0.4 copy.57
  2.6 42.0 %gather_fusion = bf16[20736,24]{1,0:T(8,128)(2,1)} fusion(bf16[3312,24]{1,0:T(8,128)(2,1)S(1)} %bitcast.87, s32[21504]{0:T(1024)S(1)} %pad_clamp_fusion), kind=kCustom, calls=%fused_computation.clone | custom fusion | bytes 2073600 | tf_op jit(solution)/shard_map/jit(_take)/gather | solution.py:22
  44.7 5.7 %copy.58 = bf16[20736,24]{0,1:T(8,128)(2,1)} copy(bf16[20736,24]{1,0:T(8,128)(2,1)} %gather_fusion) | data formatting | bytes 1990656 | tf_op jit(solution)/shard_map/jit(_take)/gather | solution.py:22
  50.5 0.4 copy.66
  50.9 42.0 %gather_fusion.1 = bf16[20736,24]{1,0:T(8,128)(2,1)} fusion(bf16[3312,24]{1,0:T(8,128)(2,1)S(1)} %bitcast.86, s32[21504]{0:T(1024)S(1)} %pad_clamp_fusion), kind=kCustom, calls=%fused_computation.1.clone | custom fusion | bytes 2073600 | tf_op jit(solution)/shard_map/jit(_take)/gather | solution.py:22
  92.9 5.7 %copy.67 = bf16[20736,24]{0,1:T(8,128)(2,1)} copy(bf16[20736,24]{1,0:T(8,128)(2,1)} %gather_fusion.1) | data formatting | bytes 1990656 | tf_op jit(solution)/shard_map/jit(_take)/gather | solution.py:22
  98.6 3.2 %select_convert_fusion = (f32[20736,24]{0,1:T(8,128)S(1)}, f32[20736,24]{0,1:T(8,128)}) fusion(bf16[20736,24]{0,1:T(8,128)(2,1)} %copy.67, pred[20736]{0:T(1024)(128)(4,1)S(1)} %compare_and_fusion.2, bf16[20736,24]{0,1:T(8,128)(2,1)} %copy.58), kind=kLoop, calls=%fused_computation.34 | loop fusion | flops 1990656 | bytes 5992704 | tf_op jit(solution)/shard_map/convert_element_type | solution.py:58
  101.8 5.0 %reshape.291 = f32[144,144,1,2,12]{1,0,4,3,2:T(8,128)} reshape(f32[20736,24]{0,1:T(8,128)} %get-tuple-element.22) | data formatting | bytes 3981312 | tf_op jit(solution)/shard_map/convert_element_type | solution.py:58
  106.7 5.6 %copy.59 = f32[144,144,1,2,12]{0,1,4,3,2:T(8,128)} copy(f32[144,144,1,2,12]{1,0,4,3,2:T(8,128)} %reshape.291) | data formatting | bytes 3981312 | tf_op jit(solution)/shard_map/convert_element_type | solution.py:58
  112.5 0.2 fusion.22
  113.0 0.7 reshape.274
  113.7 1.8 convolution_convert_fusion.2
  115.5 0.9 fusion.49
  116.4 1.1 copy.54
  117.5 1.9 copy.55
  119.3 1.8 copy.53
  121.2 4.7 %fusion = f32[2,12,144,144]{2,3,1,0:T(8,128)} fusion(f32[144,144,1,2,12]{0,1,4,3,2:T(8,128)} %copy.59, bf16[2,144,12,32]{1,3,2,0:T(8,128)(2,1)S(1)} %bitcast.95, bf16[2,144,12,32]{1,3,2,0:T(8,128)(2,1)} %bitcast.96), kind=kOutput, calls=%fused_computation.3 | convolution fusion | flops 32845824 | bytes 4423680 | tf_op jit(solution)/shard_map/rlcqhd,rlckhd->rlchqk/dot_general | solution.py:55
  125.9 3.8 %fusion.19 = bf16[1,2,1,144,12,32]{3,5,4,1,2,0:T(8,128)(2,1)S(1)} fusion(bf16[2,144,12,32]{1,3,2,0:T(8,128)(2,1)} %bitcast.98, f32[2,12,144,144]{2,3,1,0:T(8,128)} %fusion), kind=kOutput, calls=%fused_computation.33 | convolution fusion | flops 32960016 | bytes 2433024 | tf_op jit(solution)/shard_map/rlchqk,rlckhd->rlcqhd/dot_general | solution.py:61
  129.7 1.8 copy.61
  131.5 2.1 dot_general.45
  133.7 2.0 fusion.14
  135.7 13.0 %collective-permute-start = (bf16[4,6,12,384]{3,2,1,0:T(8,128)(2,1)}, bf16[4,6,12,384]{3,2,1,0:T(8,128)(2,1)S(1)}, u32[]{:S(2)}, u32[]{:S(2)}) collective-permute-start(bf16[4,6,12,384]{3,2,1,0:T(8,128)(2,1)} %fusion.14), channel_id=1, source_target_pairs={{1,0},{2,1},{3,2},{4,3},{5,4},{6,5},{7,6},{8,7},{9,8},{10,9},{11,1... | collective-permute-start | bytes 663560 | tf_op jit(solution)/shard_map/ppermute | solution.py:10
  148.7 1.0 slice.120
  149.8 4.3 %reshape.292 = f32[144,144,1,2,12]{1,0,4,3,2:T(8,128)} reshape(f32[20736,24]{0,1:T(8,128)S(1)} %get-tuple-element.21) | data formatting | bytes 3981312 | tf_op jit(solution)/shard_map/convert_element_type | solution.py:58
  154.1 5.6 %copy.68 = f32[144,144,1,2,12]{0,1,4,3,2:T(8,128)} copy(f32[144,144,1,2,12]{1,0,4,3,2:T(8,128)} %reshape.292) | data formatting | bytes 3981312 | tf_op jit(solution)/shard_map/convert_element_type | solution.py:58
  160.6 2.9 %collective-permute-start.1 = (bf16[4,6,12,384]{3,2,1,0:T(8,128)(2,1)S(1)}, bf16[4,6,12,384]{3,2,1,0:T(8,128)(2,1)S(1)}, u32[]{:S(2)}, u32[]{:S(2)}) collective-permute-start(bf16[4,6,12,384]{3,2,1,0:T(8,128)(2,1)S(1)} %pad_maximum_fusion), channel_id=1, source_target_pairs={{32,0},{64,32},{96,64},{128,96},{160,128},{192,160},{224,192},{256... | collective-permute-start | bytes 663560 | tf_op jit(solution)/shard_map/ppermute | solution.py:16
  163.6 6.1 %collective-permute-done.1 = bf16[4,6,12,384]{3,2,1,0:T(8,128)(2,1)S(1)} collective-permute-done((bf16[4,6,12,384]{3,2,1,0:T(8,128)(2,1)S(1)}, bf16[4,6,12,384]{3,2,1,0:T(8,128)(2,1)S(1)}, u32[]{:S(2)}, u32[]{:S(2)}) %collective-permute-start.1) | collective-permute-done | bytes 221216 | tf_op jit(solution)/shard_map/ppermute | solution.py:16
  170.0 0.2 multiply_reduce_fusion
  170.5 0.6 convolution_convert_fusion
  171.7 4.8 %fusion.4 = f32[2,12,144,144]{2,3,1,0:T(8,128)} fusion(f32[144,144,1,2,12]{0,1,4,3,2:T(8,128)} %copy.68, bf16[2,144,12,32]{1,3,2,0:T(8,128)(2,1)S(1)} %bitcast.93, bf16[2,144,12,32]{1,3,2,0:T(8,128)(2,1)S(1)} %bitcast.94, pred[2,144,144]{1,2,0:T(8,128)(4,1)S(1)} %get-tuple-element.20), kind=kOutput, calls=%fused_computation.9 | convolution fusion | flops 33343488 | bytes 4465152 | tf_op jit(solution)/shard_map/rlcqhd,rlckhd->rlchqk/dot_general | solution.py:55
  176.6 3.8 %fusion.17 = bf16[1,2,1,144,12,32]{3,5,4,1,2,0:T(8,128)(2,1)S(1)} fusion(bf16[2,144,12,32]{1,3,2,0:T(8,128)(2,1)S(1)} %bitcast.99, f32[2,12,144,144]{2,3,1,0:T(8,128)} %fusion.4), kind=kOutput, calls=%fused_computation.31 | convolution fusion | flops 32960016 | bytes 2433024 | tf_op jit(solution)/shard_map/rlchqk,rlckhd->rlcqhd/dot_general | solution.py:61
  180.3 0.9 copy.75
  181.2 0.8 dot_general.55
  182.1 1.3 fusion.16
  183.6 0.2 multiply_reduce_fusion.1
  184.2 0.6 convolution_convert_fusion.1
  185.4 4.8 %fusion.2 = f32[2,12,144,144]{2,3,1,0:T(8,128)} fusion(f32[144,144,1,2,12]{0,1,4,3,2:T(8,128)} %copy.68, bf16[2,144,12,32]{1,3,2,0:T(8,128)(2,1)S(1)} %bitcast.91, bf16[2,144,12,32]{1,3,2,0:T(8,128)(2,1)S(1)} %bitcast.92, pred[2,144,144]{1,2,0:T(8,128)(4,1)S(1)} %get-tuple-element.19), kind=kOutput, calls=%fused_computation.7 | convolution fusion | flops 33343488 | bytes 4465152 | tf_op jit(solution)/shard_map/rlcqhd,rlckhd->rlchqk/dot_general | solution.py:55
  190.2 3.7 %fusion.18 = bf16[1,2,1,144,12,32]{3,5,4,1,2,0:T(8,128)(2,1)S(1)} fusion(bf16[2,144,12,32]{1,3,2,0:T(8,128)(2,1)S(1)} %bitcast.97, f32[2,12,144,144]{2,3,1,0:T(8,128)} %fusion.2), kind=kOutput, calls=%fused_computation.32 | convolution fusion | flops 32960016 | bytes 2433024 | tf_op jit(solution)/shard_map/rlchqk,rlckhd->rlcqhd/dot_general | solution.py:61
  193.9 0.9 copy.70
  194.8 0.8 dot_general.50
  195.7 1.9 collective-permute-start.2
  197.7 0.3 fusion.15
  198.1 3.2 %collective-permute-done.2 = bf16[4,6,12,384]{3,2,1,0:T(8,128)(2,1)S(1)} collective-permute-done((bf16[4,6,12,384]{3,2,1,0:T(8,128)(2,1)S(1)}, bf16[4,6,12,384]{3,2,1,0:T(8,128)(2,1)S(1)}, u32[]{:S(2)}, u32[]{:S(2)}) %collective-permute-start.2) | collective-permute-done | bytes 221216 | tf_op jit(solution)/shard_map/ppermute | solution.py:16
  201.4 1.9 collective-permute-start.3
  203.4 11.0 %collective-permute-done.3 = bf16[4,6,12,384]{3,2,1,0:T(8,128)(2,1)S(1)} collective-permute-done((bf16[4,6,12,384]{3,2,1,0:T(8,128)(2,1)S(1)}, bf16[4,6,12,384]{3,2,1,0:T(8,128)(2,1)S(1)}, u32[]{:S(2)}, u32[]{:S(2)}) %collective-permute-start.3) | collective-permute-done | bytes 221216 | tf_op jit(solution)/shard_map/ppermute | solution.py:10
  214.5 0.8 copy.76
  (72 shorter events, 4.0 us)
Async XLA Ops:
  0.0 170.5 %copy-start = (bf16[384,1152]{1,0:T(8,128)(2,1)S(1)}, bf16[384,1152]{1,0:T(8,128)(2,1)}, u32[]{:S(2)}) copy-start(bf16[384,1152]{1,0:T(8,128)(2,1)} %param.19) | copy-start | bytes 2654212
  44.7 5.7 %copy-start.3 = (bf16[1,2,12,3312]{3,1,2,0:T(2,128)(2,1)S(1)}, bf16[1,2,12,3312]{3,1,2,0:T(2,128)(2,1)}, u32[]{:S(2)}) copy-start(bf16[1,2,12,3312]{3,1,2,0:T(2,128)(2,1)} %param.21) | copy-start | bytes 476932
  106.7 5.6 %copy-start.1 = (bf16[4,6,12,384]{3,0,2,1:T(4,128)(2,1)S(1)}, bf16[4,6,12,384]{3,0,2,1:T(4,128)(2,1)}, u32[]{:S(2)}) copy-start(bf16[4,6,12,384]{3,0,2,1:T(4,128)(2,1)} %param.12) | copy-start | bytes 663556
  106.7 6.1 %copy-start.5 = (f32[384]{0:T(512)S(1)}, f32[384]{0:T(512)}, u32[]{:S(2)}) copy-start(f32[384]{0:T(512)} %param.14) | copy-start | bytes 4612
  135.7 24.7 %collective-permute-start = (bf16[4,6,12,384]{3,2,1,0:T(8,128)(2,1)}, bf16[4,6,12,384]{3,2,1,0:T(8,128)(2,1)S(1)}, u32[]{:S(2)}, u32[]{:S(2)}) collective-permute-start(bf16[4,6,12,384]{3,2,1,0:T(8,128)(2,1)} %fusion.14), channel_id=1, source_target_pairs={{1,0},{2,1},{3,2},{4,3},{5,4},{6,5},{7,6},{8,7},{9,8},{10,9},{11,1... | collective-permute-start | bytes 663560 | tf_op jit(solution)/shard_map/ppermute | solution.py:10
  159.7 10.8 %copy-start.4 = (f32[384]{0:T(512)S(1)}, f32[384]{0:T(512)}, u32[]{:S(2)}) copy-start(f32[384]{0:T(512)} %param.18) | copy-start | bytes 4612
  160.6 9.1 %collective-permute-start.1 = (bf16[4,6,12,384]{3,2,1,0:T(8,128)(2,1)S(1)}, bf16[4,6,12,384]{3,2,1,0:T(8,128)(2,1)S(1)}, u32[]{:S(2)}, u32[]{:S(2)}) collective-permute-start(bf16[4,6,12,384]{3,2,1,0:T(8,128)(2,1)S(1)} %pad_maximum_fusion), channel_id=1, source_target_pairs={{32,0},{64,32},{96,64},{128,96},{160,128},{192,160},{224,192},{256... | collective-permute-start | bytes 663560 | tf_op jit(solution)/shard_map/ppermute | solution.py:16
  193.9 3.8 %copy-start.2 = (bf16[384,384]{1,0:T(8,128)(2,1)S(1)}, bf16[384,384]{1,0:T(8,128)(2,1)}, u32[]{:S(2)}) copy-start(bf16[384,384]{1,0:T(8,128)(2,1)} %param.20) | copy-start | bytes 884740
  195.7 5.6 %collective-permute-start.2 = (bf16[4,6,12,384]{3,2,1,0:T(8,128)(2,1)S(1)}, bf16[4,6,12,384]{3,2,1,0:T(8,128)(2,1)S(1)}, u32[]{:S(2)}, u32[]{:S(2)}) collective-permute-start(bf16[4,6,12,384]{3,2,1,0:T(8,128)(2,1)S(1)} %pad_maximum_fusion.1), channel_id=1, source_target_pairs={{0,32},{32,64},{64,96},{96,128},{128,160},{160,192},{192,224},{224... | collective-permute-start | bytes 663560 | tf_op jit(solution)/shard_map/ppermute | solution.py:16
  201.4 12.9 %collective-permute-start.3 = (bf16[4,6,12,384]{3,2,1,0:T(8,128)(2,1)S(1)}, bf16[4,6,12,384]{3,2,1,0:T(8,128)(2,1)S(1)}, u32[]{:S(2)}, u32[]{:S(2)}) collective-permute-start(bf16[4,6,12,384]{3,2,1,0:T(8,128)(2,1)S(1)} %pad_maximum_fusion.2), channel_id=1, source_target_pairs={{31,0},{0,1},{1,2},{2,3},{3,4},{4,5},{5,6},{6,7},{7,8},{8,9},{9,10... | collective-permute-start | bytes 663560 | tf_op jit(solution)/shard_map/ppermute | solution.py:10
where the time goes:
time: 218 us; the launch traced here: 215 us
  local copies, waits for them, and re-layouts  137 us (63%)
  matrix products  32.2 us (15%)
  waiting for transfers between devices  20.3 us (9%)
  starting transfers between devices  19.7 us (9%)
  other arithmetic  5.42 us (2%)
    gather x4, local copies, waits for them, and re-layouts, expand_bias(): picked = jnp.take(columns, position_index.reshape(-1), axis=0)  95.4 us
    convert_element_type x4, local copies, waits for them, and re-layouts, window_block(): scores = scores + bias[:, :, None]  20.5 us
    ppermute x2, starting transfers between devices, passed_along(): return lax.ppermute(block, axis, route)  14.9 us
    dot_general x3, matrix products, window_block(): jnp.einsum('rlcqhd,rlckhd->rlchqk', query, key, preferred_element_type=jn...  14.3 us
    dot_general x3, matrix products, window_block(): jnp.einsum('rlchqk,rlckhd->rlcqhd', probs, value, preferred_element_type=...  11.3 us
    ppermute x2, waiting for transfers between devices, passed_along(): return lax.ppermute(block, axis, route)  11 us
    ppermute x2, waiting for transfers between devices, from_behind(): return lax.ppermute(array, axis, pairs)  9.36 us
    ppermute x2, starting transfers between devices, from_behind(): return lax.ppermute(array, axis, pairs)  4.79 us
  transfers between devices with their start and end apart: 4, of which 3 were waited for; matrix products, arithmetic and copies ran while one was open for 6% of the time, Pallas kernels for 0%

commit v1 on v0

v1 whole, which is shorter than its diff:
```python
import functools

import jax
import jax.numpy as jnp
import numpy as np
from jax import lax
from jax.experimental import pallas as pl
from jax.experimental.pallas import tpu as pltpu
from jax.sharding import PartitionSpec as P

F32, BF16, I32 = jnp.float32, jnp.bfloat16, jnp.int32
HEADS = 12
D = 384
WIN = 144
CHUNKS = 26
LOG2E = float(np.log2(np.e))
FIX = 8191.0
SCALE = LOG2E * 32 ** -0.5
UNFIX = LOG2E / FIX


def dot(a, b):
    return jnp.dot(a, b, preferred_element_type=F32)


def dot_t(a, b):
    return lax.dot_general(a, b, (((1,), (1,)), ((), ())), preferred_element_type=F32)


def one_hot_rows(rows, width):
    out = np.zeros((len(rows), width), np.float32)
    for i, r in enumerate(rows):
        if r >= 0:
            out[i, r] = 1
    return out.astype(jnp.bfloat16)


LEVEL = [[1, 2], [3, 0]]


def compact_from_padded():
    return one_hot_rows([g * 16 + c for g in range(24) for c in range(12)], 384)


def quadrants_from_compact():
    rows = []
    for b in range(2):
        for a in range(2):
            for w in range(2):
                for lo in range(2):
                    for r in range(3):
                        for c in range(6):
                            rows.append(LEVEL[w][lo] * 72 + (3 * a + r) * 12 + 6 * b + c)
    return one_hot_rows(rows, 288)


def keys_from_pieces():
    return one_hot_rows(
        [80 * piece + 36 * w + t for w in range(2) for piece in range(4) for t in range(36)], 320
    )


def queries_from_quadrants():
    rows = []
    for a in range(2):
        for b in range(2):
            for w in range(2):
                rows += [((b * 2 + a) * 2 + w) * 36 + t for t in range(36)] + [-1] * 4
    return one_hot_rows(rows, 288)


def padded_from_queries():
    rows = []
    for l in range(4):
        w, lo = [(1, 1), (0, 0), (0, 1), (1, 0)][l]
        for r in range(6):
            for c in range(16):
                if c >= 12:
                    rows.append(-1)
                    continue
                a, b = r // 3, c // 6
                rows.append(((a * 2 + b) * 2 + w) * 40 + lo * 18 + (r % 3) * 6 + c % 6)
    return one_hot_rows(rows, 320)


def tail_copies(columns):
    order = list(columns[:128]) + list(columns[128:]) * 8
    return np.ascontiguousarray(one_hot_rows(order, WIN).T)


def tail_rows(tiles):
    packed = -(-tiles // 8)
    out = np.zeros((packed * 8, tiles * 8), np.float32)
    for t in range(tiles):
        for s in range(8):
            out[(t // 8) * 8 + s, t * 8 + s] = 1
    return out.astype(jnp.bfloat16)


def shifted_positions(a, b):
    queries = [
        72 * lo + 12 * (3 * (1 - a) + r) + 6 * (1 - b) + c
        for lo in range(2)
        for r in range(3)
        for c in range(6)
    ]
    keys = []
    for near_row, near_col in ((1, 1), (1, 0), (0, 1), (0, 0)):
        row0 = 3 * (1 - a) if near_row else 3 * a
        col0 = 6 * (1 - b) if near_col else 6 * b
        keys += [
            72 * lo + 12 * (row0 + r) + col0 + c
            for lo in range(2)
            for r in range(3)
            for c in range(6)
        ]
    return queries, keys


def pack_table(top, bottom, packed_ref):
    first = jnp.round(top.astype(F32) * FIX).astype(I32)
    second = jnp.round(bottom.astype(F32) * FIX).astype(I32)
    packed_ref[:, 0 : top.shape[1]] = (first << 16) | (second & 0xFFFF)


def split_index(position_index):
    high = (position_index >> 7).astype(F32).astype(BF16)
    low = (position_index & 127).astype(F32).astype(BF16)
    return high, low


def fold_tail(values, gather_rows, tiles):
    row = lax.broadcasted_iota(I32, values.shape, 0) // 8
    lane = lax.broadcasted_iota(I32, values.shape, 1) // 16
    kept = jnp.where((row % 8) == lane, values, 0.0).astype(BF16)
    return dot(gather_rows, kept)


def place_index(part, columns, gather_rows, dst_ref, start, tiles):
    spread = dot(part, columns)
    rows = tiles * 8
    dst_ref[start : start + rows, :] = spread[:, :128].astype(I32)
    tail = fold_tail(spread[:, 128:], gather_rows, tiles)
    dst_ref[start + rows : start + rows + tail.shape[0], :] = tail.astype(I32)


def expand(packed_ref, high_ref, low_ref, out_ref, start, count):
    def tile(t, carry):
        rows = pl.ds(pl.multiple_of(start + t * 8, 8), 8)
        low = low_ref[rows, :]
        high = high_ref[rows, :]
        picked = [None] * HEADS
        for c in range(CHUNKS):
            here = high == c
            for h in range(HEADS):
                entries = jnp.broadcast_to(packed_ref[h : h + 1, 128 * c : 128 * c + 128], (8, 128))
                got = jnp.take_along_axis(entries, low, axis=1, mode="promise_in_bounds")
                picked[h] = got if c == 0 else jnp.where(here, got, picked[h])
        for h in range(HEADS):
            out_ref[h, rows, :] = picked[h]
        return carry

    lax.fori_loop(0, count, tile, 0)


def bias_tail(bias_ref, h, base, tiles):
    out = []
    for t in range(tiles):
        at = base + (t // 8) * 8
        part = bias_ref[h, at : at + 8, :]
        j = t % 8
        out.append(part if j == 0 else pltpu.roll(part, 128 - 16 * j, 1))
    return jnp.concatenate(out, axis=0)


def upper(packed):
    return (packed >> 16).astype(F32)


def lower(packed):
    return ((packed << 16) >> 16).astype(F32)


def layer_norm(values, gain):
    center = jnp.mean(values, axis=-1, keepdims=True)
    moved = values - center
    spread = jnp.mean(moved * moved, axis=-1, keepdims=True)
    return (moved * lax.rsqrt(spread + 1e-05) * gain).astype(BF16)


def head_masks(shape):
    lane = lax.broadcasted_iota(I32, shape, 1) // 32
    return [lane == i for i in range(4)]


def softmax(scores, mask):
    raised = jnp.where(mask, jnp.exp2(scores), 0.0)
    total = jnp.sum(raised, axis=-1, keepdims=True)
    step = jnp.where(total > 1.0, 0.25, 1.0)
    return ((raised * step) * (1.0 / (total * step))).astype(BF16)


def first_kernel(
    tok_ref, idx_ref, gain_ref, wqkv_ref, wo_ref, table_ref, gain2_ref,
    perm_ref, quad_ref, cols_ref, tailrows_ref,
    first_ref, west_ref, east_ref,
    padded, packed, high_ref, low_ref, bias_ref, kpad, vpad,
):
    pack_table(table_ref[0, 0], table_ref[0, 1], packed)
    high, low = split_index(idx_ref[...])
    place_index(high, cols_ref[...], tailrows_ref[...], high_ref, 0, 18)
    place_index(low, cols_ref[...], tailrows_ref[...], low_ref, 0, 18)
    expand(packed, high_ref, low_ref, bias_ref, 0, 21)

    padded[...] = jnp.zeros_like(padded)
    for g in range(24):
        padded[16 * g : 16 * g + 12, :] = tok_ref[g]
    values = dot(perm_ref[...], padded[...])
    normed = layer_norm(values, gain_ref[...])
    qkv = dot(normed, wqkv_ref[...]).astype(BF16)

    kpad[...] = jnp.zeros_like(kpad)
    vpad[...] = jnp.zeros_like(vpad)
    for w in range(2):
        rows = slice(WIN * w, WIN * w + WIN)
        kpad[w, 0:WIN, :] = qkv[rows, D : 2 * D]
        vpad[w, 0:WIN, :] = qkv[rows, 2 * D :]

    qmasks = head_masks((WIN, 128))
    vmasks = head_masks((256, 128))
    valid = lax.broadcasted_iota(I32, (WIN, 256), 1) < WIN
    zero = jnp.zeros((), BF16)
    mixed = [[None] * 3, [None] * 3]
    for g in range(3):
        lanes = slice(128 * g, 128 * g + 128)
        biases = []
        for i in range(4):
            h = 4 * g + i
            biases.append(
                jnp.concatenate([bias_ref[h, 0:WIN, :], bias_tail(bias_ref, h, WIN, 18)], axis=1)
            )
        for w in range(2):
            query = qkv[WIN * w : WIN * w + WIN, lanes]
            key = kpad[w, :, lanes]
            value = vpad[w, :, lanes]
            total = None
            for i in range(4):
                scores = dot_t(jnp.where(qmasks[i], query, zero), key)
                bias = upper(biases[i]) if w == 0 else lower(biases[i])
                probs = softmax(scores * SCALE + bias * UNFIX, valid)
                part = dot(probs, jnp.where(vmasks[i], value, zero))
                total = part if total is None else total + part
            mixed[w][g] = total.astype(BF16)
    attended = jnp.concatenate([jnp.concatenate(row, axis=1) for row in mixed], axis=0)
    first = (values + dot(attended, wo_ref[...])).astype(BF16)
    first_ref[...] = first
    again = layer_norm(first.astype(F32), gain2_ref[...])
    parts = dot(quad_ref[...], again).astype(BF16)
    for a in range(2):
        west_ref[a] = parts[72 * a : 72 * a + 72]
        east_ref[a] = parts[144 + 72 * a : 144 + 72 * a + 72]


SIDE_ROWS = 80
SIDE_TILES = 12


def bias_kernel(
    idx_ref, table_ref, before_ref, pick_ref, cols_ref, tailrows_ref,
    bias_ref,
    packed, high_ref, low_ref,
):
    pack_table(before_ref[0, 0], before_ref[0, 1], packed.at[0])
    pack_table(table_ref[0, 0], table_ref[0, 1], packed.at[1])
    high, low = split_index(idx_ref[...])
    for part, dst in ((high, high_ref), (low, low_ref)):
        rows = dot(pick_ref[...], part).astype(BF16)
        for a in range(2):
            spread = jnp.concatenate(
                [
                    dot(rows[40 * q : 40 * q + 40], cols_ref[q])
                    for q in (2 * a, 2 * a + 1)
                ],
                axis=0,
            )
            start = a * 96
            dst[start : start + 80, :] = spread[:, :128].astype(I32)
            tail = fold_tail(spread[:, 128:], tailrows_ref[...], 10)
            dst[start + 80 : start + 96, :] = tail.astype(I32)
    for a in range(2):
        expand(packed.at[a], high_ref, low_ref, bias_ref, a * 96, SIDE_TILES)


def second_kernel(
    edge_ref,
    first_ref, west_ref, east_ref, from_west_ref, from_east_ref, north_ref, south_ref,
    wqkv_ref, wo_ref, bias_ref,
    keys_ref, queries_ref, unperm_ref, pad_ref,
    out_ref,
    cat, qbuf, kpad, vpad, obuf,
):
    own = (west_ref, east_ref)
    beside = (from_west_ref, from_east_ref)
    beyond = (north_ref, south_ref)
    tokens = jnp.concatenate([west_ref[0], west_ref[1], east_ref[0], east_ref[1]], axis=0)
    asked = dot(queries_ref[...], tokens).astype(BF16)
    qbuf[...] = dot(asked, wqkv_ref[:, 0:D]).astype(BF16).astype(F32)

    cat[...] = jnp.zeros_like(cat)
    kpad[...] = jnp.zeros_like(kpad)
    vpad[...] = jnp.zeros_like(vpad)
    for a in range(2):
        for b in range(2):
            q = 2 * a + b
            far = ((1, 0), (2, 3))[b]
            cat[q, 0:72, :] = own[b][a]
            cat[q, 80:152, :] = beside[b][a]
            cat[q, 160:232, :] = beyond[a][far[0]]
            cat[q, 240:312, :] = beyond[a][far[1]]
            window = dot(keys_ref[...], cat[q]).astype(BF16)
            kv = dot(window, wqkv_ref[:, D:]).astype(BF16)
            for w in range(2):
                rows = slice(WIN * w, WIN * w + WIN)
                kpad[2 * q + w, 0:WIN, :] = kv[rows, 0:D]
                vpad[2 * q + w, 0:WIN, :] = kv[rows, D:]

    shape = (40, 256)
    lane = lax.broadcasted_iota(I32, shape, 1)
    side_q = jnp.minimum(lax.broadcasted_iota(I32, shape, 0) // 18, 1)
    side_k = (lane % 36) // 18
    inside = lane < WIN
    near = lane < 72
    split = side_q == side_k
    masks = {}
    for a in range(2):
        open_side = edge_ref[a] > 0
        for w in range(2):
            m = jnp.logical_and(inside, jnp.logical_or(near, open_side))
            masks[a, w] = jnp.logical_and(m, split) if w == 1 else m

    qmasks = head_masks((40, 128))
    vmasks = head_masks((256, 128))
    zero = jnp.zeros((), BF16)
    for g in range(3):
        lanes = slice(128 * g, 128 * g + 128)
        for a in range(2):
            biases = []
            for i in range(4):
                h = 4 * g + i
                biases.append(
                    jnp.concatenate(
                        [bias_ref[h, 96 * a : 96 * a + 80, :], bias_tail(bias_ref, h, 96 * a + 80, 10)],
                        axis=1,
                    )
                )
            for b in range(2):
                for w in range(2):
                    at = 4 * a + 2 * b + w
                    query = qbuf[40 * at : 40 * at + 40, lanes]
                    key = kpad[at, :, lanes]
                    value = vpad[at, :, lanes]
                    total = None
                    for i in range(4):
                        scores = dot_t(jnp.where(qmasks[i], query, 0.0).astype(BF16), key)
                        bias = biases[i][40 * b : 40 * b + 40]
                        bias = upper(bias) if w == 0 else lower(bias)
                        probs = softmax(scores * SCALE + bias * UNFIX, masks[a, w])
                        part = dot(probs, jnp.where(vmasks[i], value, zero))
                        total = part if total is None else total + part
                    obuf[40 * at : 40 * at + 40, lanes] = total
    attended = dot(unperm_ref[...], obuf[...].astype(BF16)).astype(BF16)
    result = dot(pad_ref[...], first_ref[...]) + dot(attended, wo_ref[...])
    result = result.astype(BF16)
    for g in range(24):
        out_ref[g] = result[16 * g : 16 * g + 12]


VMEM = pl.BlockSpec(memory_space=pltpu.VMEM)
SMEM = pl.BlockSpec(memory_space=pltpu.SMEM)
LIMIT = 48 * 1024 * 1024


def shift(block, axis, by, wrap):
    size = lax.axis_size(axis)
    route = [(i, (i + by) % size) for i in range(size) if wrap or 0 <= i + by < size]
    return lax.ppermute(block, axis, route)


def shards(
    tokens, position_index, gain_first, qkv_first, proj_first, bias_first,
    gain_second, qkv_second, proj_second, bias_second,
):
    lat = lax.axis_index("lat")
    last = lax.axis_size("lat") - 1
    tables_before = shift(bias_second, "lat", 1, False)
    tables_before = jnp.where(lat == 0, bias_second, tables_before)

    perm = compact_from_padded()
    first, west, east = pl.pallas_call(
        first_kernel,
        out_shape=(
            jax.ShapeDtypeStruct((288, D), BF16),
            jax.ShapeDtypeStruct((2, 72, D), BF16),
            jax.ShapeDtypeStruct((2, 72, D), BF16),
        ),
        in_specs=[VMEM] * 11,
        out_specs=(VMEM,) * 3,
        scratch_shapes=[
            pltpu.VMEM((384, D), BF16),
            pltpu.VMEM((HEADS, CHUNKS * 128), I32),
            pltpu.VMEM((168, 128), I32),
            pltpu.VMEM((168, 128), I32),
            pltpu.VMEM((HEADS, 168, 128), I32),
            pltpu.VMEM((2, 256, D), BF16),
            pltpu.VMEM((2, 256, D), BF16),
        ],
        compiler_params=pltpu.CompilerParams(vmem_limit_bytes=LIMIT),
        cost_estimate=pl.CostEstimate(flops=10**9, bytes_accessed=3 * 10**6, transcendentals=10**6),
        name="first_block",
    )(
        tokens.reshape(24, 12, D), position_index, gain_first.reshape(1, D), qkv_first, proj_first,
        bias_first, gain_second.reshape(1, D),
        jnp.asarray(perm), jnp.asarray(quadrants_from_compact()),
        jnp.asarray(tail_copies(list(range(WIN)))), jnp.asarray(tail_rows(18)),
    )

    from_west = shift(east, "lon", 1, True)
    from_east = shift(west, "lon", -1, True)

    picks = np.zeros((160, WIN), np.float32).astype(jnp.bfloat16)
    columns = []
    for a in range(2):
        for b in range(2):
            queries, keys = shifted_positions(a, b)
            q = 2 * a + b
            picks[40 * q : 40 * q + 36] = one_hot_rows(queries, WIN)
            columns.append(tail_copies(keys))
    bias = pl.pallas_call(
        bias_kernel,
        out_shape=jax.ShapeDtypeStruct((HEADS, 192, 128), I32),
        in_specs=[VMEM] * 6,
        out_specs=VMEM,
        scratch_shapes=[
            pltpu.VMEM((2, HEADS, CHUNKS * 128), I32),
            pltpu.VMEM((192, 128), I32),
            pltpu.VMEM((192, 128), I32),
        ],
        compiler_params=pltpu.CompilerParams(vmem_limit_bytes=LIMIT),
        cost_estimate=pl.CostEstimate(flops=10**9, bytes_accessed=10 * 10**6, transcendentals=10**6),
        name="second_bias",
    )(
        position_index, bias_second, tables_before,
        jnp.asarray(picks), jnp.asarray(np.stack(columns)), jnp.asarray(tail_rows(10)),
    )

    up = jnp.stack([from_west[0], west[0], east[0], from_east[0]])
    down = jnp.stack([from_west[1], west[1], east[1], from_east[1]])
    south = shift(up, "lat", -1, False)
    north = shift(down, "lat", 1, False)

    edges = jnp.stack([lat > 0, lat < last]).astype(I32)
    out = pl.pallas_call(
        second_kernel,
        out_shape=jax.ShapeDtypeStruct((24, 12, D), BF16),
        in_specs=[SMEM] + [VMEM] * 14,
        out_specs=VMEM,
        scratch_shapes=[
            pltpu.VMEM((4, 320, D), BF16),
            pltpu.VMEM((320, D), F32),
            pltpu.VMEM((8, 256, D), BF16),
            pltpu.VMEM((8, 256, D), BF16),
            pltpu.VMEM((320, D), F32),
        ],
        compiler_params=pltpu.CompilerParams(vmem_limit_bytes=LIMIT),
        cost_estimate=pl.CostEstimate(flops=10**9, bytes_accessed=5 * 10**6, transcendentals=10**6),
        name="second_block",
    )(
        edges, first, west, east, from_west, from_east, north, south,
        qkv_second, proj_second, bias,
        jnp.asarray(keys_from_pieces()), jnp.asarray(queries_from_quadrants()),
        jnp.asarray(padded_from_queries()), jnp.asarray(np.ascontiguousarray(perm.T)),
    )
    return out.reshape(4, 6, 12, D)


def solution(mesh):
    return jax.shard_map(
        shards,
        mesh=mesh,
        in_specs=(
            P(None, "lat", "lon", None), P(), P(), P(), P(),
            P("lat", None, None, None), P(), P(), P(), P("lat", None, None, None),
        ),
        out_specs=P(None, "lat", "lon", None),
        check_vma=False,
    )
```

time: 218 us -> 84.7 us (0.39)
  the two profiles are of different devices: /device:TPU:11 before, /device:TPU:4 now
where the time goes in v1:
time: 84.7 us; the launch traced here: 84.3 us
  Pallas kernels  41.9 us (49%)
  starting transfers between devices  24.6 us (29%)
  waiting for transfers between devices  9.19 us (11%)
  local copies, waits for them, and re-layouts  8.04 us (9%)
    ppermute x5, starting transfers between devices, shift(): return lax.ppermute(block, axis, route)  24.6 us
    pallas_call x1, Pallas kernels, shards(): pl.pallas_call(second_kernel, out_shape=jax.ShapeDtypeStruct((24, 12, D),...  17.1 us
    pallas_call x1, Pallas kernels, shards(): pl.pallas_call(first_kernel, out_shape=(jax.ShapeDtypeStruct((288, D), BF...  14.1 us
    pallas_call x1, Pallas kernels, shards(): pl.pallas_call(bias_kernel, out_shape=jax.ShapeDtypeStruct((HEADS, 192, 1...  10.6 us
    ppermute x5, waiting for transfers between devices, shift(): return lax.ppermute(block, axis, route)  9.19 us
    unnamed x39, local copies, waits for them, and re-layouts  5.82 us
  transfers between devices with their start and end apart: 5, of which 2 were waited for; matrix products, arithmetic and copies ran while one was open for 4% of the time, Pallas kernels for 29%

profile of v1, /device:TPU:4, one launch (start us, length us, event | category | flops | bytes accessed | tf_op | source)
XLA Modules:
  0.0 84.3 jit_solution(17846673891254026432)
XLA Ops:
  0.0 0.0 copy-start.6
  0.0 1.0 %copy.26.table_ref = bf16[1,2,12,3312]{3,2,1,0:T(8,128)(2,1)S(1)} copy(bf16[1,2,12,3312]{3,1,2,0:T(2,128)(2,1)} %param.30) | data formatting | bytes 317952 | tf_op args[9]
  1.1 1.9 %collective-permute-start.4 = (bf16[1,2,12,3312]{3,2,1,0:T(8,128)(2,1)S(1)}, bf16[1,2,12,3312]{3,2,1,0:T(8,128)(2,1)S(1)}, u32[]{:S(2)}, u32[]{:S(2)}) collective-permute-start(bf16[1,2,12,3312]{3,2,1,0:T(8,128)(2,1)S(1)} %copy.26.table_ref), channel_id=1, source_target_pairs={{0,32},{32,64},{64,96},{96,128},{128,160},{160,192},{192,224},{224... | collective-permute-start | bytes 476936 | tf_op jit(solution)/shard_map/ppermute | solution.py:386
  3.0 0.7 reshape.13.gain_ref
  3.7 0.7 reshape.14.gain2_ref
  4.4 0.9 %copy.23.table_ref = bf16[1,2,12,3312]{3,2,1,0:T(8,128)(2,1)S(1)} copy(bf16[1,2,12,3312]{3,1,2,0:T(2,128)(2,1)} %param.26) | data formatting | bytes 317952 | tf_op args[5]
  5.3 1.0 %copy.22 = bf16[4,6,12,384]{3,2,1,0:T(8,128)(2,1)S(1)} copy(bf16[4,6,12,384]{3,0,2,1:T(4,128)(2,1)} %param.21) | data formatting | bytes 442368 | tf_op args[0]
  6.3 0.0 copy-done.15
  6.3 0.0 copy-done.14
  6.3 0.0 copy-done.7
  6.3 0.0 copy-done.6
  6.3 0.0 copy-start.8
  6.3 0.9 %copy-done.8 = s32[144,144]{1,0:T(8,128)S(1)} copy-done((s32[144,144]{1,0:T(8,128)S(1)}, s32[144,144]{1,0:T(8,128)}, u32[]{:S(2)}) %copy-start.8) | copy-done | bytes 82968
  7.2 0.9 %copy-done.11 = bf16[288,288]{1,0:T(8,128)(2,1)S(1)} copy-done((bf16[288,288]{1,0:T(8,128)(2,1)S(1)}, bf16[288,288]{1,0:T(8,128)(2,1)}, u32[]{:S(2)}) %copy-start.11) | copy-done | bytes 165912
  8.2 0.9 %copy-done.12 = bf16[288,384]{1,0:T(8,128)(2,1)S(1)} copy-done((bf16[288,384]{1,0:T(8,128)(2,1)S(1)}, bf16[288,384]{1,0:T(8,128)(2,1)}, u32[]{:S(2)}) %copy-start.12) | copy-done | bytes 221208
  9.1 14.1 %first_block.1 = (bf16[288,384]{1,0:T(8,128)(2,1)S(1)}, bf16[2,72,384]{2,1,0:T(8,128)(2,1)S(1)}, bf16[2,72,384]{2,1,0:T(8,128)(2,1)S(1)}) custom-call(bf16[24,12,384]{2,1,0:T(8,128)(2,1)S(1)} %bitcast.5, s32[144,144]{1,0:T(8,128)S(1)} %copy-done.8, f32[1,384]{1,0:T(1,128)S(1)} %reshape.13.gain_ref, bf16[384,1152]{1,0:T(8,128)(2,1)S(1)} %copy-done.6, ...), custom_call_target="tpu_custom_call" | custom-call | flops 1000000000 | bytes 3000000 | tf_op jit(solution)/shard_map/first_block/pallas_call | solution.py:399
  23.2 0.0 copy-start.17
  23.3 14.2 %collective-permute-start.1 = (bf16[2,72,384]{2,1,0:T(8,128)(2,1)S(1)}, bf16[2,72,384]{2,1,0:T(8,128)(2,1)S(1)}, u32[]{:S(2)}, u32[]{:S(2)}) collective-permute-start(bf16[2,72,384]{2,1,0:T(8,128)(2,1)S(1)} %get-tuple-element.9.west_ref), channel_id=1, source_target_pairs={{0,31},{1,0},{2,1},{3,2},{4,3},{5,4},{6,5},{7,6},{8,7},{9,8},{10,9... | collective-permute-start | bytes 331784 | tf_op jit(solution)/shard_map/ppermute | solution.py:386
  37.4 1.9 %collective-permute-start = (bf16[2,72,384]{2,1,0:T(8,128)(2,1)S(1)}, bf16[2,72,384]{2,1,0:T(8,128)(2,1)S(1)}, u32[]{:S(2)}, u32[]{:S(2)}) collective-permute-start(bf16[2,72,384]{2,1,0:T(8,128)(2,1)S(1)} %get-tuple-element.10.east_ref), channel_id=1, source_target_pairs={{0,1},{1,2},{2,3},{3,4},{4,5},{5,6},{6,7},{7,8},{8,9},{9,10},{10,1... | collective-permute-start | bytes 331784 | tf_op jit(solution)/shard_map/ppermute | solution.py:386
  39.4 0.0 copy-start.9
  39.4 0.0 copy-start.10
  39.4 0.0 copy-start.13
  39.4 0.0 copy-start.16
  39.5 0.1 add_convert_fusion.edge_ref
  39.5 1.0 %collective-permute-done.1.from_east_ref = bf16[2,72,384]{2,1,0:T(8,128)(2,1)S(1)} collective-permute-done((bf16[2,72,384]{2,1,0:T(8,128)(2,1)S(1)}, bf16[2,72,384]{2,1,0:T(8,128)(2,1)S(1)}, u32[]{:S(2)}, u32[]{:S(2)}) %collective-permute-start.1) | collective-permute-done | bytes 110624 | tf_op jit(solution)/shard_map/ppermute | solution.py:386
  40.5 8.2 %collective-permute-done.from_west_ref = bf16[2,72,384]{2,1,0:T(8,128)(2,1)S(1)} collective-permute-done((bf16[2,72,384]{2,1,0:T(8,128)(2,1)S(1)}, bf16[2,72,384]{2,1,0:T(8,128)(2,1)S(1)}, u32[]{:S(2)}, u32[]{:S(2)}) %collective-permute-start) | collective-permute-done | bytes 110624 | tf_op jit(solution)/shard_map/ppermute | solution.py:386
  48.8 2.0 %collective-permute-start.2 = (bf16[4,72,384]{2,1,0:T(8,128)(2,1)S(1)}, bf16[4,72,384]{2,1,0:T(8,128)(2,1)S(1)}, u32[]{:S(2)}, u32[]{:S(2)}) collective-permute-start(bf16[4,72,384]{2,1,0:T(8,128)(2,1)S(1)} %pad_maximum_fusion), channel_id=1, source_target_pairs={{0,32},{32,64},{64,96},{96,128},{128,160},{160,192},{192,224},{224... | collective-permute-start | bytes 663560 | tf_op jit(solution)/shard_map/ppermute | solution.py:386
  50.9 4.6 %collective-permute-start.3 = (bf16[4,72,384]{2,1,0:T(8,128)(2,1)S(1)}, bf16[4,72,384]{2,1,0:T(8,128)(2,1)S(1)}, u32[]{:S(2)}, u32[]{:S(2)}) collective-permute-start(bf16[4,72,384]{2,1,0:T(8,128)(2,1)S(1)} %pad_maximum_fusion.1), channel_id=1, source_target_pairs={{32,0},{64,32},{96,64},{128,96},{160,128},{192,160},{224,192},{256... | collective-permute-start | bytes 663560 | tf_op jit(solution)/shard_map/ppermute | solution.py:386
  55.5 0.0 collective-permute-done.4
  55.5 0.0 copy-done.17
  55.6 0.0 copy-done.9
  55.6 0.0 copy-done.10
  55.6 0.0 copy-done.13
  55.6 0.0 copy-done.16
  55.6 0.0 copy-start
  55.6 0.0 copy-start.1
  55.6 0.0 copy-start.2
  55.6 0.0 copy-start.3
  55.7 0.0 copy-start.4
  55.7 0.0 copy-start.5
  55.7 10.6 %second_bias.1.bias_ref = s32[12,192,128]{2,1,0:T(8,128)S(1)} custom-call(s32[144,144]{1,0:T(8,128)S(1)} %copy-done.9, bf16[1,2,12,3312]{3,2,1,0:T(8,128)(2,1)S(1)} %copy.26.table_ref, bf16[1,2,12,3312]{3,2,1,0:T(8,128)(2,1)S(1)} %broadcast_select_fusion.before_ref, bf16[160,144]{1,0:T(8,128)(2,1)S(1)} %copy-done.13, bf16[4,144,256]{2,1,0:T(8,128)(2,1)S(1)} %copy-done.10, ...), custom_call_target="tpu_custom_call" | custom-call | flops 1000000000 | bytes 10000000 | tf_op jit(solution)/shard_map/second_bias/pallas_call | solution.py:438
  66.3 0.0 collective-permute-done.2.north_ref
  66.3 0.0 collective-permute-done.3.south_ref
  66.3 0.0 copy-done
  66.3 0.0 copy-done.1
  66.3 0.0 copy-done.2
  66.4 17.1 %second_block.1 = bf16[24,12,384]{2,1,0:T(8,128)(2,1)S(1)} custom-call(s32[2]{0:T(128)S(1)} %add_convert_fusion.edge_ref, bf16[288,384]{1,0:T(8,128)(2,1)S(1)} %get-tuple-element.8.first_ref, bf16[2,72,384]{2,1,0:T(8,128)(2,1)S(1)} %get-tuple-element.9.west_ref, bf16[2,72,384]{2,1,0:T(8,128)(2,1)S(1)} %get-tuple-element.10.east_ref, ...), custom_call_target="tpu_custom_call" | custom-call | flops 1000000000 | bytes 5000000 | tf_op jit(solution)/shard_map/second_block/pallas_call | solution.py:462
  83.5 0.8 copy.27
  (14 shorter events, 0.2 us)
Async XLA Ops:
  0.0 6.3 %copy-start.15 = (bf16[24,144]{1,0:T(8,128)(2,1)S(1)}, bf16[24,144]{1,0:T(8,128)(2,1)}, u32[]{:S(2)}) copy-start(bf16[24,144]{1,0:T(8,128)(2,1)} %constant.35.clone.tailrows_ref) | copy-start | bytes 20740
  0.0 6.3 %copy-start.14 = (bf16[144,256]{1,0:T(8,128)(2,1)S(1)}, bf16[144,256]{1,0:T(8,128)(2,1)}, u32[]{:S(2)}) copy-start(bf16[144,256]{1,0:T(8,128)(2,1)} %constant.34.clone.cols_ref) | copy-start | bytes 221188
  0.0 6.3 %copy-start.7 = (bf16[384,384]{1,0:T(8,128)(2,1)S(1)}, bf16[384,384]{1,0:T(8,128)(2,1)}, u32[]{:S(2)}) copy-start(bf16[384,384]{1,0:T(8,128)(2,1)} %wo_ref.2) | copy-start | bytes 884740
  0.0 6.3 %copy-start.6 = (bf16[384,1152]{1,0:T(8,128)(2,1)S(1)}, bf16[384,1152]{1,0:T(8,128)(2,1)}, u32[]{:S(2)}) copy-start(bf16[384,1152]{1,0:T(8,128)(2,1)} %wqkv_ref.2) | copy-start | bytes 2654212
  1.1 54.4 %collective-permute-start.4 = (bf16[1,2,12,3312]{3,2,1,0:T(8,128)(2,1)S(1)}, bf16[1,2,12,3312]{3,2,1,0:T(8,128)(2,1)S(1)}, u32[]{:S(2)}, u32[]{:S(2)}) collective-permute-start(bf16[1,2,12,3312]{3,2,1,0:T(8,128)(2,1)S(1)} %copy.26.table_ref), channel_id=1, source_target_pairs={{0,32},{32,64},{64,96},{96,128},{128,160},{160,192},{192,224},{224... | collective-permute-start | bytes 476936 | tf_op jit(solution)/shard_map/ppermute | solution.py:386
  6.3 0.9 %copy-start.8 = (s32[144,144]{1,0:T(8,128)S(1)}, s32[144,144]{1,0:T(8,128)}, u32[]{:S(2)}) copy-start(s32[144,144]{1,0:T(8,128)} %idx_ref.3) | copy-start | bytes 248836
  7.2 0.9 %copy-start.11 = (bf16[288,288]{1,0:T(8,128)(2,1)S(1)}, bf16[288,288]{1,0:T(8,128)(2,1)}, u32[]{:S(2)}) copy-start(bf16[288,288]{1,0:T(8,128)(2,1)} %constant.33.clone.quad_ref) | copy-start | bytes 497668
  8.2 0.9 %copy-start.12 = (bf16[288,384]{1,0:T(8,128)(2,1)S(1)}, bf16[288,384]{1,0:T(8,128)(2,1)}, u32[]{:S(2)}) copy-start(bf16[288,384]{1,0:T(8,128)(2,1)} %constant.32.clone.perm_ref) | copy-start | bytes 663556
  23.2 32.3 %copy-start.17 = (bf16[1,2,12,3312]{3,1,2,0:T(2,128)(2,1)S(1)}, bf16[1,2,12,3312]{3,1,2,0:T(2,128)(2,1)}, u32[]{:S(2)}) copy-start(bf16[1,2,12,3312]{3,1,2,0:T(2,128)(2,1)} %param.30) | copy-start | bytes 476932
  23.3 17.3 %collective-permute-start.1 = (bf16[2,72,384]{2,1,0:T(8,128)(2,1)S(1)}, bf16[2,72,384]{2,1,0:T(8,128)(2,1)S(1)}, u32[]{:S(2)}, u32[]{:S(2)}) collective-permute-start(bf16[2,72,384]{2,1,0:T(8,128)(2,1)S(1)} %get-tuple-element.9.west_ref), channel_id=1, source_target_pairs={{0,31},{1,0},{2,1},{3,2},{4,3},{5,4},{6,5},{7,6},{8,7},{9,8},{10,9... | collective-permute-start | bytes 331784 | tf_op jit(solution)/shard_map/ppermute | solution.py:386
  37.4 11.3 %collective-permute-start = (bf16[2,72,384]{2,1,0:T(8,128)(2,1)S(1)}, bf16[2,72,384]{2,1,0:T(8,128)(2,1)S(1)}, u32[]{:S(2)}, u32[]{:S(2)}) collective-permute-start(bf16[2,72,384]{2,1,0:T(8,128)(2,1)S(1)} %get-tuple-element.10.east_ref), channel_id=1, source_target_pairs={{0,1},{1,2},{2,3},{3,4},{4,5},{5,6},{6,7},{7,8},{8,9},{9,10},{10,1... | collective-permute-start | bytes 331784 | tf_op jit(solution)/shard_map/ppermute | solution.py:386
  39.4 16.2 %copy-start.9 = (s32[144,144]{1,0:T(8,128)S(1)}, s32[144,144]{1,0:T(8,128)}, u32[]{:S(2)}) copy-start(s32[144,144]{1,0:T(8,128)} %idx_ref.3) | copy-start | bytes 248836
  39.4 16.2 %copy-start.10 = (bf16[4,144,256]{2,1,0:T(8,128)(2,1)S(1)}, bf16[4,144,256]{2,1,0:T(8,128)(2,1)}, u32[]{:S(2)}) copy-start(bf16[4,144,256]{2,1,0:T(8,128)(2,1)} %constant.37.clone.cols_ref) | copy-start | bytes 884740
  39.4 16.2 %copy-start.13 = (bf16[160,144]{1,0:T(8,128)(2,1)S(1)}, bf16[160,144]{1,0:T(8,128)(2,1)}, u32[]{:S(2)}) copy-start(bf16[160,144]{1,0:T(8,128)(2,1)} %constant.36.clone.pick_ref) | copy-start | bytes 138244
  39.4 16.2 %copy-start.16 = (bf16[16,80]{1,0:T(8,128)(2,1)S(1)}, bf16[16,80]{1,0:T(8,128)(2,1)}, u32[]{:S(2)}) copy-start(bf16[16,80]{1,0:T(8,128)(2,1)} %constant.38.clone.tailrows_ref) | copy-start | bytes 7684
  48.8 17.5 %collective-permute-start.2 = (bf16[4,72,384]{2,1,0:T(8,128)(2,1)S(1)}, bf16[4,72,384]{2,1,0:T(8,128)(2,1)S(1)}, u32[]{:S(2)}, u32[]{:S(2)}) collective-permute-start(bf16[4,72,384]{2,1,0:T(8,128)(2,1)S(1)} %pad_maximum_fusion), channel_id=1, source_target_pairs={{0,32},{32,64},{64,96},{96,128},{128,160},{160,192},{192,224},{224... | collective-permute-start | bytes 663560 | tf_op jit(solution)/shard_map/ppermute | solution.py:386
  50.9 15.4 %collective-permute-start.3 = (bf16[4,72,384]{2,1,0:T(8,128)(2,1)S(1)}, bf16[4,72,384]{2,1,0:T(8,128)(2,1)S(1)}, u32[]{:S(2)}, u32[]{:S(2)}) collective-permute-start(bf16[4,72,384]{2,1,0:T(8,128)(2,1)S(1)} %pad_maximum_fusion.1), channel_id=1, source_target_pairs={{32,0},{64,32},{96,64},{128,96},{160,128},{192,160},{224,192},{256... | collective-permute-start | bytes 663560 | tf_op jit(solution)/shard_map/ppermute | solution.py:386
  55.6 10.7 %copy-start = (bf16[384,1152]{1,0:T(8,128)(2,1)S(1)}, bf16[384,1152]{1,0:T(8,128)(2,1)}, u32[]{:S(2)}) copy-start(bf16[384,1152]{1,0:T(8,128)(2,1)} %wqkv_ref.3) | copy-start | bytes 2654212
  55.6 10.7 %copy-start.1 = (bf16[384,384]{1,0:T(8,128)(2,1)S(1)}, bf16[384,384]{1,0:T(8,128)(2,1)}, u32[]{:S(2)}) copy-start(bf16[384,384]{1,0:T(8,128)(2,1)} %wo_ref.3) | copy-start | bytes 884740
  55.6 10.7 %copy-start.2 = (bf16[384,288]{1,0:T(8,128)(2,1)S(1)}, bf16[384,288]{1,0:T(8,128)(2,1)}, u32[]{:S(2)}) copy-start(bf16[384,288]{1,0:T(8,128)(2,1)} %constant.42.clone.pad_ref) | copy-start | bytes 663556
  55.6 10.7 %copy-start.3 = (bf16[384,320]{1,0:T(8,128)(2,1)S(1)}, bf16[384,320]{1,0:T(8,128)(2,1)}, u32[]{:S(2)}) copy-start(bf16[384,320]{1,0:T(8,128)(2,1)} %constant.41.clone.unperm_ref) | copy-start | bytes 737284
  55.7 10.7 %copy-start.4 = (bf16[320,288]{1,0:T(8,128)(2,1)S(1)}, bf16[320,288]{1,0:T(8,128)(2,1)}, u32[]{:S(2)}) copy-start(bf16[320,288]{1,0:T(8,128)(2,1)} %constant.40.clone.queries_ref) | copy-start | bytes 552964
  55.7 10.7 %copy-start.5 = (bf16[288,320]{1,0:T(8,128)(2,1)S(1)}, bf16[288,320]{1,0:T(8,128)(2,1)}, u32[]{:S(2)}) copy-start(bf16[288,320]{1,0:T(8,128)(2,1)} %constant.39.clone.keys_ref) | copy-start | bytes 552964

commit v2 on v1

v2 whole, which is shorter than its diff:
```python
import jax
import jax.numpy as jnp
import numpy as np
from jax import lax
from jax.experimental import pallas as pl
from jax.experimental.pallas import tpu as pltpu
from jax.sharding import PartitionSpec as P

F32, BF16, I32 = jnp.float32, jnp.bfloat16, jnp.int32
HEADS = 12
D = 384
WIN = 144
CHUNKS = 26
POS = 3312
LOG2E = float(np.log2(np.e))
FIX = 8191.0
SCALE = LOG2E * 32 ** -0.5
UNFIX = LOG2E / FIX


def dot(a, b):
    return jnp.dot(a, b, preferred_element_type=F32)


def dot_t(a, b):
    return lax.dot_general(a, b, (((1,), (1,)), ((), ())), preferred_element_type=F32)


def one_hot(source, width):
    lane = lax.broadcasted_iota(I32, (source.shape[0], width), 1)
    return jnp.where(lane == source, 1.0, 0.0).astype(BF16)


def row_ids(count):
    return lax.broadcasted_iota(I32, (count, 1), 0)


def quadrants_from_natural():
    i = row_ids(288)
    b, a, w, lo = i // 144, i // 72 % 2, i // 36 % 2, i // 18 % 2
    level = (2 * w + lo + 1) % 4
    return one_hot(level * 72 + (3 * a + i // 6 % 3) * 12 + 6 * b + i % 6, 288)


def keys_from_pieces():
    i = row_ids(288)
    w, piece, t = i // 144, i // 36 % 4, i % 36
    return one_hot(80 * piece + 36 * w + t, 320)


def queries_from_quadrants():
    i = row_ids(320)
    a, b, w, t = i // 160, i // 80 % 2, i // 40 % 2, i % 40
    return one_hot(jnp.where(t < 36, b * 144 + a * 72 + w * 36 + t, -1), 288)


def natural_from_given():
    i = row_ids(288)
    return one_hot(i % 72 * 4 + i // 72, 288)


def given_from_natural():
    i = row_ids(288)
    return one_hot(i % 4 * 72 + i // 4, 288)


def given_from_queries():
    i = row_ids(288)
    level, r, c = (i % 4 + 3) % 4, i // 48, i // 4 % 12
    a, b, w, lo = r // 3, c // 6, level // 2, level % 2
    return one_hot(a * 160 + b * 80 + w * 40 + lo * 18 + r % 3 * 6 + c % 6, 320)


def tail_rows(tiles):
    packed = -(-tiles // 8) * 8
    shape = (packed, tiles * 8)
    i = lax.broadcasted_iota(I32, shape, 0)
    k = lax.broadcasted_iota(I32, shape, 1)
    take = jnp.logical_and(i // 8 == k // 64, i % 8 == k % 8)
    return jnp.where(take, 1.0, 0.0).astype(BF16)


def tail_columns():
    shape = (WIN, 256)
    i = lax.broadcasted_iota(I32, shape, 0)
    k = lax.broadcasted_iota(I32, shape, 1)
    return jnp.where(i == jnp.where(k < 128, k, 128 + k % 16), 1.0, 0.0).astype(BF16)


def shifted_query(a, b, i):
    return 72 * (i // 18) + 12 * (3 * (1 - a) + i // 6 % 3) + 6 * (1 - b) + i % 6


def shifted_key(a, b, i):
    piece, t = i // 36, i % 36
    row = jnp.where(piece < 2, 3 * (1 - a), 3 * a)
    col = jnp.where(piece % 2 == 0, 6 * (1 - b), 6 * b)
    return 72 * (t // 18) + 12 * (row + t // 6 % 3) + col + t % 6


def query_picks():
    i = row_ids(160)
    a, b, t = i // 80, i // 40 % 2, i % 40
    return one_hot(jnp.where(t < 36, shifted_query(a, b, t), -1), WIN)


def key_columns(a, b):
    k = lax.broadcasted_iota(I32, (1, 256), 1)
    position = shifted_key(a, b, jnp.where(k < 128, k, 128 + k % 16))
    i = lax.broadcasted_iota(I32, (WIN, 256), 0)
    return jnp.where(i == position, 1.0, 0.0).astype(BF16)


def pack_table(table_ref, packed_ref):
    for h in range(HEADS):
        fixed = jnp.round(table_ref[h].astype(F32) * FIX).astype(I32)
        packed_ref[h : h + 1, 0:POS] = (fixed[0:1] << 16) | (fixed[1:2] & 0xFFFF)


def split_index(position_index):
    high = (position_index >> 7).astype(F32).astype(BF16)
    low = (position_index & 127).astype(F32).astype(BF16)
    return high, low


def fold_tail(values, gather_rows, tiles):
    row = lax.broadcasted_iota(I32, values.shape, 0) // 8
    lane = lax.broadcasted_iota(I32, values.shape, 1) // 16
    kept = jnp.where((row % 8) == lane, values, 0.0).astype(BF16)
    return dot(gather_rows, kept)


def place_index(part, columns, gather_rows, dst_ref, start, tiles):
    spread = dot(part, columns)
    rows = tiles * 8
    dst_ref[start : start + rows, :] = spread[:, :128].astype(I32)
    tail = fold_tail(spread[:, 128:], gather_rows, tiles)
    dst_ref[start + rows : start + rows + tail.shape[0], :] = tail.astype(I32)


def expand(packed_ref, high_ref, low_ref, out_ref, start, count):
    def tile(t, carry):
        rows = pl.ds(pl.multiple_of(start + t * 8, 8), 8)
        low = low_ref[rows, :]
        high = high_ref[rows, :]
        picked = [None] * HEADS
        for c in range(CHUNKS):
            here = high == c
            for h in range(HEADS):
                entries = jnp.broadcast_to(packed_ref[h : h + 1, 128 * c : 128 * c + 128], (8, 128))
                got = jnp.take_along_axis(entries, low, axis=1, mode="promise_in_bounds")
                picked[h] = got if c == 0 else jnp.where(here, got, picked[h])
        for h in range(HEADS):
            out_ref[h, rows, :] = picked[h]
        return carry

    lax.fori_loop(0, count, tile, 0)


def bias_tail(bias_ref, h, base, tiles):
    out = []
    for t in range(tiles):
        at = base + (t // 8) * 8
        part = bias_ref[h, at : at + 8, :]
        j = t % 8
        out.append(part if j == 0 else pltpu.roll(part, 128 - 16 * j, 1))
    return jnp.concatenate(out, axis=0)


def upper(packed):
    return (packed >> 16).astype(F32)


def lower(packed):
    return ((packed << 16) >> 16).astype(F32)


def layer_norm(values, gain):
    center = jnp.mean(values, axis=-1, keepdims=True)
    moved = values - center
    spread = jnp.mean(moved * moved, axis=-1, keepdims=True)
    return (moved * lax.rsqrt(spread + 1e-05) * gain).astype(BF16)


def softmax(scores, mask):
    raised = jnp.where(mask, jnp.exp2(scores), 0.0)
    total = jnp.sum(raised, axis=-1, keepdims=True)
    step = jnp.where(total > 1.0, 0.25, 1.0)
    return ((raised * step) * (1.0 / (total * step))).astype(BF16)


def four_heads(query, key, value, biases, mask):
    n = query.shape[0]
    own = lax.broadcasted_iota(I32, query.shape, 1) // 32
    stacked = jnp.concatenate([jnp.where(own == i, query, 0.0) for i in range(4)], axis=0)
    scores = dot_t(stacked.astype(BF16), key)
    probs = [
        softmax(scores[n * i : n * i + n] * SCALE + biases[i] * UNFIX, mask) for i in range(4)
    ]
    parts = dot(jnp.concatenate(probs, axis=0), value)
    out = parts[0:n]
    for i in range(1, 4):
        out = jnp.where(own == i, parts[n * i : n * i + n], out)
    return out


def first_kernel(
    tok_ref, idx_ref, gain_ref, wqkv_ref, wo_ref, table_ref, gain2_ref,
    first_ref, west_ref, east_ref,
    values_ref, packed, high_ref, low_ref, bias_ref, qbuf, kpad, vpad, obuf,
):
    pack_table(table_ref, packed)
    high, low = split_index(idx_ref[...])
    columns, gather_rows = tail_columns(), tail_rows(18)
    place_index(high, columns, gather_rows, high_ref, 0, 18)
    place_index(low, columns, gather_rows, low_ref, 0, 18)
    expand(packed, high_ref, low_ref, bias_ref, 0, 21)

    for g in range(72):
        values_ref[4 * g : 4 * g + 4, :] = tok_ref[g].astype(F32)
    values = dot(natural_from_given(), values_ref[...].astype(BF16))
    values_ref[...] = values
    normed = layer_norm(values, gain_ref[...])
    qkv = dot(normed, wqkv_ref[...]).astype(BF16)
    qbuf[...] = qkv[:, 0:D].astype(F32)
    for w in range(2):
        rows = slice(WIN * w, WIN * w + WIN)
        kpad[w, 0:WIN, :] = qkv[rows, D : 2 * D]
        vpad[w, 0:WIN, :] = qkv[rows, 2 * D :]
        kpad[w, WIN:, :] = jnp.zeros((256 - WIN, D), BF16)
        vpad[w, WIN:, :] = jnp.zeros((256 - WIN, D), BF16)

    valid = lax.broadcasted_iota(I32, (WIN, 256), 1) < WIN
    for g in range(3):
        lanes = slice(128 * g, 128 * g + 128)
        biases = []
        for i in range(4):
            h = 4 * g + i
            biases.append(
                jnp.concatenate([bias_ref[h, 0:WIN, :], bias_tail(bias_ref, h, WIN, 18)], axis=1)
            )
        for w in range(2):
            rows = slice(WIN * w, WIN * w + WIN)
            half = upper if w == 0 else lower
            obuf[rows, lanes] = four_heads(
                qbuf[rows, lanes], kpad[w, :, lanes], vpad[w, :, lanes],
                [half(x) for x in biases], valid,
            ).astype(BF16)
    first = (values_ref[...] + dot(obuf[...], wo_ref[...])).astype(BF16)
    first_ref[...] = first
    again = layer_norm(first.astype(F32), gain2_ref[...])
    parts = dot(quadrants_from_natural(), again).astype(BF16)
    for a in range(2):
        west_ref[a] = parts[72 * a : 72 * a + 72]
        east_ref[a] = parts[144 + 72 * a : 144 + 72 * a + 72]


def bias_kernel(
    idx_ref, table_ref, before_ref, lat_ref,
    bias_ref,
    packed, high_ref, low_ref,
):
    pack_table(table_ref, packed.at[1])
    pack_table(before_ref, packed.at[0])

    @pl.when(lat_ref[0] == 0)
    def _():
        packed[0] = packed[1]

    high, low = split_index(idx_ref[...])
    picks, gather_rows = query_picks(), tail_rows(10)
    for a in range(2):
        columns = [key_columns(a, b) for b in range(2)]
        for part, dst in ((high, high_ref), (low, low_ref)):
            rows = dot(picks[80 * a : 80 * a + 80], part).astype(BF16)
            spread = jnp.concatenate(
                [dot(rows[40 * b : 40 * b + 40], columns[b]) for b in range(2)], axis=0
            )
            start = a * 96
            dst[start : start + 80, :] = spread[:, :128].astype(I32)
            tail = fold_tail(spread[:, 128:], gather_rows, 10)
            dst[start + 80 : start + 96, :] = tail.astype(I32)
    for a in range(2):
        expand(packed.at[a], high_ref, low_ref, bias_ref, a * 96, 12)


def second_kernel(
    edge_ref,
    first_ref, west_ref, east_ref, from_west_ref, from_east_ref, north_ref, south_ref,
    wqkv_ref, wo_ref, bias_ref,
    out_ref,
    cat, window, qbuf, kpad, vpad, obuf,
):
    own = (west_ref, east_ref)
    beside = (from_west_ref, from_east_ref)
    beyond = (north_ref, south_ref)
    tokens = jnp.concatenate([west_ref[0], west_ref[1], east_ref[0], east_ref[1]], axis=0)
    asked = dot(queries_from_quadrants(), tokens).astype(BF16)
    qbuf[...] = dot(asked, wqkv_ref[:, 0:D]).astype(BF16).astype(F32)

    order = keys_from_pieces()
    for piece in range(4):
        cat[80 * piece + 72 : 80 * piece + 80, :] = jnp.zeros((8, D), F32)
    for a in range(2):
        for b in range(2):
            q = 2 * a + b
            far = ((1, 0), (2, 3))[b]
            cat[0:72, :] = own[b][a].astype(F32)
            cat[80:152, :] = beside[b][a].astype(F32)
            cat[160:232, :] = beyond[a][far[0]].astype(F32)
            cat[240:312, :] = beyond[a][far[1]].astype(F32)
            window[288 * q : 288 * q + 288, :] = dot(order, cat[...].astype(BF16)).astype(BF16)
    for dst, start in ((kpad, D), (vpad, 2 * D)):
        made = dot(window[...], wqkv_ref[:, start : start + D]).astype(BF16)
        for j in range(8):
            dst[j, 0:WIN, :] = made[WIN * j : WIN * j + WIN]
            dst[j, WIN:, :] = jnp.zeros((256 - WIN, D), BF16)

    shape = (40, 256)
    lane = lax.broadcasted_iota(I32, shape, 1)
    side_q = jnp.minimum(lax.broadcasted_iota(I32, shape, 0) // 18, 1)
    side_k = (lane % 36) // 18
    inside = lane < WIN
    near = lane < 72
    split = side_q == side_k
    for a in range(2):
        open_side = edge_ref[a] > 0
        seen = jnp.logical_and(inside, jnp.logical_or(near, open_side))
        masks = (seen, jnp.logical_and(seen, split))
        for g in range(3):
            lanes = slice(128 * g, 128 * g + 128)
            biases = []
            for i in range(4):
                h = 4 * g + i
                tail = bias_tail(bias_ref, h, 96 * a + 80, 10)
                biases.append(
                    jnp.concatenate([bias_ref[h, 96 * a : 96 * a + 80, :], tail], axis=1)
                )
            for b in range(2):
                for w in range(2):
                    at = 4 * a + 2 * b + w
                    half = upper if w == 0 else lower
                    obuf[40 * at : 40 * at + 40, lanes] = four_heads(
                        qbuf[40 * at : 40 * at + 40, lanes], kpad[at, :, lanes], vpad[at, :, lanes],
                        [half(x[40 * b : 40 * b + 40]) for x in biases], masks[w],
                    )
    attended = dot(given_from_queries(), obuf[...].astype(BF16)).astype(BF16)
    qbuf[0:288, :] = dot(given_from_natural(), first_ref[...]) + dot(attended, wo_ref[...])
    for g in range(72):
        out_ref[g] = qbuf[4 * g : 4 * g + 4, :].astype(BF16)


VMEM = pl.BlockSpec(memory_space=pltpu.VMEM)
SMEM = pl.BlockSpec(memory_space=pltpu.SMEM)
LIMIT = 48 * 1024 * 1024


def shift(block, axis, by, wrap):
    size = lax.axis_size(axis)
    route = [(i, (i + by) % size) for i in range(size) if wrap or 0 <= i + by < size]
    return lax.ppermute(block, axis, route)


def cost(flops, moved):
    return pl.CostEstimate(flops=flops, bytes_accessed=moved, transcendentals=10**6)


def shards(
    tokens, position_index, gain_first, qkv_first, proj_first, bias_first,
    gain_second, qkv_second, proj_second, bias_second,
):
    lat = lax.axis_index("lat")
    last = lax.axis_size("lat") - 1
    params = pltpu.CompilerParams(vmem_limit_bytes=LIMIT)

    first, west, east = pl.pallas_call(
        first_kernel,
        out_shape=(
            jax.ShapeDtypeStruct((288, D), BF16),
            jax.ShapeDtypeStruct((2, 72, D), BF16),
            jax.ShapeDtypeStruct((2, 72, D), BF16),
        ),
        in_specs=[VMEM] * 7,
        out_specs=(VMEM,) * 3,
        scratch_shapes=[
            pltpu.VMEM((288, D), F32),
            pltpu.VMEM((HEADS, CHUNKS * 128), I32),
            pltpu.VMEM((168, 128), I32),
            pltpu.VMEM((168, 128), I32),
            pltpu.VMEM((HEADS, 168, 128), I32),
            pltpu.VMEM((288, D), F32),
            pltpu.VMEM((2, 256, D), BF16),
            pltpu.VMEM((2, 256, D), BF16),
            pltpu.VMEM((288, D), BF16),
        ],
        compiler_params=params,
        cost_estimate=cost(10**9, 3 * 10**6),
        name="first_block",
    )(
        tokens.transpose(1, 2, 0, 3).reshape(72, 4, D), position_index, gain_first, qkv_first, proj_first,
        bias_first.transpose(0, 2, 1, 3).reshape(HEADS, 2, POS), gain_second,
    )

    table = bias_second.transpose(0, 2, 1, 3).reshape(HEADS, 2, POS)
    table, first = lax.optimization_barrier((table, first))
    before = shift(table, "lat", 1, False)
    from_west = shift(east, "lon", 1, True)
    from_east = shift(west, "lon", -1, True)

    bias = pl.pallas_call(
        bias_kernel,
        out_shape=jax.ShapeDtypeStruct((HEADS, 192, 128), I32),
        in_specs=[VMEM] * 3 + [SMEM],
        out_specs=VMEM,
        scratch_shapes=[
            pltpu.VMEM((2, HEADS, CHUNKS * 128), I32),
            pltpu.VMEM((192, 128), I32),
            pltpu.VMEM((192, 128), I32),
        ],
        compiler_params=params,
        cost_estimate=cost(10**9, 10**7),
        name="second_bias",
    )(position_index, table, before, lat.astype(I32).reshape(1))

    west, east, from_west, from_east, bias = lax.optimization_barrier(
        (west, east, from_west, from_east, bias)
    )
    up = jnp.stack([from_west[0], west[0], east[0], from_east[0]])
    down = jnp.stack([from_west[1], west[1], east[1], from_east[1]])
    south = shift(up, "lat", -1, False)
    north = shift(down, "lat", 1, False)

    edges = jnp.stack([lat > 0, lat < last]).astype(I32)
    out = pl.pallas_call(
        second_kernel,
        out_shape=jax.ShapeDtypeStruct((72, 4, D), BF16),
        in_specs=[SMEM] + [VMEM] * 10,
        out_specs=VMEM,
        scratch_shapes=[
            pltpu.VMEM((320, D), F32),
            pltpu.VMEM((1152, D), BF16),
            pltpu.VMEM((320, D), F32),
            pltpu.VMEM((8, 256, D), BF16),
            pltpu.VMEM((8, 256, D), BF16),
            pltpu.VMEM((320, D), F32),
        ],
        compiler_params=params,
        cost_estimate=cost(10**9, 5 * 10**6),
        name="second_block",
    )(
        edges, first, west, east, from_west, from_east, north, south,
        qkv_second, proj_second, bias,
    )
    return out.reshape(6, 12, 4, D).transpose(2, 0, 1, 3)


def solution(mesh):
    return jax.shard_map(
        shards,
        mesh=mesh,
        in_specs=(
            P(None, "lat", "lon", None), P(), P(), P(), P(),
            P("lat", None, None, None), P(), P(), P(), P("lat", None, None, None),
        ),
        out_specs=P(None, "lat", "lon", None),
        check_vma=False,
    )
```

time: 84.7 us -> 68.7 us (0.81)
  the two profiles are of different devices: /device:TPU:4 before, /device:TPU:11 now
where the time goes in v2:
time: 68.7 us; the launch traced here: 68.3 us
  Pallas kernels  30.6 us (45%)
  starting transfers between devices  23.3 us (34%)
  waiting for transfers between devices  6.36 us (9%)
  local copies, waits for them, and re-layouts  6.32 us (9%)
  other arithmetic  1.53 us (2%)
    ppermute x5, starting transfers between devices, shift(): return lax.ppermute(block, axis, route)  23.3 us
    pallas_call x1, Pallas kernels, shards(): pl.pallas_call(first_kernel, out_shape=(jax.ShapeDtypeStruct((288, D), BF...  12.9 us
    pallas_call x1, Pallas kernels, shards(): pl.pallas_call(bias_kernel, out_shape=jax.ShapeDtypeStruct((HEADS, 192, 1...  10.8 us
    pallas_call x1, Pallas kernels, shards(): pl.pallas_call(second_kernel, out_shape=jax.ShapeDtypeStruct((72, 4, D),...  6.84 us
    ppermute x5, waiting for transfers between devices, shift(): return lax.ppermute(block, axis, route)  6.36 us
    unnamed x22, local copies, waits for them, and re-layouts  6.27 us
  transfers between devices with their start and end apart: 5, of which 2 were waited for; matrix products, arithmetic and copies ran while one was open for 1% of the time, Pallas kernels for 16%

profile of v2, /device:TPU:11, one launch (start us, length us, event | category | flops | bytes accessed | tf_op | source)
XLA Modules:
  0.0 68.3 jit_solution(12212253767181932504)
XLA Ops:
  0.0 0.0 copy-start
  0.0 1.2 %copy-done = bf16[384,1152]{1,0:T(8,128)(2,1)S(1)} copy-done((bf16[384,1152]{1,0:T(8,128)(2,1)S(1)}, bf16[384,1152]{1,0:T(8,128)(2,1)}, u32[]{:S(2)}) %copy-start) | copy-done | bytes 884760
  1.2 0.0 copy-start.2
  1.2 1.0 %copy-done.2 = bf16[384,384]{1,0:T(8,128)(2,1)S(1)} copy-done((bf16[384,384]{1,0:T(8,128)(2,1)S(1)}, bf16[384,384]{1,0:T(8,128)(2,1)}, u32[]{:S(2)}) %copy-start.2) | copy-done | bytes 294936
  2.1 0.0 copy-start.4
  2.1 0.9 %copy-done.4 = bf16[4,6,12,384]{3,0,2,1:T(4,128)(2,1)S(1)} copy-done((bf16[4,6,12,384]{3,0,2,1:T(4,128)(2,1)S(1)}, bf16[4,6,12,384]{3,0,2,1:T(4,128)(2,1)}, u32[]{:S(2)}) %copy-start.4) | copy-done | bytes 221208
  3.1 0.0 copy-start.5
  3.1 0.9 %copy-done.5 = bf16[1,2,12,3312]{3,1,2,0:T(2,128)(2,1)S(1)} copy-done((bf16[1,2,12,3312]{3,1,2,0:T(2,128)(2,1)S(1)}, bf16[1,2,12,3312]{3,1,2,0:T(2,128)(2,1)}, u32[]{:S(2)}) %copy-start.5) | copy-done | bytes 159000
  4.0 0.0 copy-start.7
  4.0 0.9 %copy-done.7 = s32[144,144]{1,0:T(8,128)S(1)} copy-done((s32[144,144]{1,0:T(8,128)S(1)}, s32[144,144]{1,0:T(8,128)}, u32[]{:S(2)}) %copy-start.7) | copy-done | bytes 82968
  4.9 0.0 copy-start.9
  4.9 0.7 copy-done.9
  5.6 0.0 copy-start.10
  5.6 0.7 copy-done.10
  6.3 0.0 copy-start.6
  6.3 0.0 copy-start.8
  6.3 12.9 %first_block.1 = (bf16[288,384]{1,0:T(8,128)(2,1)S(1)}, bf16[2,72,384]{2,1,0:T(8,128)(2,1)S(1)}, bf16[2,72,384]{2,1,0:T(8,128)(2,1)S(1)}) custom-call(bf16[72,4,384]{2,1,0:T(4,128)(2,1)S(1)} %bitcast.15, s32[144,144]{1,0:T(8,128)S(1)} %copy-done.7, f32[384]{0:T(512)S(1)} %copy-done.9, bf16[384,1152]{1,0:T(8,128)(2,1)S(1)} %copy-done, ...), custom_call_target="tpu_custom_call" | custom-call | flops 1000000000 | bytes 3000000 | tf_op jit(solution)/shard_map/first_block/pallas_call | solution.py:376
  19.2 0.0 copy-done.6
  19.2 3.6 %collective-permute-start.2 = (bf16[12,2,3312]{2,1,0:T(2,128)(2,1)S(1)}, bf16[12,2,3312]{2,1,0:T(2,128)(2,1)S(1)}, u32[]{:S(2)}, u32[]{:S(2)}) collective-permute-start(bf16[12,2,3312]{2,1,0:T(2,128)(2,1)S(1)} %bitcast.17), channel_id=1, source_target_pairs={{0,32},{32,64},{64,96},{96,128},{128,160},{160,192},{192,224},{224... | collective-permute-start | bytes 476936 | tf_op jit(solution)/shard_map/ppermute | solution.py:361
  22.8 13.1 %collective-permute-start.1 = (bf16[2,72,384]{2,1,0:T(8,128)(2,1)S(1)}, bf16[2,72,384]{2,1,0:T(8,128)(2,1)S(1)}, u32[]{:S(2)}, u32[]{:S(2)}) collective-permute-start(bf16[2,72,384]{2,1,0:T(8,128)(2,1)S(1)} %get-tuple-element.20.west_ref), channel_id=1, source_target_pairs={{0,31},{1,0},{2,1},{3,2},{4,3},{5,4},{6,5},{7,6},{8,7},{9,8},{10,9... | collective-permute-start | bytes 331784 | tf_op jit(solution)/shard_map/ppermute | solution.py:361
  35.9 1.9 %collective-permute-start = (bf16[2,72,384]{2,1,0:T(8,128)(2,1)S(1)}, bf16[2,72,384]{2,1,0:T(8,128)(2,1)S(1)}, u32[]{:S(2)}, u32[]{:S(2)}) collective-permute-start(bf16[2,72,384]{2,1,0:T(8,128)(2,1)S(1)} %get-tuple-element.21.east_ref), channel_id=1, source_target_pairs={{0,1},{1,2},{2,3},{3,4},{4,5},{5,6},{6,7},{7,8},{8,9},{9,10},{10,1... | collective-permute-start | bytes 331784 | tf_op jit(solution)/shard_map/ppermute | solution.py:361
  37.8 0.0 collective-permute-done.2.before_ref
  37.9 0.0 copy-done.8
  37.9 10.8 %second_bias.1.bias_ref = s32[12,192,128]{2,1,0:T(8,128)S(1)} custom-call(s32[144,144]{1,0:T(8,128)S(1)} %copy-done.8, bf16[12,2,3312]{2,1,0:T(2,128)(2,1)S(1)} %bitcast.18, bf16[12,2,3312]{2,1,0:T(2,128)(2,1)S(1)} %collective-permute-done.2.before_ref, s32[1]{0:T(128)} %bitcast.8.lat_ref), custom_call_target="tpu_custom_call" | custom-call | flops 1000000000 | bytes 10000000 | tf_op jit(solution)/shard_map/second_bias/pallas_call | solution.py:410
  48.7 0.0 copy-start.1
  48.7 0.0 copy-start.3
  48.7 0.0 collective-permute-done.1.from_east_ref
  48.8 0.0 collective-permute-done.from_west_ref
  48.8 0.7 %pad_maximum_fusion = bf16[4,72,384]{2,1,0:T(8,128)(2,1)} fusion(bf16[1,72,384]{2,1,0:T(8,128)(2,1)S(1)} %get-tuple-element.35, bf16[1,72,384]{2,1,0:T(8,128)(2,1)S(1)} %get-tuple-element.30, bf16[1,72,384]{2,1,0:T(8,128)(2,1)S(1)} %get-tuple-element.33, bf16[1,72,384]{2,1,0:T(8,128)(2,1)S(1)} %get-tuple-element.26), kind=kLoop, calls=%fused_computation | loop fusion | flops 331776 | bytes 442368 | tf_op jit(solution)/shard_map/stack | solution.py:429
  49.6 2.8 %collective-permute-start.3 = (bf16[4,72,384]{2,1,0:T(8,128)(2,1)}, bf16[4,72,384]{2,1,0:T(8,128)(2,1)S(1)}, u32[]{:S(2)}, u32[]{:S(2)}) collective-permute-start(bf16[4,72,384]{2,1,0:T(8,128)(2,1)} %pad_maximum_fusion), channel_id=1, source_target_pairs={{0,32},{32,64},{64,96},{96,128},{128,160},{160,192},{192,224},{224... | collective-permute-start | bytes 663560 | tf_op jit(solution)/shard_map/ppermute | solution.py:361
  52.4 0.7 %pad_maximum_fusion.1 = bf16[4,72,384]{2,1,0:T(8,128)(2,1)} fusion(bf16[1,72,384]{2,1,0:T(8,128)(2,1)S(1)} %get-tuple-element.36, bf16[1,72,384]{2,1,0:T(8,128)(2,1)S(1)} %get-tuple-element.29, bf16[1,72,384]{2,1,0:T(8,128)(2,1)S(1)} %get-tuple-element.34, bf16[1,72,384]{2,1,0:T(8,128)(2,1)S(1)} %get-tuple-element.25), kind=kLoop, calls=%fused_computation.1 | loop fusion | flops 331776 | bytes 442368 | tf_op jit(solution)/shard_map/stack | solution.py:428
  53.1 1.9 %collective-permute-start.4 = (bf16[4,72,384]{2,1,0:T(8,128)(2,1)}, bf16[4,72,384]{2,1,0:T(8,128)(2,1)S(1)}, u32[]{:S(2)}, u32[]{:S(2)}) collective-permute-start(bf16[4,72,384]{2,1,0:T(8,128)(2,1)} %pad_maximum_fusion.1), channel_id=1, source_target_pairs={{32,0},{64,32},{96,64},{128,96},{160,128},{192,160},{224,192},{256... | collective-permute-start | bytes 663560 | tf_op jit(solution)/shard_map/ppermute | solution.py:361
  55.0 0.1 add_convert_fusion.edge_ref
  55.1 0.4 collective-permute-done.3.north_ref
  55.5 5.9 %collective-permute-done.4.south_ref = bf16[4,72,384]{2,1,0:T(8,128)(2,1)S(1)} collective-permute-done((bf16[4,72,384]{2,1,0:T(8,128)(2,1)}, bf16[4,72,384]{2,1,0:T(8,128)(2,1)S(1)}, u32[]{:S(2)}, u32[]{:S(2)}) %collective-permute-start.4) | collective-permute-done | bytes 221216 | tf_op jit(solution)/shard_map/ppermute | solution.py:361
  61.4 0.0 copy-done.1
  61.4 0.0 copy-done.3
  61.4 6.8 %second_block.1 = bf16[72,4,384]{2,1,0:T(4,128)(2,1)} custom-call(s32[2]{0:T(128)S(1)} %add_convert_fusion.edge_ref, bf16[288,384]{1,0:T(8,128)(2,1)S(1)} %get-tuple-element.16.first_ref, bf16[2,72,384]{2,1,0:T(8,128)(2,1)S(1)} %get-tuple-element.20.west_ref, bf16[2,72,384]{2,1,0:T(8,128)(2,1)S(1)} %get-tuple-element.21.east_ref, ...), custom_call_target="tpu_custom_call" | custom-call | flops 1000000000 | bytes 5000000 | tf_op jit(solution)/shard_map/second_block/pallas_call | solution.py:434
  (2 shorter events, 0.1 us)
Async XLA Ops:
  0.0 1.2 %copy-start = (bf16[384,1152]{1,0:T(8,128)(2,1)S(1)}, bf16[384,1152]{1,0:T(8,128)(2,1)}, u32[]{:S(2)}) copy-start(bf16[384,1152]{1,0:T(8,128)(2,1)} %wqkv_ref.2) | copy-start | bytes 2654212
  1.2 1.0 %copy-start.2 = (bf16[384,384]{1,0:T(8,128)(2,1)S(1)}, bf16[384,384]{1,0:T(8,128)(2,1)}, u32[]{:S(2)}) copy-start(bf16[384,384]{1,0:T(8,128)(2,1)} %wo_ref.2) | copy-start | bytes 884740
  2.1 0.9 %copy-start.4 = (bf16[4,6,12,384]{3,0,2,1:T(4,128)(2,1)S(1)}, bf16[4,6,12,384]{3,0,2,1:T(4,128)(2,1)}, u32[]{:S(2)}) copy-start(bf16[4,6,12,384]{3,0,2,1:T(4,128)(2,1)} %param.10) | copy-start | bytes 663556
  3.1 0.9 %copy-start.5 = (bf16[1,2,12,3312]{3,1,2,0:T(2,128)(2,1)S(1)}, bf16[1,2,12,3312]{3,1,2,0:T(2,128)(2,1)}, u32[]{:S(2)}) copy-start(bf16[1,2,12,3312]{3,1,2,0:T(2,128)(2,1)} %param.15) | copy-start | bytes 476932
  4.0 0.9 %copy-start.7 = (s32[144,144]{1,0:T(8,128)S(1)}, s32[144,144]{1,0:T(8,128)}, u32[]{:S(2)}) copy-start(s32[144,144]{1,0:T(8,128)} %idx_ref.3) | copy-start | bytes 248836
  4.9 0.7 copy-start.9
  5.6 0.7 copy-start.10
  6.3 12.9 %copy-start.6 = (bf16[1,2,12,3312]{3,1,2,0:T(2,128)(2,1)S(1)}, bf16[1,2,12,3312]{3,1,2,0:T(2,128)(2,1)}, u32[]{:S(2)}) copy-start(bf16[1,2,12,3312]{3,1,2,0:T(2,128)(2,1)} %param.19) | copy-start | bytes 476932
  6.3 31.6 %copy-start.8 = (s32[144,144]{1,0:T(8,128)S(1)}, s32[144,144]{1,0:T(8,128)}, u32[]{:S(2)}) copy-start(s32[144,144]{1,0:T(8,128)} %idx_ref.3) | copy-start | bytes 248836
  19.2 18.7 %collective-permute-start.2 = (bf16[12,2,3312]{2,1,0:T(2,128)(2,1)S(1)}, bf16[12,2,3312]{2,1,0:T(2,128)(2,1)S(1)}, u32[]{:S(2)}, u32[]{:S(2)}) collective-permute-start(bf16[12,2,3312]{2,1,0:T(2,128)(2,1)S(1)} %bitcast.17), channel_id=1, source_target_pairs={{0,32},{32,64},{64,96},{96,128},{128,160},{160,192},{192,224},{224... | collective-permute-start | bytes 476936 | tf_op jit(solution)/shard_map/ppermute | solution.py:361
  22.8 26.0 %collective-permute-start.1 = (bf16[2,72,384]{2,1,0:T(8,128)(2,1)S(1)}, bf16[2,72,384]{2,1,0:T(8,128)(2,1)S(1)}, u32[]{:S(2)}, u32[]{:S(2)}) collective-permute-start(bf16[2,72,384]{2,1,0:T(8,128)(2,1)S(1)} %get-tuple-element.20.west_ref), channel_id=1, source_target_pairs={{0,31},{1,0},{2,1},{3,2},{4,3},{5,4},{6,5},{7,6},{8,7},{9,8},{10,9... | collective-permute-start | bytes 331784 | tf_op jit(solution)/shard_map/ppermute | solution.py:361
  35.9 12.8 %collective-permute-start = (bf16[2,72,384]{2,1,0:T(8,128)(2,1)S(1)}, bf16[2,72,384]{2,1,0:T(8,128)(2,1)S(1)}, u32[]{:S(2)}, u32[]{:S(2)}) collective-permute-start(bf16[2,72,384]{2,1,0:T(8,128)(2,1)S(1)} %get-tuple-element.21.east_ref), channel_id=1, source_target_pairs={{0,1},{1,2},{2,3},{3,4},{4,5},{5,6},{6,7},{7,8},{8,9},{9,10},{10,1... | collective-permute-start | bytes 331784 | tf_op jit(solution)/shard_map/ppermute | solution.py:361
  48.7 12.7 %copy-start.1 = (bf16[384,1152]{1,0:T(8,128)(2,1)S(1)}, bf16[384,1152]{1,0:T(8,128)(2,1)}, u32[]{:S(2)}) copy-start(bf16[384,1152]{1,0:T(8,128)(2,1)} %wqkv_ref.3) | copy-start | bytes 2654212
  48.7 12.7 %copy-start.3 = (bf16[384,384]{1,0:T(8,128)(2,1)S(1)}, bf16[384,384]{1,0:T(8,128)(2,1)}, u32[]{:S(2)}) copy-start(bf16[384,384]{1,0:T(8,128)(2,1)} %wo_ref.3) | copy-start | bytes 884740
  49.6 6.0 %collective-permute-start.3 = (bf16[4,72,384]{2,1,0:T(8,128)(2,1)}, bf16[4,72,384]{2,1,0:T(8,128)(2,1)S(1)}, u32[]{:S(2)}, u32[]{:S(2)}) collective-permute-start(bf16[4,72,384]{2,1,0:T(8,128)(2,1)} %pad_maximum_fusion), channel_id=1, source_target_pairs={{0,32},{32,64},{64,96},{96,128},{128,160},{160,192},{192,224},{224... | collective-permute-start | bytes 663560 | tf_op jit(solution)/shard_map/ppermute | solution.py:361
  53.1 8.3 %collective-permute-start.4 = (bf16[4,72,384]{2,1,0:T(8,128)(2,1)}, bf16[4,72,384]{2,1,0:T(8,128)(2,1)S(1)}, u32[]{:S(2)}, u32[]{:S(2)}) collective-permute-start(bf16[4,72,384]{2,1,0:T(8,128)(2,1)} %pad_maximum_fusion.1), channel_id=1, source_target_pairs={{32,0},{64,32},{96,64},{128,96},{160,128},{192,160},{224,192},{256... | collective-permute-start | bytes 663560 | tf_op jit(solution)/shard_map/ppermute | solution.py:361

commit v3 on v2

--- a/solution.py
+++ b/solution.py
@@ -205,10 +205,20 @@
 
 
 def first_kernel(
-    tok_ref, idx_ref, gain_ref, wqkv_ref, wo_ref, table_ref, gain2_ref,
+    idx_in, table_in, tok_in, wqkv_in, wo_in, gain_in, gain2_in,
     first_ref, west_ref, east_ref,
+    idx_ref, table_ref, tok_ref, wqkv_ref, wo_ref, gain_ref, gain2_ref, sems,
     values_ref, packed, high_ref, low_ref, bias_ref, qbuf, kpad, vpad, obuf,
 ):
+    pairs = (
+        (idx_in, idx_ref), (table_in, table_ref), (tok_in, tok_ref), (wqkv_in, wqkv_ref),
+        (wo_in, wo_ref), (gain_in, gain_ref), (gain2_in, gain2_ref),
+    )
+    copies = [pltpu.make_async_copy(src, dst, sems.at[i]) for i, (src, dst) in enumerate(pairs)]
+    for copy in copies:
+        copy.start()
+    copies[0].wait()
+    copies[1].wait()
     pack_table(table_ref, packed)
     high, low = split_index(idx_ref[...])
     columns, gather_rows = tail_columns(), tail_rows(18)
@@ -216,6 +226,8 @@
     place_index(low, columns, gather_rows, low_ref, 0, 18)
     expand(packed, high_ref, low_ref, bias_ref, 0, 21)
 
+    for copy in copies[2:]:
+        copy.wait()
     for g in range(72):
         values_ref[4 * g : 4 * g + 4, :] = tok_ref[g].astype(F32)
     values = dot(natural_from_given(), values_ref[...].astype(BF16))
@@ -255,13 +267,19 @@
         east_ref[a] = parts[144 + 72 * a : 144 + 72 * a + 72]
 
 
-def bias_kernel(
-    idx_ref, table_ref, before_ref, lat_ref,
-    bias_ref,
-    packed, high_ref, low_ref,
-):
-    pack_table(table_ref, packed.at[1])
-    pack_table(before_ref, packed.at[0])
+def fill_bias(lat_ref, idx_in, table_in, before_in, bias_ref, idx_ref, tables, packed, high_ref, low_ref, sems):
+    copies = [
+        pltpu.make_async_copy(src, dst, sems.at[i])
+        for i, (src, dst) in enumerate(
+            ((idx_in, idx_ref), (before_in, tables.at[0]), (table_in, tables.at[1]))
+        )
+    ]
+    for copy in copies:
+        copy.start()
+    for copy in copies:
+        copy.wait()
+    pack_table(tables.at[0], packed.at[0])
+    pack_table(tables.at[1], packed.at[1])
 
     @pl.when(lat_ref[0] == 0)
     def _():
@@ -282,6 +300,18 @@
             dst[start + 80 : start + 96, :] = tail.astype(I32)
     for a in range(2):
         expand(packed.at[a], high_ref, low_ref, bias_ref, a * 96, 12)
+
+
+def early_kernel(where_ref, idx_in, table_in, before_in, bias_ref, *scratch):
+    @pl.when(where_ref[1] == 1)
+    def _():
+        fill_bias(where_ref, idx_in, table_in, before_in, bias_ref, *scratch)
+
+
+def late_kernel(where_ref, idx_in, table_in, before_in, bias_in, bias_ref, *scratch):
+    @pl.when(where_ref[1] == 0)
+    def _():
+        fill_bias(where_ref, idx_in, table_in, before_in, bias_ref, *scratch)
 
 
 def second_kernel(
@@ -352,7 +382,10 @@
 
 VMEM = pl.BlockSpec(memory_space=pltpu.VMEM)
 SMEM = pl.BlockSpec(memory_space=pltpu.SMEM)
-LIMIT = 48 * 1024 * 1024
+HBM = pl.BlockSpec(memory_space=pltpu.HBM)
+ANY = pl.BlockSpec(memory_space=pl.ANY)
+LIMIT = 32 * 1024 * 1024
+WIDE = 60 * 1024 * 1024
 
 
 def shift(block, axis, by, wrap):
@@ -373,6 +406,11 @@
     last = lax.axis_size("lat") - 1
     params = pltpu.CompilerParams(vmem_limit_bytes=LIMIT)
 
+    part = max(1, lax.axis_size("lon") // 2)
+    where = jnp.stack([lat, (lax.axis_index("lon") % part == 0).astype(lat.dtype)]).astype(I32)
+    table = bias_second.transpose(0, 2, 1, 3).reshape(HEADS, 2, POS)
+    before = shift(table, "lat", 1, False)
+
     first, west, east = pl.pallas_call(
         first_kernel,
         out_shape=(
@@ -380,9 +418,17 @@
             jax.ShapeDtypeStruct((2, 72, D), BF16),
             jax.ShapeDtypeStruct((2, 72, D), BF16),
         ),
-        in_specs=[VMEM] * 7,
+        in_specs=[HBM] * 7,
         out_specs=(VMEM,) * 3,
         scratch_shapes=[
+            pltpu.VMEM((WIN, WIN), I32),
+            pltpu.VMEM((HEADS, 2, POS), BF16),
+            pltpu.VMEM((72, 4, D), BF16),
+            pltpu.VMEM((D, 3 * D), BF16),
+            pltpu.VMEM((D, D), BF16),
+            pltpu.VMEM((D,), F32),
+            pltpu.VMEM((D,), F32),
+            pltpu.SemaphoreType.DMA((7,)),
             pltpu.VMEM((288, D), F32),
             pltpu.VMEM((HEADS, CHUNKS * 128), I32),
             pltpu.VMEM((168, 128), I32),
@@ -393,34 +439,50 @@
             pltpu.VMEM((2, 256, D), BF16),
             pltpu.VMEM((288, D), BF16),
         ],
-        compiler_params=params,
+        compiler_params=pltpu.CompilerParams(vmem_limit_bytes=WIDE),
         cost_estimate=cost(10**9, 3 * 10**6),
         name="first_block",
     )(
-        tokens.transpose(1, 2, 0, 3).reshape(72, 4, D), position_index, gain_first, qkv_first, proj_first,
-        bias_first.transpose(0, 2, 1, 3).reshape(HEADS, 2, POS), gain_second,
+        position_index,
+        bias_first.transpose(0, 2, 1, 3).reshape(HEADS, 2, POS),
+        tokens.transpose(1, 2, 0, 3).reshape(72, 4, D),
+        qkv_first, proj_first, gain_first, gain_second,
     )
 
-    table = bias_second.transpose(0, 2, 1, 3).reshape(HEADS, 2, POS)
-    table, first = lax.optimization_barrier((table, first))
-    before = shift(table, "lat", 1, False)
+    bias_shape = jax.ShapeDtypeStruct((HEADS, 192, 128), I32)
+    bias_scratch = [
+        pltpu.VMEM((WIN, WIN), I32),
+        pltpu.VMEM((2, HEADS, 2, POS), BF16),
+        pltpu.VMEM((2, HEADS, CHUNKS * 128), I32),
+        pltpu.VMEM((192, 128), I32),
+        pltpu.VMEM((192, 128), I32),
+        pltpu.SemaphoreType.DMA((3,)),
+    ]
+    before, west, east = lax.optimization_barrier((before, west, east))
+    bias = pl.pallas_call(
+        early_kernel,
+        out_shape=bias_shape,
+        in_specs=[SMEM, HBM, HBM, ANY],
+        out_specs=VMEM,
+        scratch_shapes=bias_scratch,
+        compiler_params=params,
+        cost_estimate=cost(10**6, 10**5),
+        name="early_bias",
+    )(where, position_index, table, before)
+    bias, west, east = lax.optimization_barrier((bias, west, east))
+    from_east = shift(west, "lon", -1, True)
     from_west = shift(east, "lon", 1, True)
-    from_east = shift(west, "lon", -1, True)
-
     bias = pl.pallas_call(
-        bias_kernel,
-        out_shape=jax.ShapeDtypeStruct((HEADS, 192, 128), I32),
-        in_specs=[VMEM] * 3 + [SMEM],
+        late_kernel,
+        out_shape=bias_shape,
+        in_specs=[SMEM, HBM, HBM, ANY, VMEM],
         out_specs=VMEM,
-        scratch_shapes=[
-            pltpu.VMEM((2, HEADS, CHUNKS * 128), I32),
-            pltpu.VMEM((192, 128), I32),
-            pltpu.VMEM((192, 128), I32),
-        ],
+        scratch_shapes=bias_scratch,
+        input_output_aliases={4: 0},
         compiler_params=params,
         cost_estimate=cost(10**9, 10**7),
-        name="second_bias",
-    )(position_index, table, before, lat.astype(I32).reshape(1))
+        name="late_bias",
+    )(where, position_index, table, before, bias)
 
     west, east, from_west, from_east, bias = lax.optimization_barrier(
         (west, east, from_west, from_east, bias)

time: 68.7 us -> 65.7 us (0.956)
  the two profiles are of different devices: /device:TPU:11 before, /device:TPU:57 now
where the time goes in v3:
time: 65.7 us; the launch traced here: 65.5 us
  Pallas kernels  34.1 us (52%)
  starting transfers between devices  23.3 us (35%)
  waiting for transfers between devices  5.97 us (9%)
  other arithmetic  1.61 us (2%)
    ppermute x5, starting transfers between devices, shift(): return lax.ppermute(block, axis, route)  23.3 us
    pallas_call x1, Pallas kernels, shards(): pl.pallas_call(first_kernel, out_shape=(jax.ShapeDtypeStruct((288, D), BF...  14.7 us
    pallas_call x1, Pallas kernels, shards(): pl.pallas_call(late_kernel, out_shape=bias_shape, in_specs=[SMEM, HBM, HB...  12 us
    pallas_call x1, Pallas kernels, shards(): pl.pallas_call(second_kernel, out_shape=jax.ShapeDtypeStruct((72, 4, D),...  6.85 us
    ppermute x5, waiting for transfers between devices, shift(): return lax.ppermute(block, axis, route)  5.97 us
  transfers between devices with their start and end apart: 5, of which 2 were waited for; matrix products, arithmetic and copies ran while one was open for 1% of the time, Pallas kernels for 41%

profile of v3, /device:TPU:57, one launch (start us, length us, event | category | flops | bytes accessed | tf_op | source)
XLA Modules:
  0.0 65.5 jit_solution(8498745167645776494)
XLA Ops:
  0.0 3.8 %collective-permute-start = (bf16[12,2,3312]{2,1,0:T(2,128)(2,1)}, bf16[12,2,3312]{2,1,0:T(2,128)(2,1)S(1)}, u32[]{:S(2)}, u32[]{:S(2)}) collective-permute-start(bf16[12,2,3312]{2,1,0:T(2,128)(2,1)} %bitcast.16), channel_id=1, source_target_pairs={{0,32},{32,64},{64,96},{96,128},{128,160},{160,192},{192,224},{224... | collective-permute-start | bytes 476936 | tf_op jit(solution)/shard_map/ppermute | solution.py:394
  3.9 0.0 copy-start.4
  3.9 0.0 copy-start.5
  3.9 14.7 %first_block.1 = (bf16[288,384]{1,0:T(8,128)(2,1)}, bf16[2,72,384]{2,1,0:T(8,128)(2,1)}, bf16[2,72,384]{2,1,0:T(8,128)(2,1)}) custom-call(s32[144,144]{1,0:T(8,128)} %idx_in.5, bf16[12,2,3312]{2,1,0:T(2,128)(2,1)} %bitcast.20, bf16[72,4,384]{2,1,0:T(4,128)(2,1)} %bitcast.19, bf16[384,1152]{1,0:T(8,128)(2,1)} %wqkv_in.1, bf16[384,384]{1,0:T(8,128)(2,1)} %wo_in.1, ...), custom_call_target="tpu_custom_call" | custom-call | flops 1000000000 | bytes 3000000 | tf_op jit(solution)/shard_map/first_block/pallas_call | solution.py:414
  18.6 0.0 copy-start
  18.6 0.0 copy-start.1
  18.6 0.1 pad_add_fusion.where_ref
  18.7 0.0 collective-permute-done.before_in
  18.7 0.0 copy-done.4
  18.7 0.0 copy-done.5
  18.7 0.6 early_bias.1.bias_in
  19.3 0.2 copy-done
  19.5 13.0 %collective-permute-start.2 = (bf16[2,72,384]{2,1,0:T(8,128)(2,1)S(1)}, bf16[2,72,384]{2,1,0:T(8,128)(2,1)S(1)}, u32[]{:S(2)}, u32[]{:S(2)}) collective-permute-start(bf16[2,72,384]{2,1,0:T(8,128)(2,1)S(1)} %copy-done), channel_id=1, source_target_pairs={{0,31},{1,0},{2,1},{3,2},{4,3},{5,4},{6,5},{7,6},{8,7},{9,8},{10,9... | collective-permute-start | bytes 331784 | tf_op jit(solution)/shard_map/ppermute | solution.py:394
  32.5 0.0 copy-done.1
  32.5 1.9 %collective-permute-start.1 = (bf16[2,72,384]{2,1,0:T(8,128)(2,1)S(1)}, bf16[2,72,384]{2,1,0:T(8,128)(2,1)S(1)}, u32[]{:S(2)}, u32[]{:S(2)}) collective-permute-start(bf16[2,72,384]{2,1,0:T(8,128)(2,1)S(1)} %copy-done.1), channel_id=1, source_target_pairs={{0,1},{1,2},{2,3},{3,4},{4,5},{5,6},{6,7},{7,8},{8,9},{9,10},{10,1... | collective-permute-start | bytes 331784 | tf_op jit(solution)/shard_map/ppermute | solution.py:394
  34.4 12.0 %late_bias.1.bias_ref = s32[12,192,128]{2,1,0:T(8,128)S(1)} custom-call(s32[2]{0:T(128)S(1)} %pad_add_fusion.where_ref, s32[144,144]{1,0:T(8,128)S(1)} %copy-done.5, bf16[12,2,3312]{2,1,0:T(2,128)(2,1)S(1)} %bitcast.18, bf16[12,2,3312]{2,1,0:T(2,128)(2,1)S(1)} %collective-permute-done.before_in, ...), custom_call_target="tpu_custom_call", output_to_operand_aliasing={{}: (4, {})} | custom-call | flops 1000000000 | bytes 10000000 | tf_op jit(solution)/shard_map/late_bias/pallas_call | solution.py:475
  46.5 0.0 copy-start.2
  46.5 0.0 copy-start.3
  46.5 0.0 copy-start.6
  46.5 0.0 collective-permute-done.2.from_east_ref
  46.5 0.0 collective-permute-done.1.from_west_ref
  46.6 0.7 %pad_maximum_fusion = bf16[4,72,384]{2,1,0:T(8,128)(2,1)} fusion(bf16[1,72,384]{2,1,0:T(8,128)(2,1)S(1)} %get-tuple-element.43, bf16[1,72,384]{2,1,0:T(8,128)(2,1)S(1)} %get-tuple-element.38, bf16[1,72,384]{2,1,0:T(8,128)(2,1)S(1)} %get-tuple-element.41, bf16[1,72,384]{2,1,0:T(8,128)(2,1)S(1)} %get-tuple-element.34), kind=kLoop, calls=%fused_computation | loop fusion | flops 331776 | bytes 442368 | tf_op jit(solution)/shard_map/stack | solution.py:491
  47.3 2.2 %collective-permute-start.3 = (bf16[4,72,384]{2,1,0:T(8,128)(2,1)}, bf16[4,72,384]{2,1,0:T(8,128)(2,1)S(1)}, u32[]{:S(2)}, u32[]{:S(2)}) collective-permute-start(bf16[4,72,384]{2,1,0:T(8,128)(2,1)} %pad_maximum_fusion), channel_id=1, source_target_pairs={{0,32},{32,64},{64,96},{96,128},{128,160},{160,192},{192,224},{224... | collective-permute-start | bytes 663560 | tf_op jit(solution)/shard_map/ppermute | solution.py:394
  49.5 0.7 %pad_maximum_fusion.1 = bf16[4,72,384]{2,1,0:T(8,128)(2,1)} fusion(bf16[1,72,384]{2,1,0:T(8,128)(2,1)S(1)} %get-tuple-element.44, bf16[1,72,384]{2,1,0:T(8,128)(2,1)S(1)} %get-tuple-element.37, bf16[1,72,384]{2,1,0:T(8,128)(2,1)S(1)} %get-tuple-element.42, bf16[1,72,384]{2,1,0:T(8,128)(2,1)S(1)} %get-tuple-element.33), kind=kLoop, calls=%fused_computation.1 | loop fusion | flops 331776 | bytes 442368 | tf_op jit(solution)/shard_map/stack | solution.py:490
  50.2 2.3 %collective-permute-start.4 = (bf16[4,72,384]{2,1,0:T(8,128)(2,1)}, bf16[4,72,384]{2,1,0:T(8,128)(2,1)S(1)}, u32[]{:S(2)}, u32[]{:S(2)}) collective-permute-start(bf16[4,72,384]{2,1,0:T(8,128)(2,1)} %pad_maximum_fusion.1), channel_id=1, source_target_pairs={{32,0},{64,32},{96,64},{128,96},{160,128},{192,160},{224,192},{256... | collective-permute-start | bytes 663560 | tf_op jit(solution)/shard_map/ppermute | solution.py:394
  52.6 0.1 add_convert_fusion.edge_ref
  52.6 0.1 collective-permute-done.3.north_ref
  52.7 5.9 %collective-permute-done.4.south_ref = bf16[4,72,384]{2,1,0:T(8,128)(2,1)S(1)} collective-permute-done((bf16[4,72,384]{2,1,0:T(8,128)(2,1)}, bf16[4,72,384]{2,1,0:T(8,128)(2,1)S(1)}, u32[]{:S(2)}, u32[]{:S(2)}) %collective-permute-start.4) | collective-permute-done | bytes 221216 | tf_op jit(solution)/shard_map/ppermute | solution.py:394
  58.6 0.0 copy-done.2
  58.6 0.0 copy-done.3
  58.6 0.0 copy-done.6
  58.6 6.8 %second_block.1 = bf16[72,4,384]{2,1,0:T(4,128)(2,1)} custom-call(s32[2]{0:T(128)S(1)} %add_convert_fusion.edge_ref, bf16[288,384]{1,0:T(8,128)(2,1)S(1)} %copy-done.6, bf16[2,72,384]{2,1,0:T(8,128)(2,1)S(1)} %copy-done, bf16[2,72,384]{2,1,0:T(8,128)(2,1)S(1)} %copy-done.1, bf16[2,72,384]{2,1,0:T(8,128)(2,1)S(1)} %collective-permute-done.1.from_west_ref, ...), custom_call_target="tpu_custom_call" | custom-call | flops 1000000000 | bytes 5000000 | tf_op jit(solution)/shard_map/second_block/pallas_call | solution.py:496
  (2 shorter events, 0.1 us)
Async XLA Ops:
  0.0 18.7 %collective-permute-start = (bf16[12,2,3312]{2,1,0:T(2,128)(2,1)}, bf16[12,2,3312]{2,1,0:T(2,128)(2,1)S(1)}, u32[]{:S(2)}, u32[]{:S(2)}) collective-permute-start(bf16[12,2,3312]{2,1,0:T(2,128)(2,1)} %bitcast.16), channel_id=1, source_target_pairs={{0,32},{32,64},{64,96},{96,128},{128,160},{160,192},{192,224},{224... | collective-permute-start | bytes 476936 | tf_op jit(solution)/shard_map/ppermute | solution.py:394
  3.9 14.8 %copy-start.4 = (bf16[1,2,12,3312]{3,1,2,0:T(2,128)(2,1)S(1)}, bf16[1,2,12,3312]{3,1,2,0:T(2,128)(2,1)}, u32[]{:S(2)}) copy-start(bf16[1,2,12,3312]{3,1,2,0:T(2,128)(2,1)} %param.19) | copy-start | bytes 476932
  3.9 14.8 %copy-start.5 = (s32[144,144]{1,0:T(8,128)S(1)}, s32[144,144]{1,0:T(8,128)}, u32[]{:S(2)}) copy-start(s32[144,144]{1,0:T(8,128)} %idx_in.5) | copy-start | bytes 248836
  18.6 0.9 %copy-start = (bf16[2,72,384]{2,1,0:T(8,128)(2,1)S(1)}, bf16[2,72,384]{2,1,0:T(8,128)(2,1)}, u32[]{:S(2)}) copy-start(bf16[2,72,384]{2,1,0:T(8,128)(2,1)} %get-tuple-element.28.west_ref) | copy-start | bytes 331780
  18.6 13.9 %copy-start.1 = (bf16[2,72,384]{2,1,0:T(8,128)(2,1)S(1)}, bf16[2,72,384]{2,1,0:T(8,128)(2,1)}, u32[]{:S(2)}) copy-start(bf16[2,72,384]{2,1,0:T(8,128)(2,1)} %get-tuple-element.29.east_ref) | copy-start | bytes 331780
  19.5 27.0 %collective-permute-start.2 = (bf16[2,72,384]{2,1,0:T(8,128)(2,1)S(1)}, bf16[2,72,384]{2,1,0:T(8,128)(2,1)S(1)}, u32[]{:S(2)}, u32[]{:S(2)}) collective-permute-start(bf16[2,72,384]{2,1,0:T(8,128)(2,1)S(1)} %copy-done), channel_id=1, source_target_pairs={{0,31},{1,0},{2,1},{3,2},{4,3},{5,4},{6,5},{7,6},{8,7},{9,8},{10,9... | collective-permute-start | bytes 331784 | tf_op jit(solution)/shard_map/ppermute | solution.py:394
  32.5 14.0 %collective-permute-start.1 = (bf16[2,72,384]{2,1,0:T(8,128)(2,1)S(1)}, bf16[2,72,384]{2,1,0:T(8,128)(2,1)S(1)}, u32[]{:S(2)}, u32[]{:S(2)}) collective-permute-start(bf16[2,72,384]{2,1,0:T(8,128)(2,1)S(1)} %copy-done.1), channel_id=1, source_target_pairs={{0,1},{1,2},{2,3},{3,4},{4,5},{5,6},{6,7},{7,8},{8,9},{9,10},{10,1... | collective-permute-start | bytes 331784 | tf_op jit(solution)/shard_map/ppermute | solution.py:394
  46.5 12.1 %copy-start.2 = (bf16[384,1152]{1,0:T(8,128)(2,1)S(1)}, bf16[384,1152]{1,0:T(8,128)(2,1)}, u32[]{:S(2)}) copy-start(bf16[384,1152]{1,0:T(8,128)(2,1)} %wqkv_ref.1) | copy-start | bytes 2654212
  46.5 12.1 %copy-start.3 = (bf16[384,384]{1,0:T(8,128)(2,1)S(1)}, bf16[384,384]{1,0:T(8,128)(2,1)}, u32[]{:S(2)}) copy-start(bf16[384,384]{1,0:T(8,128)(2,1)} %wo_ref.1) | copy-start | bytes 884740
  46.5 12.1 %copy-start.6 = (bf16[288,384]{1,0:T(8,128)(2,1)S(1)}, bf16[288,384]{1,0:T(8,128)(2,1)}, u32[]{:S(2)}) copy-start(bf16[288,384]{1,0:T(8,128)(2,1)} %get-tuple-element.19.first_ref) | copy-start | bytes 663556
  47.3 5.4 %collective-permute-start.3 = (bf16[4,72,384]{2,1,0:T(8,128)(2,1)}, bf16[4,72,384]{2,1,0:T(8,128)(2,1)S(1)}, u32[]{:S(2)}, u32[]{:S(2)}) collective-permute-start(bf16[4,72,384]{2,1,0:T(8,128)(2,1)} %pad_maximum_fusion), channel_id=1, source_target_pairs={{0,32},{32,64},{64,96},{96,128},{128,160},{160,192},{192,224},{224... | collective-permute-start | bytes 663560 | tf_op jit(solution)/shard_map/ppermute | solution.py:394
  50.2 8.3 %collective-permute-start.4 = (bf16[4,72,384]{2,1,0:T(8,128)(2,1)}, bf16[4,72,384]{2,1,0:T(8,128)(2,1)S(1)}, u32[]{:S(2)}, u32[]{:S(2)}) collective-permute-start(bf16[4,72,384]{2,1,0:T(8,128)(2,1)} %pad_maximum_fusion.1), channel_id=1, source_target_pairs={{32,0},{64,32},{96,64},{128,96},{160,128},{192,160},{224,192},{256... | collective-permute-start | bytes 663560 | tf_op jit(solution)/shard_map/ppermute | solution.py:394

commit v4 on v3

--- a/solution.py
+++ b/solution.py
@@ -13,9 +13,8 @@
 CHUNKS = 26
 POS = 3312
 LOG2E = float(np.log2(np.e))
-FIX = 8191.0
+FIELDS = ((11, 256.0, 21), (11, 256.0, 10), (10, 128.0, 0))
 SCALE = LOG2E * 32 ** -0.5
-UNFIX = LOG2E / FIX
 
 
 def dot(a, b):
@@ -112,9 +111,20 @@
 
 
 def pack_table(table_ref, packed_ref):
-    for h in range(HEADS):
-        fixed = jnp.round(table_ref[h].astype(F32) * FIX).astype(I32)
-        packed_ref[h : h + 1, 0:POS] = (fixed[0:1] << 16) | (fixed[1:2] & 0xFFFF)
+    for i in range(4):
+        word = None
+        for g, (bits, steps, place) in enumerate(FIELDS):
+            top = 2.0 ** (bits - 1) - 1
+            fixed = jnp.minimum(jnp.round(table_ref[4 * g + i].astype(F32) * steps), top).astype(I32)
+            field = (fixed & (2**bits - 1)) << place
+            word = field if word is None else word | field
+        packed_ref[2 * i : 2 * i + 2, 0:POS] = word
+
+
+def unpack(words, g):
+    bits, steps, place = FIELDS[g]
+    fixed = (words << (32 - bits - place)) >> (32 - bits)
+    return fixed.astype(F32) * (LOG2E / steps)
 
 
 def split_index(position_index):
@@ -138,41 +148,35 @@
     dst_ref[start + rows : start + rows + tail.shape[0], :] = tail.astype(I32)
 
 
-def expand(packed_ref, high_ref, low_ref, out_ref, start, count):
-    def tile(t, carry):
-        rows = pl.ds(pl.multiple_of(start + t * 8, 8), 8)
+def expand(packed_ref, high_ref, low_ref, main_ref, tail_ref, tiles):
+    def picked(t):
+        rows = pl.ds(pl.multiple_of(t * 8, 8), 8)
         low = low_ref[rows, :]
         high = high_ref[rows, :]
-        picked = [None] * HEADS
+        words = [None] * 8
         for c in range(CHUNKS):
             here = high == c
-            for h in range(HEADS):
-                entries = jnp.broadcast_to(packed_ref[h : h + 1, 128 * c : 128 * c + 128], (8, 128))
+            for r in range(8):
+                entries = jnp.broadcast_to(packed_ref[r : r + 1, 128 * c : 128 * c + 128], (8, 128))
                 got = jnp.take_along_axis(entries, low, axis=1, mode="promise_in_bounds")
-                picked[h] = got if c == 0 else jnp.where(here, got, picked[h])
-        for h in range(HEADS):
-            out_ref[h, rows, :] = picked[h]
+                words[r] = got if c == 0 else jnp.where(here, got, words[r])
+        return words
+
+    def main(t, carry):
+        for r, words in enumerate(picked(t)):
+            main_ref[r, pl.ds(pl.multiple_of(t * 8, 8), 8), :] = words
         return carry
 
-    lax.fori_loop(0, count, tile, 0)
-
-
-def bias_tail(bias_ref, h, base, tiles):
-    out = []
-    for t in range(tiles):
-        at = base + (t // 8) * 8
-        part = bias_ref[h, at : at + 8, :]
-        j = t % 8
-        out.append(part if j == 0 else pltpu.roll(part, 128 - 16 * j, 1))
-    return jnp.concatenate(out, axis=0)
-
-
-def upper(packed):
-    return (packed >> 16).astype(F32)
-
-
-def lower(packed):
-    return ((packed << 16) >> 16).astype(F32)
+    def tail(v, carry):
+        for r, words in enumerate(picked(tiles + v)):
+            tail_ref[r, pl.ds(pl.multiple_of(v * 64, 64), 8), :] = words
+            for j in range(1, 8):
+                at = pl.multiple_of(v * 64 + 8 * j, 8)
+                tail_ref[r, pl.ds(at, 8), :] = pltpu.roll(words, 128 - 16 * j, 1)
+        return carry
+
+    lax.fori_loop(0, tiles, main, 0)
+    lax.fori_loop(0, -(-tiles // 8), tail, 0)
 
 
 def layer_norm(values, gain):
@@ -195,7 +199,7 @@
     stacked = jnp.concatenate([jnp.where(own == i, query, 0.0) for i in range(4)], axis=0)
     scores = dot_t(stacked.astype(BF16), key)
     probs = [
-        softmax(scores[n * i : n * i + n] * SCALE + biases[i] * UNFIX, mask) for i in range(4)
+        softmax(scores[n * i : n * i + n] * SCALE + biases[i], mask) for i in range(4)
     ]
     parts = dot(jnp.concatenate(probs, axis=0), value)
     out = parts[0:n]
@@ -208,7 +212,7 @@
     idx_in, table_in, tok_in, wqkv_in, wo_in, gain_in, gain2_in,
     first_ref, west_ref, east_ref,
     idx_ref, table_ref, tok_ref, wqkv_ref, wo_ref, gain_ref, gain2_ref, sems,
-    values_ref, packed, high_ref, low_ref, bias_ref, qbuf, kpad, vpad, obuf,
+    values_ref, packed, high_ref, low_ref, main_ref, tail_ref, qbuf, kpad, vpad, obuf,
 ):
     pairs = (
         (idx_in, idx_ref), (table_in, table_ref), (tok_in, tok_ref), (wqkv_in, wqkv_ref),
@@ -224,7 +228,7 @@
     columns, gather_rows = tail_columns(), tail_rows(18)
     place_index(high, columns, gather_rows, high_ref, 0, 18)
     place_index(low, columns, gather_rows, low_ref, 0, 18)
-    expand(packed, high_ref, low_ref, bias_ref, 0, 21)
+    expand(packed, high_ref, low_ref, main_ref, tail_ref, 18)
 
     for copy in copies[2:]:
         copy.wait()
@@ -245,18 +249,16 @@
     valid = lax.broadcasted_iota(I32, (WIN, 256), 1) < WIN
     for g in range(3):
         lanes = slice(128 * g, 128 * g + 128)
-        biases = []
-        for i in range(4):
-            h = 4 * g + i
-            biases.append(
-                jnp.concatenate([bias_ref[h, 0:WIN, :], bias_tail(bias_ref, h, WIN, 18)], axis=1)
-            )
         for w in range(2):
             rows = slice(WIN * w, WIN * w + WIN)
-            half = upper if w == 0 else lower
+            biases = [
+                unpack(
+                    jnp.concatenate([main_ref[2 * i + w], tail_ref[2 * i + w, 0:WIN, :]], axis=1), g
+                )
+                for i in range(4)
+            ]
             obuf[rows, lanes] = four_heads(
-                qbuf[rows, lanes], kpad[w, :, lanes], vpad[w, :, lanes],
-                [half(x) for x in biases], valid,
+                qbuf[rows, lanes], kpad[w, :, lanes], vpad[w, :, lanes], biases, valid
             ).astype(BF16)
     first = (values_ref[...] + dot(obuf[...], wo_ref[...])).astype(BF16)
     first_ref[...] = first
@@ -267,7 +269,10 @@
         east_ref[a] = parts[144 + 72 * a : 144 + 72 * a + 72]
 
 
-def fill_bias(lat_ref, idx_in, table_in, before_in, bias_ref, idx_ref, tables, packed, high_ref, low_ref, sems):
+def fill_bias(
+    where_ref, idx_in, table_in, before_in, main_ref, tail_ref,
+    idx_ref, tables, packed, high_ref, low_ref, sems,
+):
     copies = [
         pltpu.make_async_copy(src, dst, sems.at[i])
         for i, (src, dst) in enumerate(
@@ -281,7 +286,7 @@
     pack_table(tables.at[0], packed.at[0])
     pack_table(tables.at[1], packed.at[1])
 
-    @pl.when(lat_ref[0] == 0)
+    @pl.when(where_ref[0] == 0)
     def _():
         packed[0] = packed[1]
 
@@ -294,37 +299,50 @@
             spread = jnp.concatenate(
                 [dot(rows[40 * b : 40 * b + 40], columns[b]) for b in range(2)], axis=0
             )
-            start = a * 96
-            dst[start : start + 80, :] = spread[:, :128].astype(I32)
+            dst[a, 0:80, :] = spread[:, :128].astype(I32)
             tail = fold_tail(spread[:, 128:], gather_rows, 10)
-            dst[start + 80 : start + 96, :] = tail.astype(I32)
+            dst[a, 80:96, :] = tail.astype(I32)
     for a in range(2):
-        expand(packed.at[a], high_ref, low_ref, bias_ref, a * 96, 12)
-
-
-def early_kernel(where_ref, idx_in, table_in, before_in, bias_ref, *scratch):
+        expand(packed.at[a], high_ref.at[a], low_ref.at[a], main_ref.at[a], tail_ref.at[a], 10)
+
+
+def early_kernel(where_ref, idx_in, table_in, before_in, main_ref, tail_ref, *scratch):
     @pl.when(where_ref[1] == 1)
     def _():
-        fill_bias(where_ref, idx_in, table_in, before_in, bias_ref, *scratch)
-
-
-def late_kernel(where_ref, idx_in, table_in, before_in, bias_in, bias_ref, *scratch):
+        fill_bias(where_ref, idx_in, table_in, before_in, main_ref, tail_ref, *scratch)
+
+
+def late_kernel(
+    where_ref, idx_in, table_in, before_in, main_in, tail_in, main_ref, tail_ref, *scratch
+):
     @pl.when(where_ref[1] == 0)
     def _():
-        fill_bias(where_ref, idx_in, table_in, before_in, bias_ref, *scratch)
+        fill_bias(where_ref, idx_in, table_in, before_in, main_ref, tail_ref, *scratch)
+
+    @pl.when(where_ref[1] == 1)
+    def _():
+        main_ref[...] = main_in[...]
+        tail_ref[...] = tail_in[...]
+
+
+def stack_kernel(where_ref, west_ref, east_ref, from_west_ref, from_east_ref, seam_ref, up_ref, down_ref):
+    for a, dst in enumerate((up_ref, down_ref)):
+        dst[0] = from_west_ref[a]
+        dst[1] = west_ref[a]
+        dst[2] = east_ref[a]
+        dst[3] = jnp.where(where_ref[2] == 1, seam_ref[a], from_east_ref[a])
 
 
 def second_kernel(
     edge_ref,
-    first_ref, west_ref, east_ref, from_west_ref, from_east_ref, north_ref, south_ref,
-    wqkv_ref, wo_ref, bias_ref,
+    first_ref, up_ref, down_ref, north_ref, south_ref,
+    wqkv_ref, wo_ref, main_ref, tail_ref,
     out_ref,
     cat, window, qbuf, kpad, vpad, obuf,
 ):
-    own = (west_ref, east_ref)
-    beside = (from_west_ref, from_east_ref)
+    here = (up_ref, down_ref)
     beyond = (north_ref, south_ref)
-    tokens = jnp.concatenate([west_ref[0], west_ref[1], east_ref[0], east_ref[1]], axis=0)
+    tokens = jnp.concatenate([up_ref[1], down_ref[1], up_ref[2], down_ref[2]], axis=0)
     asked = dot(queries_from_quadrants(), tokens).astype(BF16)
     qbuf[...] = dot(asked, wqkv_ref[:, 0:D]).astype(BF16).astype(F32)
 
@@ -335,8 +353,8 @@
         for b in range(2):
             q = 2 * a + b
             far = ((1, 0), (2, 3))[b]
-            cat[0:72, :] = own[b][a].astype(F32)
-            cat[80:152, :] = beside[b][a].astype(F32)
+            cat[0:72, :] = here[a][1 + b].astype(F32)
+            cat[80:152, :] = here[a][3 * b].astype(F32)
             cat[160:232, :] = beyond[a][far[0]].astype(F32)
             cat[240:312, :] = beyond[a][far[1]].astype(F32)
             window[288 * q : 288 * q + 288, :] = dot(order, cat[...].astype(BF16)).astype(BF16)
@@ -359,20 +377,22 @@
         masks = (seen, jnp.logical_and(seen, split))
         for g in range(3):
             lanes = slice(128 * g, 128 * g + 128)
-            biases = []
-            for i in range(4):
-                h = 4 * g + i
-                tail = bias_tail(bias_ref, h, 96 * a + 80, 10)
-                biases.append(
-                    jnp.concatenate([bias_ref[h, 96 * a : 96 * a + 80, :], tail], axis=1)
-                )
             for b in range(2):
+                rows = slice(40 * b, 40 * b + 40)
                 for w in range(2):
                     at = 4 * a + 2 * b + w
-                    half = upper if w == 0 else lower
+                    biases = [
+                        unpack(
+                            jnp.concatenate(
+                                [main_ref[a, 2 * i + w, rows, :], tail_ref[a, 2 * i + w, rows, :]], axis=1
+                            ),
+                            g,
+                        )
+                        for i in range(4)
+                    ]
                     obuf[40 * at : 40 * at + 40, lanes] = four_heads(
                         qbuf[40 * at : 40 * at + 40, lanes], kpad[at, :, lanes], vpad[at, :, lanes],
-                        [half(x[40 * b : 40 * b + 40]) for x in biases], masks[w],
+                        biases, masks[w],
                     )
     attended = dot(given_from_queries(), obuf[...].astype(BF16)).astype(BF16)
     qbuf[0:288, :] = dot(given_from_natural(), first_ref[...]) + dot(attended, wo_ref[...])
@@ -406,8 +426,10 @@
     last = lax.axis_size("lat") - 1
     params = pltpu.CompilerParams(vmem_limit_bytes=LIMIT)
 
-    part = max(1, lax.axis_size("lon") // 2)
-    where = jnp.stack([lat, (lax.axis_index("lon") % part == 0).astype(lat.dtype)]).astype(I32)
+    part = lax.axis_size("lon") // 2
+    place = lax.axis_index("lon") % part
+    where = jnp.stack([lat, (place == 0).astype(lat.dtype), (place == part - 1).astype(lat.dtype)])
+    where = where.astype(I32)
     table = bias_second.transpose(0, 2, 1, 3).reshape(HEADS, 2, POS)
     before = shift(table, "lat", 1, False)
 
@@ -430,10 +452,11 @@
             pltpu.VMEM((D,), F32),
             pltpu.SemaphoreType.DMA((7,)),
             pltpu.VMEM((288, D), F32),
-            pltpu.VMEM((HEADS, CHUNKS * 128), I32),
+            pltpu.VMEM((8, CHUNKS * 128), I32),
             pltpu.VMEM((168, 128), I32),
             pltpu.VMEM((168, 128), I32),
-            pltpu.VMEM((HEADS, 168, 128), I32),
+            pltpu.VMEM((8, WIN, 128), I32),
+            pltpu.VMEM((8, 192, 128), I32),
             pltpu.VMEM((288, D), F32),
             pltpu.VMEM((2, 256, D), BF16),
             pltpu.VMEM((2, 256, D), BF16),
@@ -449,46 +472,60 @@
         qkv_first, proj_first, gain_first, gain_second,
     )
 
-    bias_shape = jax.ShapeDtypeStruct((HEADS, 192, 128), I32)
+    bias_shapes = (
+        jax.ShapeDtypeStruct((2, 8, 80, 128), I32),
+        jax.ShapeDtypeStruct((2, 8, 128, 128), I32),
+    )
     bias_scratch = [
         pltpu.VMEM((WIN, WIN), I32),
         pltpu.VMEM((2, HEADS, 2, POS), BF16),
-        pltpu.VMEM((2, HEADS, CHUNKS * 128), I32),
-        pltpu.VMEM((192, 128), I32),
-        pltpu.VMEM((192, 128), I32),
+        pltpu.VMEM((2, 8, CHUNKS * 128), I32),
+        pltpu.VMEM((2, 96, 128), I32),
+        pltpu.VMEM((2, 96, 128), I32),
         pltpu.SemaphoreType.DMA((3,)),
     ]
-    before, west, east = lax.optimization_barrier((before, west, east))
-    bias = pl.pallas_call(
+    from_west = shift(east, "lon", 1, True)
+    size = lax.axis_size("lon")
+    inner = [(i, i - 1) for i in range(size) if i % part]
+    seam = [(i, (i - 1) % size) for i in range(size) if i % part == 0]
+    from_east = lax.ppermute(west, "lon", inner)
+    before, west = lax.optimization_barrier((before, west))
+    main, tail = pl.pallas_call(
         early_kernel,
-        out_shape=bias_shape,
+        out_shape=bias_shapes,
         in_specs=[SMEM, HBM, HBM, ANY],
-        out_specs=VMEM,
+        out_specs=(VMEM, VMEM),
         scratch_shapes=bias_scratch,
         compiler_params=params,
         cost_estimate=cost(10**6, 10**5),
         name="early_bias",
     )(where, position_index, table, before)
-    bias, west, east = lax.optimization_barrier((bias, west, east))
-    from_east = shift(west, "lon", -1, True)
-    from_west = shift(east, "lon", 1, True)
-    bias = pl.pallas_call(
+    main, tail, west = lax.optimization_barrier((main, tail, west))
+    from_seam = lax.ppermute(west, "lon", seam)
+    main, tail = pl.pallas_call(
         late_kernel,
-        out_shape=bias_shape,
-        in_specs=[SMEM, HBM, HBM, ANY, VMEM],
-        out_specs=VMEM,
+        out_shape=bias_shapes,
+        in_specs=[SMEM, HBM, HBM, ANY, VMEM, VMEM],
+        out_specs=(VMEM, VMEM),
         scratch_shapes=bias_scratch,
-        input_output_aliases={4: 0},
         compiler_params=params,
         cost_estimate=cost(10**9, 10**7),
         name="late_bias",
-    )(where, position_index, table, before, bias)
-
-    west, east, from_west, from_east, bias = lax.optimization_barrier(
-        (west, east, from_west, from_east, bias)
+    )(where, position_index, table, before, main, tail)
+
+    west, east, from_west, from_east, from_seam, main, tail = lax.optimization_barrier(
+        (west, east, from_west, from_east, from_seam, main, tail)
     )
-    up = jnp.stack([from_west[0], west[0], east[0], from_east[0]])
-    down = jnp.stack([from_west[1], west[1], east[1], from_east[1]])
+    pieces = jax.ShapeDtypeStruct((4, 72, D), BF16)
+    up, down = pl.pallas_call(
+        stack_kernel,
+        out_shape=(pieces, pieces),
+        in_specs=[SMEM] + [VMEM] * 5,
+        out_specs=(VMEM, VMEM),
+        compiler_params=params,
+        cost_estimate=cost(10**5, 10**6),
+        name="stack_pieces",
+    )(where, west, east, from_west, from_east, from_seam)
     south = shift(up, "lat", -1, False)
     north = shift(down, "lat", 1, False)
 
@@ -496,7 +533,7 @@
     out = pl.pallas_call(
         second_kernel,
         out_shape=jax.ShapeDtypeStruct((72, 4, D), BF16),
-        in_specs=[SMEM] + [VMEM] * 10,
+        in_specs=[SMEM] + [VMEM] * 9,
         out_specs=VMEM,
         scratch_shapes=[
             pltpu.VMEM((320, D), F32),
@@ -510,8 +547,7 @@
         cost_estimate=cost(10**9, 5 * 10**6),
         name="second_block",
     )(
-        edges, first, west, east, from_west, from_east, north, south,
-        qkv_second, proj_second, bias,
+        edges, first, up, down, north, south, qkv_second, proj_second, main, tail,
     )
     return out.reshape(6, 12, 4, D).transpose(2, 0, 1, 3)
 

time: 65.7 us -> 60.7 us (0.924)
  the two profiles are of different devices: /device:TPU:57 before, /device:TPU:9 now
where the time goes in v4:
time: 60.7 us; the launch traced here: 60.4 us
  Pallas kernels  31.1 us (51%)
  starting transfers between devices  19.2 us (32%)
  waiting for transfers between devices  6.68 us (11%)
  local copies, waits for them, and re-layouts  3.1 us (5%)
    ppermute x4, starting transfers between devices, shift(): return lax.ppermute(block, axis, route)  13.2 us
    pallas_call x1, Pallas kernels, shards(): pl.pallas_call(first_kernel, out_shape=(jax.ShapeDtypeStruct((288, D), BF...  12.5 us
    pallas_call x1, Pallas kernels, shards(): pl.pallas_call(early_kernel, out_shape=bias_shapes, in_specs=[SMEM, HBM,...  9.91 us
    pallas_call x1, Pallas kernels, shards(): pl.pallas_call(second_kernel, out_shape=jax.ShapeDtypeStruct((72, 4, D),...  7.4 us
    ppermute x4, waiting for transfers between devices, shift(): return lax.ppermute(block, axis, route)  6.07 us
    ppermute x1, starting transfers between devices, shards(): from_seam = lax.ppermute(west, 'lon', seam)  4.65 us
    unnamed x22, local copies, waits for them, and re-layouts  3.1 us
    ppermute x1, starting transfers between devices, shards(): from_east = lax.ppermute(west, 'lon', inner)  1.29 us
  transfers between devices with their start and end apart: 6, of which 3 were waited for; matrix products, arithmetic and copies ran while one was open for 0% of the time, Pallas kernels for 38%

profile of v4, /device:TPU:9, one launch (start us, length us, event | category | flops | bytes accessed | tf_op | source)
XLA Modules:
  0.0 60.4 jit_solution(10042521511403685762)
XLA Ops:
  0.0 3.6 %collective-permute-start = (bf16[12,2,3312]{2,1,0:T(2,128)(2,1)}, bf16[12,2,3312]{2,1,0:T(2,128)(2,1)S(1)}, u32[]{:S(2)}, u32[]{:S(2)}) collective-permute-start(bf16[12,2,3312]{2,1,0:T(2,128)(2,1)} %bitcast.17), channel_id=1, source_target_pairs={{0,32},{32,64},{64,96},{96,128},{128,160},{160,192},{192,224},{224... | collective-permute-start | bytes 476936 | tf_op jit(solution)/shard_map/ppermute | solution.py:414
  3.6 0.0 copy-start.3
  3.6 0.0 copy-start.4
  3.6 12.5 %first_block.1 = (bf16[288,384]{1,0:T(8,128)(2,1)}, bf16[2,72,384]{2,1,0:T(8,128)(2,1)}, bf16[2,72,384]{2,1,0:T(8,128)(2,1)}) custom-call(s32[144,144]{1,0:T(8,128)} %idx_in.5, bf16[12,2,3312]{2,1,0:T(2,128)(2,1)} %bitcast.21, bf16[72,4,384]{2,1,0:T(4,128)(2,1)} %bitcast.20, bf16[384,1152]{1,0:T(8,128)(2,1)} %wqkv_in.1, bf16[384,384]{1,0:T(8,128)(2,1)} %wo_in.1, ...), custom_call_target="tpu_custom_call" | custom-call | flops 1000000000 | bytes 3000000 | tf_op jit(solution)/shard_map/first_block/pallas_call | solution.py:436
  16.1 3.5 %collective-permute-start.1 = (bf16[2,72,384]{2,1,0:T(8,128)(2,1)}, bf16[2,72,384]{2,1,0:T(8,128)(2,1)S(1)}, u32[]{:S(2)}, u32[]{:S(2)}) collective-permute-start(bf16[2,72,384]{2,1,0:T(8,128)(2,1)} %get-tuple-element.39.east_ref), channel_id=1, source_target_pairs={{0,1},{1,2},{2,3},{3,4},{4,5},{5,6},{6,7},{7,8},{8,9},{9,10},{10,1... | collective-permute-start | bytes 331784 | tf_op jit(solution)/shard_map/ppermute | solution.py:414
  19.6 1.3 %collective-permute-start.2 = (bf16[2,72,384]{2,1,0:T(8,128)(2,1)}, bf16[2,72,384]{2,1,0:T(8,128)(2,1)S(1)}, u32[]{:S(2)}, u32[]{:S(2)}) collective-permute-start(bf16[2,72,384]{2,1,0:T(8,128)(2,1)} %get-tuple-element.38.west_ref), channel_id=1, source_target_pairs={{1,0},{2,1},{3,2},{4,3},{5,4},{6,5},{7,6},{8,7},{9,8},{10,9},{11,1... | collective-permute-start | bytes 331784 | tf_op jit(solution)/shard_map/ppermute | solution.py:491
  21.0 0.1 pad_add_fusion.where_ref
  21.0 0.0 copy-start.5
  21.0 0.0 collective-permute-done.before_in
  21.0 0.0 copy-done.3
  21.1 0.0 copy-done.4
  21.1 9.9 %early_bias.1 = (s32[2,8,80,128]{3,2,1,0:T(8,128)S(1)}, s32[2,8,128,128]{3,2,1,0:T(8,128)S(1)}) custom-call(s32[3]{0:T(128)S(1)} %pad_add_fusion.where_ref, s32[144,144]{1,0:T(8,128)S(1)} %copy-done.4, bf16[12,2,3312]{2,1,0:T(2,128)(2,1)S(1)} %bitcast.18, bf16[12,2,3312]{2,1,0:T(2,128)(2,1)S(1)} %collective-permute-done.before_in), custom_call_target="tpu_custom_call" | custom-call | flops 1000000 | bytes 100000 | tf_op jit(solution)/shard_map/early_bias/pallas_call | solution.py:493
  31.0 0.0 copy-done.5
  31.0 0.0 copy-start.6
  31.0 4.7 %collective-permute-start.3 = (bf16[2,72,384]{2,1,0:T(8,128)(2,1)S(1)}, bf16[2,72,384]{2,1,0:T(8,128)(2,1)S(1)}, u32[]{:S(2)}, u32[]{:S(2)}) collective-permute-start(bf16[2,72,384]{2,1,0:T(8,128)(2,1)S(1)} %copy-done.5), channel_id=1, source_target_pairs={{0,31},{16,15},{32,63},{48,47},{64,95},{80,79},{96,127},{112,111},... | collective-permute-start | bytes 331784 | tf_op jit(solution)/shard_map/ppermute | solution.py:504
  35.7 0.7 %late_bias.1 = (s32[2,8,80,128]{3,2,1,0:T(8,128)S(1)}, s32[2,8,128,128]{3,2,1,0:T(8,128)S(1)}) custom-call(s32[3]{0:T(128)S(1)} %pad_add_fusion.where_ref, s32[144,144]{1,0:T(8,128)S(1)} %copy-done.4, bf16[12,2,3312]{2,1,0:T(2,128)(2,1)S(1)} %bitcast.19, bf16[12,2,3312]{2,1,0:T(2,128)(2,1)S(1)} %collective-permute-done.before_in, ...), custom_call_target="tpu_custom_call" | custom-call | flops 1000000000 | bytes 10000000 | tf_op jit(solution)/shard_map/late_bias/pallas_call | solution.py:505
  36.4 0.0 collective-permute-done.1.from_west_ref
  36.4 0.0 copy-start.7
  36.4 0.6 %copy-done.7 = bf16[2,72,384]{2,1,0:T(8,128)(2,1)} copy-done((bf16[2,72,384]{2,1,0:T(8,128)(2,1)}, bf16[2,72,384]{2,1,0:T(8,128)(2,1)S(1)}, u32[]{:S(2)}) %copy-start.7) | copy-done | bytes 110616
  37.0 0.0 collective-permute-done.2.from_east_ref
  37.0 0.0 copy-start.9
  37.0 0.6 %copy-done.9 = bf16[2,72,384]{2,1,0:T(8,128)(2,1)} copy-done((bf16[2,72,384]{2,1,0:T(8,128)(2,1)}, bf16[2,72,384]{2,1,0:T(8,128)(2,1)S(1)}, u32[]{:S(2)}) %copy-start.9) | copy-done | bytes 110616
  37.7 0.6 collective-permute-done.3.seam_ref
  38.3 0.0 copy-done.6
  38.3 0.0 copy-start.8
  38.3 0.9 %copy-done.8 = bf16[2,72,384]{2,1,0:T(8,128)(2,1)S(1)} copy-done((bf16[2,72,384]{2,1,0:T(8,128)(2,1)S(1)}, bf16[2,72,384]{2,1,0:T(8,128)(2,1)}, u32[]{:S(2)}) %copy-start.8) | copy-done | bytes 110616
  39.2 0.0 copy-start.10
  39.2 0.9 %copy-done.10 = bf16[2,72,384]{2,1,0:T(8,128)(2,1)S(1)} copy-done((bf16[2,72,384]{2,1,0:T(8,128)(2,1)S(1)}, bf16[2,72,384]{2,1,0:T(8,128)(2,1)}, u32[]{:S(2)}) %copy-start.10) | copy-done | bytes 110616
  40.1 0.0 copy-start
  40.1 0.0 copy-start.1
  40.1 0.0 copy-start.2
  40.1 0.6 stack_pieces.1
  40.7 4.0 %collective-permute-start.4 = (bf16[4,72,384]{2,1,0:T(8,128)(2,1)S(1)}, bf16[4,72,384]{2,1,0:T(8,128)(2,1)}, u32[]{:S(2)}, u32[]{:S(2)}) collective-permute-start(bf16[4,72,384]{2,1,0:T(8,128)(2,1)S(1)} %get-tuple-element.44.down_ref), channel_id=1, source_target_pairs={{0,32},{32,64},{64,96},{96,128},{128,160},{160,192},{192,224},{224... | collective-permute-start | bytes 663560 | tf_op jit(solution)/shard_map/ppermute | solution.py:414
  44.7 2.1 %collective-permute-start.5 = (bf16[4,72,384]{2,1,0:T(8,128)(2,1)S(1)}, bf16[4,72,384]{2,1,0:T(8,128)(2,1)}, u32[]{:S(2)}, u32[]{:S(2)}) collective-permute-start(bf16[4,72,384]{2,1,0:T(8,128)(2,1)S(1)} %get-tuple-element.43.up_ref), channel_id=1, source_target_pairs={{32,0},{64,32},{96,64},{128,96},{160,128},{192,160},{224,192},{256... | collective-permute-start | bytes 663560 | tf_op jit(solution)/shard_map/ppermute | solution.py:414
  46.8 0.1 add_convert_fusion.edge_ref
  46.9 0.7 %collective-permute-done.4.north_ref = bf16[4,72,384]{2,1,0:T(8,128)(2,1)} collective-permute-done((bf16[4,72,384]{2,1,0:T(8,128)(2,1)S(1)}, bf16[4,72,384]{2,1,0:T(8,128)(2,1)}, u32[]{:S(2)}, u32[]{:S(2)}) %collective-permute-start.4) | collective-permute-done | bytes 221216 | tf_op jit(solution)/shard_map/ppermute | solution.py:414
  47.6 5.4 %collective-permute-done.5.south_ref = bf16[4,72,384]{2,1,0:T(8,128)(2,1)} collective-permute-done((bf16[4,72,384]{2,1,0:T(8,128)(2,1)S(1)}, bf16[4,72,384]{2,1,0:T(8,128)(2,1)}, u32[]{:S(2)}, u32[]{:S(2)}) %collective-permute-start.5) | collective-permute-done | bytes 221216 | tf_op jit(solution)/shard_map/ppermute | solution.py:414
  53.0 0.0 copy-done
  53.0 0.0 copy-done.1
  53.0 0.0 copy-done.2
  53.0 7.4 %second_block.1 = bf16[72,4,384]{2,1,0:T(4,128)(2,1)} custom-call(s32[2]{0:T(128)S(1)} %add_convert_fusion.edge_ref, bf16[288,384]{1,0:T(8,128)(2,1)S(1)} %copy-done.2, bf16[4,72,384]{2,1,0:T(8,128)(2,1)S(1)} %get-tuple-element.43.up_ref, bf16[4,72,384]{2,1,0:T(8,128)(2,1)S(1)} %get-tuple-element.44.down_ref, ...), custom_call_target="tpu_custom_call" | custom-call | flops 1000000000 | bytes 5000000 | tf_op jit(solution)/shard_map/second_block/pallas_call | solution.py:533
Async XLA Ops:
  0.0 21.0 %collective-permute-start = (bf16[12,2,3312]{2,1,0:T(2,128)(2,1)}, bf16[12,2,3312]{2,1,0:T(2,128)(2,1)S(1)}, u32[]{:S(2)}, u32[]{:S(2)}) collective-permute-start(bf16[12,2,3312]{2,1,0:T(2,128)(2,1)} %bitcast.17), channel_id=1, source_target_pairs={{0,32},{32,64},{64,96},{96,128},{128,160},{160,192},{192,224},{224... | collective-permute-start | bytes 476936 | tf_op jit(solution)/shard_map/ppermute | solution.py:414
  3.6 17.5 %copy-start.3 = (bf16[1,2,12,3312]{3,1,2,0:T(2,128)(2,1)S(1)}, bf16[1,2,12,3312]{3,1,2,0:T(2,128)(2,1)}, u32[]{:S(2)}) copy-start(bf16[1,2,12,3312]{3,1,2,0:T(2,128)(2,1)} %param.19) | copy-start | bytes 476932
  3.6 17.5 %copy-start.4 = (s32[144,144]{1,0:T(8,128)S(1)}, s32[144,144]{1,0:T(8,128)}, u32[]{:S(2)}) copy-start(s32[144,144]{1,0:T(8,128)} %idx_in.5) | copy-start | bytes 248836
  16.1 20.3 %collective-permute-start.1 = (bf16[2,72,384]{2,1,0:T(8,128)(2,1)}, bf16[2,72,384]{2,1,0:T(8,128)(2,1)S(1)}, u32[]{:S(2)}, u32[]{:S(2)}) collective-permute-start(bf16[2,72,384]{2,1,0:T(8,128)(2,1)} %get-tuple-element.39.east_ref), channel_id=1, source_target_pairs={{0,1},{1,2},{2,3},{3,4},{4,5},{5,6},{6,7},{7,8},{8,9},{9,10},{10,1... | collective-permute-start | bytes 331784 | tf_op jit(solution)/shard_map/ppermute | solution.py:414
  19.6 17.4 %collective-permute-start.2 = (bf16[2,72,384]{2,1,0:T(8,128)(2,1)}, bf16[2,72,384]{2,1,0:T(8,128)(2,1)S(1)}, u32[]{:S(2)}, u32[]{:S(2)}) collective-permute-start(bf16[2,72,384]{2,1,0:T(8,128)(2,1)} %get-tuple-element.38.west_ref), channel_id=1, source_target_pairs={{1,0},{2,1},{3,2},{4,3},{5,4},{6,5},{7,6},{8,7},{9,8},{10,9},{11,1... | collective-permute-start | bytes 331784 | tf_op jit(solution)/shard_map/ppermute | solution.py:491
  21.0 9.9 %copy-start.5 = (bf16[2,72,384]{2,1,0:T(8,128)(2,1)S(1)}, bf16[2,72,384]{2,1,0:T(8,128)(2,1)}, u32[]{:S(2)}) copy-start(bf16[2,72,384]{2,1,0:T(8,128)(2,1)} %get-tuple-element.38.west_ref) | copy-start | bytes 331780
  31.0 7.3 %copy-start.6 = (bf16[2,72,384]{2,1,0:T(8,128)(2,1)S(1)}, bf16[2,72,384]{2,1,0:T(8,128)(2,1)}, u32[]{:S(2)}) copy-start(bf16[2,72,384]{2,1,0:T(8,128)(2,1)} %get-tuple-element.39.east_ref) | copy-start | bytes 331780
  31.0 7.3 %collective-permute-start.3 = (bf16[2,72,384]{2,1,0:T(8,128)(2,1)S(1)}, bf16[2,72,384]{2,1,0:T(8,128)(2,1)S(1)}, u32[]{:S(2)}, u32[]{:S(2)}) collective-permute-start(bf16[2,72,384]{2,1,0:T(8,128)(2,1)S(1)} %copy-done.5), channel_id=1, source_target_pairs={{0,31},{16,15},{32,63},{48,47},{64,95},{80,79},{96,127},{112,111},... | collective-permute-start | bytes 331784 | tf_op jit(solution)/shard_map/ppermute | solution.py:504
  36.4 0.6 %copy-start.7 = (bf16[2,72,384]{2,1,0:T(8,128)(2,1)}, bf16[2,72,384]{2,1,0:T(8,128)(2,1)S(1)}, u32[]{:S(2)}) copy-start(bf16[2,72,384]{2,1,0:T(8,128)(2,1)S(1)} %collective-permute-done.1.from_west_ref) | copy-start | bytes 331780
  37.0 0.6 %copy-start.9 = (bf16[2,72,384]{2,1,0:T(8,128)(2,1)}, bf16[2,72,384]{2,1,0:T(8,128)(2,1)S(1)}, u32[]{:S(2)}) copy-start(bf16[2,72,384]{2,1,0:T(8,128)(2,1)S(1)} %collective-permute-done.2.from_east_ref) | copy-start | bytes 331780
  38.3 0.9 %copy-start.8 = (bf16[2,72,384]{2,1,0:T(8,128)(2,1)S(1)}, bf16[2,72,384]{2,1,0:T(8,128)(2,1)}, u32[]{:S(2)}) copy-start(bf16[2,72,384]{2,1,0:T(8,128)(2,1)} %copy-done.7) | copy-start | bytes 331780
  39.2 0.9 %copy-start.10 = (bf16[2,72,384]{2,1,0:T(8,128)(2,1)S(1)}, bf16[2,72,384]{2,1,0:T(8,128)(2,1)}, u32[]{:S(2)}) copy-start(bf16[2,72,384]{2,1,0:T(8,128)(2,1)} %copy-done.9) | copy-start | bytes 331780
  40.1 12.9 %copy-start = (bf16[384,1152]{1,0:T(8,128)(2,1)S(1)}, bf16[384,1152]{1,0:T(8,128)(2,1)}, u32[]{:S(2)}) copy-start(bf16[384,1152]{1,0:T(8,128)(2,1)} %wqkv_ref.1) | copy-start | bytes 2654212
  40.1 12.9 %copy-start.1 = (bf16[384,384]{1,0:T(8,128)(2,1)S(1)}, bf16[384,384]{1,0:T(8,128)(2,1)}, u32[]{:S(2)}) copy-start(bf16[384,384]{1,0:T(8,128)(2,1)} %wo_ref.1) | copy-start | bytes 884740
  40.1 12.9 %copy-start.2 = (bf16[288,384]{1,0:T(8,128)(2,1)S(1)}, bf16[288,384]{1,0:T(8,128)(2,1)}, u32[]{:S(2)}) copy-start(bf16[288,384]{1,0:T(8,128)(2,1)} %get-tuple-element.26.first_ref) | copy-start | bytes 663556
  40.7 6.9 %collective-permute-start.4 = (bf16[4,72,384]{2,1,0:T(8,128)(2,1)S(1)}, bf16[4,72,384]{2,1,0:T(8,128)(2,1)}, u32[]{:S(2)}, u32[]{:S(2)}) collective-permute-start(bf16[4,72,384]{2,1,0:T(8,128)(2,1)S(1)} %get-tuple-element.44.down_ref), channel_id=1, source_target_pairs={{0,32},{32,64},{64,96},{96,128},{128,160},{160,192},{192,224},{224... | collective-permute-start | bytes 663560 | tf_op jit(solution)/shard_map/ppermute | solution.py:414
  44.7 8.3 %collective-permute-start.5 = (bf16[4,72,384]{2,1,0:T(8,128)(2,1)S(1)}, bf16[4,72,384]{2,1,0:T(8,128)(2,1)}, u32[]{:S(2)}, u32[]{:S(2)}) collective-permute-start(bf16[4,72,384]{2,1,0:T(8,128)(2,1)S(1)} %get-tuple-element.43.up_ref), channel_id=1, source_target_pairs={{32,0},{64,32},{96,64},{128,96},{160,128},{192,160},{224,192},{256... | collective-permute-start | bytes 663560 | tf_op jit(solution)/shard_map/ppermute | solution.py:414

commit v5 on v4

--- a/solution.py
+++ b/solution.py
@@ -42,9 +42,9 @@
 
 
 def keys_from_pieces():
-    i = row_ids(288)
-    w, piece, t = i // 144, i // 36 % 4, i % 36
-    return one_hot(80 * piece + 36 * w + t, 320)
+    i = row_ids(WIN)
+    w, piece, t = i // 72, i // 36 % 2, i % 36
+    return one_hot(80 * piece + 36 * w + t, 160)
 
 
 def queries_from_quadrants():
@@ -313,8 +313,15 @@
 
 
 def late_kernel(
-    where_ref, idx_in, table_in, before_in, main_in, tail_in, main_ref, tail_ref, *scratch
+    where_ref, idx_in, table_in, before_in, main_in, tail_in, *refs
 ):
+    kept, (main_ref, tail_ref), staged, scratch, sems = refs[:5], refs[5:7], refs[7:12], refs[12:-1], refs[-1]
+    copies = [
+        pltpu.make_async_copy(src, dst, sems.at[i]) for i, (src, dst) in enumerate(zip(kept, staged))
+    ]
+    for copy in copies:
+        copy.start()
+
     @pl.when(where_ref[1] == 0)
     def _():
         fill_bias(where_ref, idx_in, table_in, before_in, main_ref, tail_ref, *scratch)
@@ -323,6 +330,9 @@
     def _():
         main_ref[...] = main_in[...]
         tail_ref[...] = tail_in[...]
+
+    for copy in copies:
+        copy.wait()
 
 
 def stack_kernel(where_ref, west_ref, east_ref, from_west_ref, from_east_ref, seam_ref, up_ref, down_ref):
@@ -333,35 +343,51 @@
         dst[3] = jnp.where(where_ref[2] == 1, seam_ref[a], from_east_ref[a])
 
 
+def half_window(cat, order, pieces):
+    cat[72:80, :] = jnp.zeros((8, D), F32)
+    cat[152:160, :] = jnp.zeros((8, D), F32)
+    for i, piece in enumerate(pieces):
+        cat[80 * i : 80 * i + 72, :] = piece.astype(F32)
+    return dot(order, cat[...].astype(BF16)).astype(BF16)
+
+
+def near_kernel(up_ref, down_ref, wqkv_ref, query_ref, near_ref, cat, window):
+    here = (up_ref, down_ref)
+    tokens = jnp.concatenate([up_ref[1], down_ref[1], up_ref[2], down_ref[2]], axis=0)
+    asked = dot(queries_from_quadrants(), tokens).astype(BF16)
+    query_ref[...] = dot(asked, wqkv_ref[:, 0:D]).astype(BF16).astype(F32)
+    order = keys_from_pieces()
+    for a in range(2):
+        for b in range(2):
+            q = 2 * a + b
+            window[WIN * q : WIN * q + WIN, :] = half_window(
+                cat.at[q], order, (here[a][1 + b], here[a][3 * b])
+            )
+    near_ref[...] = dot(window[...], wqkv_ref[:, D:]).astype(BF16).astype(F32)
+
+
 def second_kernel(
     edge_ref,
-    first_ref, up_ref, down_ref, north_ref, south_ref,
+    first_ref, query_ref, near_ref, north_ref, south_ref,
     wqkv_ref, wo_ref, main_ref, tail_ref,
     out_ref,
-    cat, window, qbuf, kpad, vpad, obuf,
+    cat, window, result, kpad, vpad, obuf,
 ):
-    here = (up_ref, down_ref)
     beyond = (north_ref, south_ref)
-    tokens = jnp.concatenate([up_ref[1], down_ref[1], up_ref[2], down_ref[2]], axis=0)
-    asked = dot(queries_from_quadrants(), tokens).astype(BF16)
-    qbuf[...] = dot(asked, wqkv_ref[:, 0:D]).astype(BF16).astype(F32)
-
     order = keys_from_pieces()
-    for piece in range(4):
-        cat[80 * piece + 72 : 80 * piece + 80, :] = jnp.zeros((8, D), F32)
     for a in range(2):
         for b in range(2):
             q = 2 * a + b
             far = ((1, 0), (2, 3))[b]
-            cat[0:72, :] = here[a][1 + b].astype(F32)
-            cat[80:152, :] = here[a][3 * b].astype(F32)
-            cat[160:232, :] = beyond[a][far[0]].astype(F32)
-            cat[240:312, :] = beyond[a][far[1]].astype(F32)
-            window[288 * q : 288 * q + 288, :] = dot(order, cat[...].astype(BF16)).astype(BF16)
-    for dst, start in ((kpad, D), (vpad, 2 * D)):
-        made = dot(window[...], wqkv_ref[:, start : start + D]).astype(BF16)
+            window[WIN * q : WIN * q + WIN, :] = half_window(
+                cat.at[q], order, (beyond[a][far[0]], beyond[a][far[1]])
+            )
+    for dst, start in ((kpad, 0), (vpad, D)):
+        made = dot(window[...], wqkv_ref[:, D + start : 2 * D + start]).astype(BF16).astype(F32)
         for j in range(8):
-            dst[j, 0:WIN, :] = made[WIN * j : WIN * j + WIN]
+            rows = slice(72 * j, 72 * j + 72)
+            both = jnp.concatenate([near_ref[rows, start : start + D], made[rows]], axis=0)
+            dst[j, 0:WIN, :] = both.astype(BF16)
             dst[j, WIN:, :] = jnp.zeros((256 - WIN, D), BF16)
 
     shape = (40, 256)
@@ -391,13 +417,13 @@
                         for i in range(4)
                     ]
                     obuf[40 * at : 40 * at + 40, lanes] = four_heads(
-                        qbuf[40 * at : 40 * at + 40, lanes], kpad[at, :, lanes], vpad[at, :, lanes],
+                        query_ref[40 * at : 40 * at + 40, lanes], kpad[at, :, lanes], vpad[at, :, lanes],
                         biases, masks[w],
                     )
     attended = dot(given_from_queries(), obuf[...].astype(BF16)).astype(BF16)
-    qbuf[0:288, :] = dot(given_from_natural(), first_ref[...]) + dot(attended, wo_ref[...])
+    result[...] = dot(given_from_natural(), first_ref[...]) + dot(attended, wo_ref[...])
     for g in range(72):
-        out_ref[g] = qbuf[4 * g : 4 * g + 4, :].astype(BF16)
+        out_ref[g] = result[4 * g : 4 * g + 4, :].astype(BF16)
 
 
 VMEM = pl.BlockSpec(memory_space=pltpu.VMEM)
@@ -502,19 +528,20 @@
     )(where, position_index, table, before)
     main, tail, west = lax.optimization_barrier((main, tail, west))
     from_seam = lax.ppermute(west, "lon", seam)
-    main, tail = pl.pallas_call(
+    staged = (west, east, first, qkv_second, proj_second)
+    main, tail, west, east, first, w_qkv, w_proj = pl.pallas_call(
         late_kernel,
-        out_shape=bias_shapes,
-        in_specs=[SMEM, HBM, HBM, ANY, VMEM, VMEM],
-        out_specs=(VMEM, VMEM),
-        scratch_shapes=bias_scratch,
+        out_shape=bias_shapes + tuple(jax.ShapeDtypeStruct(x.shape, x.dtype) for x in staged),
+        in_specs=[SMEM, HBM, HBM, ANY, VMEM, VMEM] + [ANY] * 5,
+        out_specs=(VMEM,) * 7,
+        scratch_shapes=bias_scratch + [pltpu.SemaphoreType.DMA((5,))],
         compiler_params=params,
         cost_estimate=cost(10**9, 10**7),
         name="late_bias",
-    )(where, position_index, table, before, main, tail)
-
-    west, east, from_west, from_east, from_seam, main, tail = lax.optimization_barrier(
-        (west, east, from_west, from_east, from_seam, main, tail)
+    )(where, position_index, table, before, main, tail, *staged)
+
+    west, east, from_west, from_east, from_seam = lax.optimization_barrier(
+        (west, east, from_west, from_east, from_seam)
     )
     pieces = jax.ShapeDtypeStruct((4, 72, D), BF16)
     up, down = pl.pallas_call(
@@ -529,6 +556,17 @@
     south = shift(up, "lat", -1, False)
     north = shift(down, "lat", 1, False)
 
+    query, near = pl.pallas_call(
+        near_kernel,
+        out_shape=(jax.ShapeDtypeStruct((320, D), F32), jax.ShapeDtypeStruct((576, 2 * D), F32)),
+        in_specs=[VMEM] * 3,
+        out_specs=(VMEM, VMEM),
+        scratch_shapes=[pltpu.VMEM((4, 160, D), F32), pltpu.VMEM((576, D), BF16)],
+        compiler_params=params,
+        cost_estimate=cost(10**9, 10**7),
+        name="near_half",
+    )(up, down, w_qkv)
+
     edges = jnp.stack([lat > 0, lat < last]).astype(I32)
     out = pl.pallas_call(
         second_kernel,
@@ -536,9 +574,9 @@
         in_specs=[SMEM] + [VMEM] * 9,
         out_specs=VMEM,
         scratch_shapes=[
-            pltpu.VMEM((320, D), F32),
-            pltpu.VMEM((1152, D), BF16),
-            pltpu.VMEM((320, D), F32),
+            pltpu.VMEM((4, 160, D), F32),
+            pltpu.VMEM((576, D), BF16),
+            pltpu.VMEM((288, D), F32),
             pltpu.VMEM((8, 256, D), BF16),
             pltpu.VMEM((8, 256, D), BF16),
             pltpu.VMEM((320, D), F32),
@@ -546,9 +584,7 @@
         compiler_params=params,
         cost_estimate=cost(10**9, 5 * 10**6),
         name="second_block",
-    )(
-        edges, first, up, down, north, south, qkv_second, proj_second, main, tail,
-    )
+    )(edges, first, query, near, north, south, w_qkv, w_proj, main, tail)
     return out.reshape(6, 12, 4, D).transpose(2, 0, 1, 3)
 
 

time: 60.7 us -> 61.9 us (1.020)
  the two profiles are of different devices: /device:TPU:9 before, /device:TPU:11 now
where the time goes in v5:
time: 61.9 us; the launch traced here: 61.5 us
  Pallas kernels  33.6 us (54%)
  starting transfers between devices  18.8 us (30%)
  local copies, waits for them, and re-layouts  5.13 us (8%)
  waiting for transfers between devices  3.56 us (6%)
    ppermute x4, starting transfers between devices, shift(): return lax.ppermute(block, axis, route)  12.7 us
    pallas_call x1, Pallas kernels, shards(): pl.pallas_call(first_kernel, out_shape=(jax.ShapeDtypeStruct((288, D), BF...  12.5 us
    pallas_call x1, Pallas kernels, shards(): pl.pallas_call(early_kernel, out_shape=bias_shapes, in_specs=[SMEM, HBM,...  9.92 us
    pallas_call x1, Pallas kernels, shards(): pl.pallas_call(second_kernel, out_shape=jax.ShapeDtypeStruct((72, 4, D),...  5.61 us
    unnamed x28, local copies, waits for them, and re-layouts  5.13 us
    ppermute x1, starting transfers between devices, shards(): from_seam = lax.ppermute(west, 'lon', seam)  4.85 us
    ppermute x4, waiting for transfers between devices, shift(): return lax.ppermute(block, axis, route)  3.56 us
    pallas_call x1, Pallas kernels, shards(): pl.pallas_call(near_kernel, out_shape=(jax.ShapeDtypeStruct((320, D), F32...  2.39 us
  transfers between devices with their start and end apart: 6, of which 1 were waited for; matrix products, arithmetic and copies ran while one was open for 0% of the time, Pallas kernels for 43%

profile of v5, /device:TPU:11, one launch (start us, length us, event | category | flops | bytes accessed | tf_op | source)
XLA Modules:
  0.0 61.5 jit_solution(14475535235781972437)
XLA Ops:
  0.0 3.6 %collective-permute-start = (bf16[12,2,3312]{2,1,0:T(2,128)(2,1)}, bf16[12,2,3312]{2,1,0:T(2,128)(2,1)S(1)}, u32[]{:S(2)}, u32[]{:S(2)}) collective-permute-start(bf16[12,2,3312]{2,1,0:T(2,128)(2,1)} %bitcast.17), channel_id=1, source_target_pairs={{0,32},{32,64},{64,96},{96,128},{128,160},{160,192},{192,224},{224... | collective-permute-start | bytes 476936 | tf_op jit(solution)/shard_map/ppermute | solution.py:440
  3.6 0.0 copy-start.7
  3.6 0.0 copy-start.11
  3.6 12.5 %first_block.1 = (bf16[288,384]{1,0:T(8,128)(2,1)}, bf16[2,72,384]{2,1,0:T(8,128)(2,1)}, bf16[2,72,384]{2,1,0:T(8,128)(2,1)}) custom-call(s32[144,144]{1,0:T(8,128)} %idx_in.5, bf16[12,2,3312]{2,1,0:T(2,128)(2,1)} %bitcast.21, bf16[72,4,384]{2,1,0:T(4,128)(2,1)} %bitcast.20, bf16[384,1152]{1,0:T(8,128)(2,1)} %wqkv_in.1, bf16[384,384]{1,0:T(8,128)(2,1)} %wo_in.1, ...), custom_call_target="tpu_custom_call" | custom-call | flops 1000000000 | bytes 3000000 | tf_op jit(solution)/shard_map/first_block/pallas_call | solution.py:462
  16.1 0.0 copy-start
  16.1 3.7 %collective-permute-start.1 = (bf16[2,72,384]{2,1,0:T(8,128)(2,1)}, bf16[2,72,384]{2,1,0:T(8,128)(2,1)}, u32[]{:S(2)}, u32[]{:S(2)}) collective-permute-start(bf16[2,72,384]{2,1,0:T(8,128)(2,1)} %get-tuple-element.39.refs_1_), channel_id=1, source_target_pairs={{0,1},{1,2},{2,3},{3,4},{4,5},{5,6},{6,7},{7,8},{8,9},{9,10},{10,1... | collective-permute-start | bytes 331784 | tf_op jit(solution)/shard_map/ppermute | solution.py:440
  19.8 1.3 %collective-permute-start.2 = (bf16[2,72,384]{2,1,0:T(8,128)(2,1)}, bf16[2,72,384]{2,1,0:T(8,128)(2,1)}, u32[]{:S(2)}, u32[]{:S(2)}) collective-permute-start(bf16[2,72,384]{2,1,0:T(8,128)(2,1)} %get-tuple-element.38.refs_0_), channel_id=1, source_target_pairs={{1,0},{2,1},{3,2},{4,3},{5,4},{6,5},{7,6},{8,7},{9,8},{10,9},{11,1... | collective-permute-start | bytes 331784 | tf_op jit(solution)/shard_map/ppermute | solution.py:517
  21.1 0.0 copy-start.4
  21.1 0.0 copy-start.13
  21.1 0.1 pad_add_fusion.where_ref
  21.2 0.0 collective-permute-done.before_in
  21.2 0.0 copy-done.7
  21.2 0.0 copy-done.11
  21.2 0.0 copy-start.9
  21.2 9.9 %early_bias.1 = (s32[2,8,80,128]{3,2,1,0:T(8,128)S(1)}, s32[2,8,128,128]{3,2,1,0:T(8,128)S(1)}) custom-call(s32[3]{0:T(128)S(1)} %pad_add_fusion.where_ref, s32[144,144]{1,0:T(8,128)S(1)} %copy-done.11, bf16[12,2,3312]{2,1,0:T(2,128)(2,1)S(1)} %bitcast.18, bf16[12,2,3312]{2,1,0:T(2,128)(2,1)S(1)} %collective-permute-done.before_in), custom_call_target="tpu_custom_call" | custom-call | flops 1000000 | bytes 100000 | tf_op jit(solution)/shard_map/early_bias/pallas_call | solution.py:519
  31.2 4.9 %collective-permute-start.3 = (bf16[2,72,384]{2,1,0:T(8,128)(2,1)}, bf16[2,72,384]{2,1,0:T(8,128)(2,1)S(1)}, u32[]{:S(2)}, u32[]{:S(2)}) collective-permute-start(bf16[2,72,384]{2,1,0:T(8,128)(2,1)} %get-tuple-element.38.refs_0_), channel_id=1, source_target_pairs={{0,31},{16,15},{32,63},{48,47},{64,95},{80,79},{96,127},{112,111},... | collective-permute-start | bytes 331784 | tf_op jit(solution)/shard_map/ppermute | solution.py:530
  36.0 0.0 copy-done.9
  36.0 0.0 copy-done
  36.0 0.0 copy-done.4
  36.1 0.0 copy-done.13
  36.1 0.0 copy-start.3
  36.1 1.0 %copy-done.3 = bf16[384,384]{1,0:T(8,128)(2,1)S(1)} copy-done((bf16[384,384]{1,0:T(8,128)(2,1)S(1)}, bf16[384,384]{1,0:T(8,128)(2,1)}, u32[]{:S(2)}) %copy-start.3) | copy-done | bytes 294936
  37.0 0.0 copy-start.8
  37.0 0.9 %copy-done.8 = bf16[1,2,12,3312]{3,1,2,0:T(2,128)(2,1)S(1)} copy-done((bf16[1,2,12,3312]{3,1,2,0:T(2,128)(2,1)S(1)}, bf16[1,2,12,3312]{3,1,2,0:T(2,128)(2,1)}, u32[]{:S(2)}) %copy-start.8) | copy-done | bytes 159000
  38.0 0.0 copy-start.10
  38.0 0.9 %copy-done.10 = bf16[12,2,3312]{2,1,0:T(2,128)(2,1)S(1)} copy-done((bf16[12,2,3312]{2,1,0:T(2,128)(2,1)S(1)}, bf16[12,2,3312]{2,1,0:T(2,128)(2,1)}, u32[]{:S(2)}) %copy-start.10) | copy-done | bytes 159000
  38.9 0.0 copy-start.12
  38.9 0.9 %copy-done.12 = s32[144,144]{1,0:T(8,128)S(1)} copy-done((s32[144,144]{1,0:T(8,128)S(1)}, s32[144,144]{1,0:T(8,128)}, u32[]{:S(2)}) %copy-start.12) | copy-done | bytes 82968
  39.8 1.5 %late_bias.1 = (s32[2,8,80,128]{3,2,1,0:T(8,128)S(1)}, s32[2,8,128,128]{3,2,1,0:T(8,128)S(1)}, bf16[2,72,384]{2,1,0:T(8,128)(2,1)S(1)}, bf16[2,72,384]{2,1,0:T(8...) custom-call(s32[3]{0:T(128)S(1)} %pad_add_fusion.where_ref, ...), custom_call_target="tpu_custom_call" | custom-call | flops 1000000000 | bytes 10000000 | tf_op jit(solution)/shard_map/late_bias/pallas_call | solution.py:532
  41.3 0.0 copy-start.1
  41.3 0.7 %copy-done.1 = bf16[384,384]{1,0:T(8,128)(2,1)} copy-done((bf16[384,384]{1,0:T(8,128)(2,1)}, bf16[384,384]{1,0:T(8,128)(2,1)S(1)}, u32[]{:S(2)}) %copy-start.1) | copy-done | bytes 294936
  42.0 0.0 copy-start.5
  42.0 0.7 %copy-done.5 = bf16[288,384]{1,0:T(8,128)(2,1)} copy-done((bf16[288,384]{1,0:T(8,128)(2,1)}, bf16[288,384]{1,0:T(8,128)(2,1)S(1)}, u32[]{:S(2)}) %copy-start.5) | copy-done | bytes 221208
  42.7 0.0 collective-permute-done.1.from_west_ref
  42.7 0.0 collective-permute-done.2.from_east_ref
  42.7 0.0 collective-permute-done.3.seam_ref
  42.7 1.7 %stack_pieces.1 = (bf16[4,72,384]{2,1,0:T(8,128)(2,1)S(1)}, bf16[4,72,384]{2,1,0:T(8,128)(2,1)}) custom-call(s32[3]{0:T(128)S(1)} %pad_add_fusion.where_ref, bf16[2,72,384]{2,1,0:T(8,128)(2,1)S(1)} %get-tuple-element.44.west_ref, bf16[2,72,384]{2,1,0:T(8,128)(2,1)S(1)} %get-tuple-element.45.east_ref, ...), custom_call_target="tpu_custom_call" | custom-call | flops 100000 | bytes 1000000 | tf_op jit(solution)/shard_map/stack_pieces/pallas_call | solution.py:547
  44.4 3.4 %collective-permute-start.4 = (bf16[4,72,384]{2,1,0:T(8,128)(2,1)}, bf16[4,72,384]{2,1,0:T(8,128)(2,1)S(1)}, u32[]{:S(2)}, u32[]{:S(2)}) collective-permute-start(bf16[4,72,384]{2,1,0:T(8,128)(2,1)} %get-tuple-element.50.down_ref), channel_id=1, source_target_pairs={{0,32},{32,64},{64,96},{96,128},{128,160},{160,192},{192,224},{224... | collective-permute-start | bytes 663560 | tf_op jit(solution)/shard_map/ppermute | solution.py:440
  47.8 2.1 %collective-permute-start.5 = (bf16[4,72,384]{2,1,0:T(8,128)(2,1)S(1)}, bf16[4,72,384]{2,1,0:T(8,128)(2,1)S(1)}, u32[]{:S(2)}, u32[]{:S(2)}) collective-permute-start(bf16[4,72,384]{2,1,0:T(8,128)(2,1)S(1)} %get-tuple-element.49.up_ref), channel_id=1, source_target_pairs={{32,0},{64,32},{96,64},{128,96},{160,128},{192,160},{224,192},{256... | collective-permute-start | bytes 663560 | tf_op jit(solution)/shard_map/ppermute | solution.py:440
  49.9 0.1 add_convert_fusion.edge_ref
  49.9 0.0 copy-start.2
  49.9 0.0 copy-start.6
  49.9 2.4 %near_half.1 = (f32[320,384]{1,0:T(8,128)S(1)}, f32[576,768]{1,0:T(8,128)S(1)}) custom-call(bf16[4,72,384]{2,1,0:T(8,128)(2,1)S(1)} %get-tuple-element.49.up_ref, bf16[4,72,384]{2,1,0:T(8,128)(2,1)} %get-tuple-element.50.down_ref, bf16[384,1152]{1,0:T(8,128)(2,1)S(1)} %get-tuple-element.51.wqkv_ref), custom_call_target="tpu_custom_call" | custom-call | flops 1000000000 | bytes 10000000 | tf_op jit(solution)/shard_map/near_half/pallas_call | solution.py:559
  52.3 0.0 collective-permute-done.4.north_ref
  52.4 3.5 %collective-permute-done.5.south_ref = bf16[4,72,384]{2,1,0:T(8,128)(2,1)S(1)} collective-permute-done((bf16[4,72,384]{2,1,0:T(8,128)(2,1)S(1)}, bf16[4,72,384]{2,1,0:T(8,128)(2,1)S(1)}, u32[]{:S(2)}, u32[]{:S(2)}) %collective-permute-start.5) | collective-permute-done | bytes 221216 | tf_op jit(solution)/shard_map/ppermute | solution.py:440
  55.9 0.0 copy-done.2
  55.9 0.0 copy-done.6
  55.9 5.6 %second_block.1 = bf16[72,4,384]{2,1,0:T(4,128)(2,1)} custom-call(s32[2]{0:T(128)S(1)} %add_convert_fusion.edge_ref, bf16[288,384]{1,0:T(8,128)(2,1)S(1)} %copy-done.6, f32[320,384]{1,0:T(8,128)S(1)} %get-tuple-element.52.query_ref, f32[576,768]{1,0:T(8,128)S(1)} %get-tuple-element.53.near_ref, bf16[4,72,384]{2,1,0:T(8,128)(2,1)S(1)} %collective-permute-done.4.north_ref, ...), custom_call_target="tpu_custom_call" | custom-call | flops 1000000000 | bytes 5000000 | tf_op jit(solution)/shard_map/second_block/pallas_call | solution.py:571
Async XLA Ops:
  0.0 21.2 %collective-permute-start = (bf16[12,2,3312]{2,1,0:T(2,128)(2,1)}, bf16[12,2,3312]{2,1,0:T(2,128)(2,1)S(1)}, u32[]{:S(2)}, u32[]{:S(2)}) collective-permute-start(bf16[12,2,3312]{2,1,0:T(2,128)(2,1)} %bitcast.17), channel_id=1, source_target_pairs={{0,32},{32,64},{64,96},{96,128},{128,160},{160,192},{192,224},{224... | collective-permute-start | bytes 476936 | tf_op jit(solution)/shard_map/ppermute | solution.py:440
  3.6 17.7 %copy-start.7 = (bf16[1,2,12,3312]{3,1,2,0:T(2,128)(2,1)S(1)}, bf16[1,2,12,3312]{3,1,2,0:T(2,128)(2,1)}, u32[]{:S(2)}) copy-start(bf16[1,2,12,3312]{3,1,2,0:T(2,128)(2,1)} %param.19) | copy-start | bytes 476932
  3.6 17.7 %copy-start.11 = (s32[144,144]{1,0:T(8,128)S(1)}, s32[144,144]{1,0:T(8,128)}, u32[]{:S(2)}) copy-start(s32[144,144]{1,0:T(8,128)} %idx_in.5) | copy-start | bytes 248836
  16.1 19.9 %copy-start = (bf16[384,1152]{1,0:T(8,128)(2,1)S(1)}, bf16[384,1152]{1,0:T(8,128)(2,1)}, u32[]{:S(2)}) copy-start(bf16[384,1152]{1,0:T(8,128)(2,1)} %refs_3_.1) | copy-start | bytes 2654212
  16.1 26.6 %collective-permute-start.1 = (bf16[2,72,384]{2,1,0:T(8,128)(2,1)}, bf16[2,72,384]{2,1,0:T(8,128)(2,1)}, u32[]{:S(2)}, u32[]{:S(2)}) collective-permute-start(bf16[2,72,384]{2,1,0:T(8,128)(2,1)} %get-tuple-element.39.refs_1_), channel_id=1, source_target_pairs={{0,1},{1,2},{2,3},{3,4},{4,5},{5,6},{6,7},{7,8},{8,9},{9,10},{10,1... | collective-permute-start | bytes 331784 | tf_op jit(solution)/shard_map/ppermute | solution.py:440
  19.8 22.9 %collective-permute-start.2 = (bf16[2,72,384]{2,1,0:T(8,128)(2,1)}, bf16[2,72,384]{2,1,0:T(8,128)(2,1)}, u32[]{:S(2)}, u32[]{:S(2)}) collective-permute-start(bf16[2,72,384]{2,1,0:T(8,128)(2,1)} %get-tuple-element.38.refs_0_), channel_id=1, source_target_pairs={{1,0},{2,1},{3,2},{4,3},{5,4},{6,5},{7,6},{8,7},{9,8},{10,9},{11,1... | collective-permute-start | bytes 331784 | tf_op jit(solution)/shard_map/ppermute | solution.py:517
  21.1 14.9 %copy-start.4 = (bf16[288,384]{1,0:T(8,128)(2,1)S(1)}, bf16[288,384]{1,0:T(8,128)(2,1)}, u32[]{:S(2)}) copy-start(bf16[288,384]{1,0:T(8,128)(2,1)} %get-tuple-element.40.refs_2_) | copy-start | bytes 663556
  21.1 14.9 %copy-start.13 = (bf16[2,72,384]{2,1,0:T(8,128)(2,1)S(1)}, bf16[2,72,384]{2,1,0:T(8,128)(2,1)}, u32[]{:S(2)}) copy-start(bf16[2,72,384]{2,1,0:T(8,128)(2,1)} %get-tuple-element.39.refs_1_) | copy-start | bytes 331780
  21.2 14.8 %copy-start.9 = (bf16[12,2,3312]{2,1,0:T(2,128)(2,1)}, bf16[12,2,3312]{2,1,0:T(2,128)(2,1)S(1)}, u32[]{:S(2)}) copy-start(bf16[12,2,3312]{2,1,0:T(2,128)(2,1)S(1)} %collective-permute-done.before_in) | copy-start | bytes 476932
  31.2 11.5 %collective-permute-start.3 = (bf16[2,72,384]{2,1,0:T(8,128)(2,1)}, bf16[2,72,384]{2,1,0:T(8,128)(2,1)S(1)}, u32[]{:S(2)}, u32[]{:S(2)}) collective-permute-start(bf16[2,72,384]{2,1,0:T(8,128)(2,1)} %get-tuple-element.38.refs_0_), channel_id=1, source_target_pairs={{0,31},{16,15},{32,63},{48,47},{64,95},{80,79},{96,127},{112,111},... | collective-permute-start | bytes 331784 | tf_op jit(solution)/shard_map/ppermute | solution.py:530
  36.1 1.0 %copy-start.3 = (bf16[384,384]{1,0:T(8,128)(2,1)S(1)}, bf16[384,384]{1,0:T(8,128)(2,1)}, u32[]{:S(2)}) copy-start(bf16[384,384]{1,0:T(8,128)(2,1)} %refs_4_.1) | copy-start | bytes 884740
  37.0 0.9 %copy-start.8 = (bf16[1,2,12,3312]{3,1,2,0:T(2,128)(2,1)S(1)}, bf16[1,2,12,3312]{3,1,2,0:T(2,128)(2,1)}, u32[]{:S(2)}) copy-start(bf16[1,2,12,3312]{3,1,2,0:T(2,128)(2,1)} %param.19) | copy-start | bytes 476932
  38.0 0.9 %copy-start.10 = (bf16[12,2,3312]{2,1,0:T(2,128)(2,1)S(1)}, bf16[12,2,3312]{2,1,0:T(2,128)(2,1)}, u32[]{:S(2)}) copy-start(bf16[12,2,3312]{2,1,0:T(2,128)(2,1)} %copy-done.9) | copy-start | bytes 476932
  38.9 0.9 %copy-start.12 = (s32[144,144]{1,0:T(8,128)S(1)}, s32[144,144]{1,0:T(8,128)}, u32[]{:S(2)}) copy-start(s32[144,144]{1,0:T(8,128)} %idx_in.5) | copy-start | bytes 248836
  41.3 0.7 %copy-start.1 = (bf16[384,384]{1,0:T(8,128)(2,1)}, bf16[384,384]{1,0:T(8,128)(2,1)S(1)}, u32[]{:S(2)}) copy-start(bf16[384,384]{1,0:T(8,128)(2,1)S(1)} %get-tuple-element.54.wo_ref) | copy-start | bytes 884740
  42.0 0.7 %copy-start.5 = (bf16[288,384]{1,0:T(8,128)(2,1)}, bf16[288,384]{1,0:T(8,128)(2,1)S(1)}, u32[]{:S(2)}) copy-start(bf16[288,384]{1,0:T(8,128)(2,1)S(1)} %get-tuple-element.41.first_ref) | copy-start | bytes 663556
  44.4 8.0 %collective-permute-start.4 = (bf16[4,72,384]{2,1,0:T(8,128)(2,1)}, bf16[4,72,384]{2,1,0:T(8,128)(2,1)S(1)}, u32[]{:S(2)}, u32[]{:S(2)}) collective-permute-start(bf16[4,72,384]{2,1,0:T(8,128)(2,1)} %get-tuple-element.50.down_ref), channel_id=1, source_target_pairs={{0,32},{32,64},{64,96},{96,128},{128,160},{160,192},{192,224},{224... | collective-permute-start | bytes 663560 | tf_op jit(solution)/shard_map/ppermute | solution.py:440
  47.8 8.2 %collective-permute-start.5 = (bf16[4,72,384]{2,1,0:T(8,128)(2,1)S(1)}, bf16[4,72,384]{2,1,0:T(8,128)(2,1)S(1)}, u32[]{:S(2)}, u32[]{:S(2)}) collective-permute-start(bf16[4,72,384]{2,1,0:T(8,128)(2,1)S(1)} %get-tuple-element.49.up_ref), channel_id=1, source_target_pairs={{32,0},{64,32},{96,64},{128,96},{160,128},{192,160},{224,192},{256... | collective-permute-start | bytes 663560 | tf_op jit(solution)/shard_map/ppermute | solution.py:440
  49.9 6.0 %copy-start.2 = (bf16[384,384]{1,0:T(8,128)(2,1)S(1)}, bf16[384,384]{1,0:T(8,128)(2,1)}, u32[]{:S(2)}) copy-start(bf16[384,384]{1,0:T(8,128)(2,1)} %copy-done.1) | copy-start | bytes 884740
  49.9 6.0 %copy-start.6 = (bf16[288,384]{1,0:T(8,128)(2,1)S(1)}, bf16[288,384]{1,0:T(8,128)(2,1)}, u32[]{:S(2)}) copy-start(bf16[288,384]{1,0:T(8,128)(2,1)} %copy-done.5) | copy-start | bytes 663556

commit v6 on v5

--- a/solution.py
+++ b/solution.py
@@ -313,15 +313,8 @@
 
 
 def late_kernel(
-    where_ref, idx_in, table_in, before_in, main_in, tail_in, *refs
+    where_ref, idx_in, table_in, before_in, main_in, tail_in, main_ref, tail_ref, *scratch
 ):
-    kept, (main_ref, tail_ref), staged, scratch, sems = refs[:5], refs[5:7], refs[7:12], refs[12:-1], refs[-1]
-    copies = [
-        pltpu.make_async_copy(src, dst, sems.at[i]) for i, (src, dst) in enumerate(zip(kept, staged))
-    ]
-    for copy in copies:
-        copy.start()
-
     @pl.when(where_ref[1] == 0)
     def _():
         fill_bias(where_ref, idx_in, table_in, before_in, main_ref, tail_ref, *scratch)
@@ -331,11 +324,10 @@
         main_ref[...] = main_in[...]
         tail_ref[...] = tail_in[...]
 
-    for copy in copies:
-        copy.wait()
-
-
-def stack_kernel(where_ref, west_ref, east_ref, from_west_ref, from_east_ref, seam_ref, up_ref, down_ref):
+
+def stack_kernel(
+    where_ref, west_ref, east_ref, from_west_ref, from_east_ref, seam_ref, after_ref, up_ref, down_ref
+):
     for a, dst in enumerate((up_ref, down_ref)):
         dst[0] = from_west_ref[a]
         dst[1] = west_ref[a]
@@ -430,7 +422,7 @@
 SMEM = pl.BlockSpec(memory_space=pltpu.SMEM)
 HBM = pl.BlockSpec(memory_space=pltpu.HBM)
 ANY = pl.BlockSpec(memory_space=pl.ANY)
-LIMIT = 32 * 1024 * 1024
+LIMIT = 16 * 1024 * 1024
 WIDE = 60 * 1024 * 1024
 
 
@@ -528,31 +520,27 @@
     )(where, position_index, table, before)
     main, tail, west = lax.optimization_barrier((main, tail, west))
     from_seam = lax.ppermute(west, "lon", seam)
-    staged = (west, east, first, qkv_second, proj_second)
-    main, tail, west, east, first, w_qkv, w_proj = pl.pallas_call(
+    main, tail = pl.pallas_call(
         late_kernel,
-        out_shape=bias_shapes + tuple(jax.ShapeDtypeStruct(x.shape, x.dtype) for x in staged),
-        in_specs=[SMEM, HBM, HBM, ANY, VMEM, VMEM] + [ANY] * 5,
-        out_specs=(VMEM,) * 7,
-        scratch_shapes=bias_scratch + [pltpu.SemaphoreType.DMA((5,))],
+        out_shape=bias_shapes,
+        in_specs=[SMEM, HBM, HBM, ANY, VMEM, VMEM],
+        out_specs=(VMEM, VMEM),
+        scratch_shapes=bias_scratch,
         compiler_params=params,
         cost_estimate=cost(10**9, 10**7),
         name="late_bias",
-    )(where, position_index, table, before, main, tail, *staged)
-
-    west, east, from_west, from_east, from_seam = lax.optimization_barrier(
-        (west, east, from_west, from_east, from_seam)
-    )
+    )(where, position_index, table, before, main, tail)
+
     pieces = jax.ShapeDtypeStruct((4, 72, D), BF16)
     up, down = pl.pallas_call(
         stack_kernel,
         out_shape=(pieces, pieces),
-        in_specs=[SMEM] + [VMEM] * 5,
+        in_specs=[SMEM] + [VMEM] * 5 + [ANY],
         out_specs=(VMEM, VMEM),
-        compiler_params=params,
+        compiler_params=pltpu.CompilerParams(vmem_limit_bytes=4 * 1024 * 1024),
         cost_estimate=cost(10**5, 10**6),
         name="stack_pieces",
-    )(where, west, east, from_west, from_east, from_seam)
+    )(where, west, east, from_west, from_east, from_seam, main)
     south = shift(up, "lat", -1, False)
     north = shift(down, "lat", 1, False)
 
@@ -565,7 +553,7 @@
         compiler_params=params,
         cost_estimate=cost(10**9, 10**7),
         name="near_half",
-    )(up, down, w_qkv)
+    )(up, down, qkv_second)
 
     edges = jnp.stack([lat > 0, lat < last]).astype(I32)
     out = pl.pallas_call(
@@ -584,7 +572,7 @@
         compiler_params=params,
         cost_estimate=cost(10**9, 5 * 10**6),
         name="second_block",
-    )(edges, first, query, near, north, south, w_qkv, w_proj, main, tail)
+    )(edges, first, query, near, north, south, qkv_second, proj_second, main, tail)
     return out.reshape(6, 12, 4, D).transpose(2, 0, 1, 3)
 
 

time: 61.9 us -> 56.8 us (0.918)
  local copies, waits for them, and re-layouts: 5.13 us -> 0.03 us
  Pallas kernels: 33.6 us -> 30.7 us
  waiting for transfers between devices: 3.56 us -> 6.43 us
    unnamed x28 -> x14, local copies, waits for them, and re-layouts: 5.13 us -> 0.03 us
    ppermute x1, waiting for transfers between devices: 0.01 us -> 1.88 us  [shards(): from_seam = lax.ppermute(west, 'lon', seam)]
    pallas_call x1, Pallas kernels: 1.68 us -> 0.59 us  [shards(): pl.pallas_call(stack_kernel, out_shape=(pieces, pieces), in_specs=[SMEM]...]
    pallas_call x1, Pallas kernels: 2.39 us -> 1.4 us  [shards(): pl.pallas_call(near_kernel, out_shape=(jax.ShapeDtypeStruct((320, D), F32...]
    ppermute x4, waiting for transfers between devices: 3.56 us -> 4.54 us  [shift(): return lax.ppermute(block, axis, route)]
    pallas_call x1, Pallas kernels: 1.51 us -> 0.69 us  [shards(): pl.pallas_call(late_kernel, out_shape=bias_shapes, in_specs=[SMEM, HBM, H...]
    ppermute x4, starting transfers between devices: 12.7 us -> 13.4 us  [shift(): return lax.ppermute(block, axis, route)]
  transfers between devices with their start and end apart: 6 -> 6, of which waited for: 1 -> 2; matrix products, arithmetic and copies ran while one was open for 0% -> 0% of each run, Pallas kernels for 43% -> 43%
where the time goes in v6:
time: 56.8 us; the launch traced here: 56.6 us
  Pallas kernels  30.7 us (54%)
  starting transfers between devices  19.1 us (34%)
  waiting for transfers between devices  6.43 us (11%)
    ppermute x4, starting transfers between devices, shift(): return lax.ppermute(block, axis, route)  13.4 us
    pallas_call x1, Pallas kernels, shards(): pl.pallas_call(first_kernel, out_shape=(jax.ShapeDtypeStruct((288, D), BF...  12.5 us
    pallas_call x1, Pallas kernels, shards(): pl.pallas_call(early_kernel, out_shape=bias_shapes, in_specs=[SMEM, HBM,...  9.91 us
    pallas_call x1, Pallas kernels, shards(): pl.pallas_call(second_kernel, out_shape=jax.ShapeDtypeStruct((72, 4, D),...  5.61 us
    ppermute x4, waiting for transfers between devices, shift(): return lax.ppermute(block, axis, route)  4.54 us
    ppermute x1, starting transfers between devices, shards(): from_seam = lax.ppermute(west, 'lon', seam)  4.38 us
    ppermute x1, waiting for transfers between devices, shards(): from_seam = lax.ppermute(west, 'lon', seam)  1.88 us
    pallas_call x1, Pallas kernels, shards(): pl.pallas_call(near_kernel, out_shape=(jax.ShapeDtypeStruct((320, D), F32...  1.4 us
  transfers between devices with their start and end apart: 6, of which 2 were waited for; matrix products, arithmetic and copies ran while one was open for 0% of the time, Pallas kernels for 43%

profile of v6, /device:TPU:11, one launch (start us, length us, event | category | flops | bytes accessed | tf_op | source)
XLA Modules:
  0.0 56.6 jit_solution(8708738017725825288)
XLA Ops:
  0.0 3.6 %collective-permute-start = (bf16[12,2,3312]{2,1,0:T(2,128)(2,1)}, bf16[12,2,3312]{2,1,0:T(2,128)(2,1)S(1)}, u32[]{:S(2)}, u32[]{:S(2)}) collective-permute-start(bf16[12,2,3312]{2,1,0:T(2,128)(2,1)} %bitcast.17), channel_id=1, source_target_pairs={{0,32},{32,64},{64,96},{96,128},{128,160},{160,192},{192,224},{224... | collective-permute-start | bytes 476936 | tf_op jit(solution)/shard_map/ppermute | solution.py:432
  3.6 0.0 copy-start.3
  3.6 0.0 copy-start.4
  3.6 12.5 %first_block.1 = (bf16[288,384]{1,0:T(8,128)(2,1)}, bf16[2,72,384]{2,1,0:T(8,128)(2,1)}, bf16[2,72,384]{2,1,0:T(8,128)(2,1)}) custom-call(s32[144,144]{1,0:T(8,128)} %idx_in.5, bf16[12,2,3312]{2,1,0:T(2,128)(2,1)} %bitcast.21, bf16[72,4,384]{2,1,0:T(4,128)(2,1)} %bitcast.20, bf16[384,1152]{1,0:T(8,128)(2,1)} %wqkv_in.1, bf16[384,384]{1,0:T(8,128)(2,1)} %wo_in.1, ...), custom_call_target="tpu_custom_call" | custom-call | flops 1000000000 | bytes 3000000 | tf_op jit(solution)/shard_map/first_block/pallas_call | solution.py:454
  16.1 0.0 copy-start.5
  16.1 3.7 %collective-permute-start.1 = (bf16[2,72,384]{2,1,0:T(8,128)(2,1)}, bf16[2,72,384]{2,1,0:T(8,128)(2,1)S(1)}, u32[]{:S(2)}, u32[]{:S(2)}) collective-permute-start(bf16[2,72,384]{2,1,0:T(8,128)(2,1)} %get-tuple-element.28.east_ref), channel_id=1, source_target_pairs={{0,1},{1,2},{2,3},{3,4},{4,5},{5,6},{6,7},{7,8},{8,9},{9,10},{10,1... | collective-permute-start | bytes 331784 | tf_op jit(solution)/shard_map/ppermute | solution.py:432
  19.8 1.3 %collective-permute-start.2 = (bf16[2,72,384]{2,1,0:T(8,128)(2,1)}, bf16[2,72,384]{2,1,0:T(8,128)(2,1)S(1)}, u32[]{:S(2)}, u32[]{:S(2)}) collective-permute-start(bf16[2,72,384]{2,1,0:T(8,128)(2,1)} %get-tuple-element.27.west_ref), channel_id=1, source_target_pairs={{1,0},{2,1},{3,2},{4,3},{5,4},{6,5},{7,6},{8,7},{9,8},{10,9},{11,1... | collective-permute-start | bytes 331784 | tf_op jit(solution)/shard_map/ppermute | solution.py:509
  21.1 0.1 pad_add_fusion.where_ref
  21.2 0.0 collective-permute-done.before_in
  21.2 0.0 copy-done.3
  21.2 0.0 copy-done.4
  21.2 9.9 %early_bias.1 = (s32[2,8,80,128]{3,2,1,0:T(8,128)S(1)}, s32[2,8,128,128]{3,2,1,0:T(8,128)S(1)}) custom-call(s32[3]{0:T(128)S(1)} %pad_add_fusion.where_ref, s32[144,144]{1,0:T(8,128)S(1)} %copy-done.4, bf16[12,2,3312]{2,1,0:T(2,128)(2,1)S(1)} %bitcast.18, bf16[12,2,3312]{2,1,0:T(2,128)(2,1)S(1)} %collective-permute-done.before_in), custom_call_target="tpu_custom_call" | custom-call | flops 1000000 | bytes 100000 | tf_op jit(solution)/shard_map/early_bias/pallas_call | solution.py:511
  31.1 0.0 copy-done.5
  31.1 0.0 copy-start.6
  31.1 4.4 %collective-permute-start.3 = (bf16[2,72,384]{2,1,0:T(8,128)(2,1)S(1)}, bf16[2,72,384]{2,1,0:T(8,128)(2,1)S(1)}, u32[]{:S(2)}, u32[]{:S(2)}) collective-permute-start(bf16[2,72,384]{2,1,0:T(8,128)(2,1)S(1)} %copy-done.5), channel_id=1, source_target_pairs={{0,31},{16,15},{32,63},{48,47},{64,95},{80,79},{96,127},{112,111},... | collective-permute-start | bytes 331784 | tf_op jit(solution)/shard_map/ppermute | solution.py:522
  35.5 0.7 %late_bias.1 = (s32[2,8,80,128]{3,2,1,0:T(8,128)S(1)}, s32[2,8,128,128]{3,2,1,0:T(8,128)S(1)}) custom-call(s32[3]{0:T(128)S(1)} %pad_add_fusion.where_ref, s32[144,144]{1,0:T(8,128)S(1)} %copy-done.4, bf16[12,2,3312]{2,1,0:T(2,128)(2,1)S(1)} %bitcast.19, bf16[12,2,3312]{2,1,0:T(2,128)(2,1)S(1)} %collective-permute-done.before_in, ...), custom_call_target="tpu_custom_call" | custom-call | flops 1000000000 | bytes 10000000 | tf_op jit(solution)/shard_map/late_bias/pallas_call | solution.py:523
  36.2 0.0 copy-start
  36.2 0.0 collective-permute-done.1.from_west_ref
  36.3 0.0 collective-permute-done.2.from_east_ref
  36.3 1.9 %collective-permute-done.3.seam_ref = bf16[2,72,384]{2,1,0:T(8,128)(2,1)S(1)} collective-permute-done((bf16[2,72,384]{2,1,0:T(8,128)(2,1)S(1)}, bf16[2,72,384]{2,1,0:T(8,128)(2,1)S(1)}, u32[]{:S(2)}, u32[]{:S(2)}) %collective-permute-start.3) | collective-permute-done | bytes 110624 | tf_op jit(solution)/shard_map/ppermute | solution.py:522
  38.1 0.0 copy-done.6
  38.1 0.6 %stack_pieces.1 = (bf16[4,72,384]{2,1,0:T(8,128)(2,1)S(1)}, bf16[4,72,384]{2,1,0:T(8,128)(2,1)S(1)}) custom-call(s32[3]{0:T(128)S(1)} %pad_add_fusion.where_ref, bf16[2,72,384]{2,1,0:T(8,128)(2,1)S(1)} %copy-done.5, bf16[2,72,384]{2,1,0:T(8,128)(2,1)S(1)} %copy-done.6, bf16[2,72,384]{2,1,0:T(8,128)(2,1)S(1)} %collective-permute-done.1.from_west_ref, ...), custom_call_target="tpu_custom_call" | custom-call | flops 100000 | bytes 1000000 | tf_op jit(solution)/shard_map/stack_pieces/pallas_call | solution.py:535
  38.7 4.0 %collective-permute-start.4 = (bf16[4,72,384]{2,1,0:T(8,128)(2,1)S(1)}, bf16[4,72,384]{2,1,0:T(8,128)(2,1)S(1)}, u32[]{:S(2)}, u32[]{:S(2)}) collective-permute-start(bf16[4,72,384]{2,1,0:T(8,128)(2,1)S(1)} %get-tuple-element.33.down_ref), channel_id=1, source_target_pairs={{0,32},{32,64},{64,96},{96,128},{128,160},{160,192},{192,224},{224... | collective-permute-start | bytes 663560 | tf_op jit(solution)/shard_map/ppermute | solution.py:432
  42.8 2.1 %collective-permute-start.5 = (bf16[4,72,384]{2,1,0:T(8,128)(2,1)S(1)}, bf16[4,72,384]{2,1,0:T(8,128)(2,1)S(1)}, u32[]{:S(2)}, u32[]{:S(2)}) collective-permute-start(bf16[4,72,384]{2,1,0:T(8,128)(2,1)S(1)} %get-tuple-element.32.up_ref), channel_id=1, source_target_pairs={{32,0},{64,32},{96,64},{128,96},{160,128},{192,160},{224,192},{256... | collective-permute-start | bytes 663560 | tf_op jit(solution)/shard_map/ppermute | solution.py:432
  44.9 0.1 add_convert_fusion.edge_ref
  45.0 0.0 copy-done
  45.0 0.0 copy-start.1
  45.0 0.0 copy-start.2
  45.0 1.4 %near_half.1 = (f32[320,384]{1,0:T(8,128)S(1)}, f32[576,768]{1,0:T(8,128)S(1)}) custom-call(bf16[4,72,384]{2,1,0:T(8,128)(2,1)S(1)} %get-tuple-element.32.up_ref, bf16[4,72,384]{2,1,0:T(8,128)(2,1)S(1)} %get-tuple-element.33.down_ref, bf16[384,1152]{1,0:T(8,128)(2,1)S(1)} %copy-done), custom_call_target="tpu_custom_call" | custom-call | flops 1000000000 | bytes 10000000 | tf_op jit(solution)/shard_map/near_half/pallas_call | solution.py:547
  46.4 0.0 collective-permute-done.4.north_ref
  46.4 4.5 %collective-permute-done.5.south_ref = bf16[4,72,384]{2,1,0:T(8,128)(2,1)S(1)} collective-permute-done((bf16[4,72,384]{2,1,0:T(8,128)(2,1)S(1)}, bf16[4,72,384]{2,1,0:T(8,128)(2,1)S(1)}, u32[]{:S(2)}, u32[]{:S(2)}) %collective-permute-start.5) | collective-permute-done | bytes 221216 | tf_op jit(solution)/shard_map/ppermute | solution.py:432
  50.9 0.0 copy-done.1
  50.9 0.0 copy-done.2
  51.0 5.6 %second_block.1 = bf16[72,4,384]{2,1,0:T(4,128)(2,1)} custom-call(s32[2]{0:T(128)S(1)} %add_convert_fusion.edge_ref, bf16[288,384]{1,0:T(8,128)(2,1)S(1)} %copy-done.2, f32[320,384]{1,0:T(8,128)S(1)} %get-tuple-element.34.query_ref, f32[576,768]{1,0:T(8,128)S(1)} %get-tuple-element.35.near_ref, bf16[4,72,384]{2,1,0:T(8,128)(2,1)S(1)} %collective-permute-done.4.north_ref, ...), custom_call_target="tpu_custom_call" | custom-call | flops 1000000000 | bytes 5000000 | tf_op jit(solution)/shard_map/second_block/pallas_call | solution.py:559
Async XLA Ops:
  0.0 21.2 %collective-permute-start = (bf16[12,2,3312]{2,1,0:T(2,128)(2,1)}, bf16[12,2,3312]{2,1,0:T(2,128)(2,1)S(1)}, u32[]{:S(2)}, u32[]{:S(2)}) collective-permute-start(bf16[12,2,3312]{2,1,0:T(2,128)(2,1)} %bitcast.17), channel_id=1, source_target_pairs={{0,32},{32,64},{64,96},{96,128},{128,160},{160,192},{192,224},{224... | collective-permute-start | bytes 476936 | tf_op jit(solution)/shard_map/ppermute | solution.py:432
  3.6 17.6 %copy-start.3 = (bf16[1,2,12,3312]{3,1,2,0:T(2,128)(2,1)S(1)}, bf16[1,2,12,3312]{3,1,2,0:T(2,128)(2,1)}, u32[]{:S(2)}) copy-start(bf16[1,2,12,3312]{3,1,2,0:T(2,128)(2,1)} %param.19) | copy-start | bytes 476932
  3.6 17.6 %copy-start.4 = (s32[144,144]{1,0:T(8,128)S(1)}, s32[144,144]{1,0:T(8,128)}, u32[]{:S(2)}) copy-start(s32[144,144]{1,0:T(8,128)} %idx_in.5) | copy-start | bytes 248836
  16.1 15.0 %copy-start.5 = (bf16[2,72,384]{2,1,0:T(8,128)(2,1)S(1)}, bf16[2,72,384]{2,1,0:T(8,128)(2,1)}, u32[]{:S(2)}) copy-start(bf16[2,72,384]{2,1,0:T(8,128)(2,1)} %get-tuple-element.27.west_ref) | copy-start | bytes 331780
  16.1 20.1 %collective-permute-start.1 = (bf16[2,72,384]{2,1,0:T(8,128)(2,1)}, bf16[2,72,384]{2,1,0:T(8,128)(2,1)S(1)}, u32[]{:S(2)}, u32[]{:S(2)}) collective-permute-start(bf16[2,72,384]{2,1,0:T(8,128)(2,1)} %get-tuple-element.28.east_ref), channel_id=1, source_target_pairs={{0,1},{1,2},{2,3},{3,4},{4,5},{5,6},{6,7},{7,8},{8,9},{9,10},{10,1... | collective-permute-start | bytes 331784 | tf_op jit(solution)/shard_map/ppermute | solution.py:432
  19.8 16.5 %collective-permute-start.2 = (bf16[2,72,384]{2,1,0:T(8,128)(2,1)}, bf16[2,72,384]{2,1,0:T(8,128)(2,1)S(1)}, u32[]{:S(2)}, u32[]{:S(2)}) collective-permute-start(bf16[2,72,384]{2,1,0:T(8,128)(2,1)} %get-tuple-element.27.west_ref), channel_id=1, source_target_pairs={{1,0},{2,1},{3,2},{4,3},{5,4},{6,5},{7,6},{8,7},{9,8},{10,9},{11,1... | collective-permute-start | bytes 331784 | tf_op jit(solution)/shard_map/ppermute | solution.py:509
  31.1 7.0 %copy-start.6 = (bf16[2,72,384]{2,1,0:T(8,128)(2,1)S(1)}, bf16[2,72,384]{2,1,0:T(8,128)(2,1)}, u32[]{:S(2)}) copy-start(bf16[2,72,384]{2,1,0:T(8,128)(2,1)} %get-tuple-element.28.east_ref) | copy-start | bytes 331780
  31.1 7.0 %collective-permute-start.3 = (bf16[2,72,384]{2,1,0:T(8,128)(2,1)S(1)}, bf16[2,72,384]{2,1,0:T(8,128)(2,1)S(1)}, u32[]{:S(2)}, u32[]{:S(2)}) collective-permute-start(bf16[2,72,384]{2,1,0:T(8,128)(2,1)S(1)} %copy-done.5), channel_id=1, source_target_pairs={{0,31},{16,15},{32,63},{48,47},{64,95},{80,79},{96,127},{112,111},... | collective-permute-start | bytes 331784 | tf_op jit(solution)/shard_map/ppermute | solution.py:522
  36.2 8.8 %copy-start = (bf16[384,1152]{1,0:T(8,128)(2,1)S(1)}, bf16[384,1152]{1,0:T(8,128)(2,1)}, u32[]{:S(2)}) copy-start(bf16[384,1152]{1,0:T(8,128)(2,1)} %wqkv_ref.3) | copy-start | bytes 2654212
  38.7 7.7 %collective-permute-start.4 = (bf16[4,72,384]{2,1,0:T(8,128)(2,1)S(1)}, bf16[4,72,384]{2,1,0:T(8,128)(2,1)S(1)}, u32[]{:S(2)}, u32[]{:S(2)}) collective-permute-start(bf16[4,72,384]{2,1,0:T(8,128)(2,1)S(1)} %get-tuple-element.33.down_ref), channel_id=1, source_target_pairs={{0,32},{32,64},{64,96},{96,128},{128,160},{160,192},{192,224},{224... | collective-permute-start | bytes 663560 | tf_op jit(solution)/shard_map/ppermute | solution.py:432
  42.8 8.2 %collective-permute-start.5 = (bf16[4,72,384]{2,1,0:T(8,128)(2,1)S(1)}, bf16[4,72,384]{2,1,0:T(8,128)(2,1)S(1)}, u32[]{:S(2)}, u32[]{:S(2)}) collective-permute-start(bf16[4,72,384]{2,1,0:T(8,128)(2,1)S(1)} %get-tuple-element.32.up_ref), channel_id=1, source_target_pairs={{32,0},{64,32},{96,64},{128,96},{160,128},{192,160},{224,192},{256... | collective-permute-start | bytes 663560 | tf_op jit(solution)/shard_map/ppermute | solution.py:432
  45.0 6.0 %copy-start.1 = (bf16[384,384]{1,0:T(8,128)(2,1)S(1)}, bf16[384,384]{1,0:T(8,128)(2,1)}, u32[]{:S(2)}) copy-start(bf16[384,384]{1,0:T(8,128)(2,1)} %wo_ref.1) | copy-start | bytes 884740
  45.0 6.0 %copy-start.2 = (bf16[288,384]{1,0:T(8,128)(2,1)S(1)}, bf16[288,384]{1,0:T(8,128)(2,1)}, u32[]{:S(2)}) copy-start(bf16[288,384]{1,0:T(8,128)(2,1)} %get-tuple-element.21.first_ref) | copy-start | bytes 663556

commit v7 on v6

--- a/solution.py
+++ b/solution.py
@@ -446,7 +446,7 @@
 
     part = lax.axis_size("lon") // 2
     place = lax.axis_index("lon") % part
-    where = jnp.stack([lat, (place == 0).astype(lat.dtype), (place == part - 1).astype(lat.dtype)])
+    where = jnp.stack([lat, (place == 0).astype(lat.dtype), (place >= part - 2).astype(lat.dtype)])
     where = where.astype(I32)
     table = bias_second.transpose(0, 2, 1, 3).reshape(HEADS, 2, POS)
     before = shift(table, "lat", 1, False)
@@ -504,8 +504,8 @@
     ]
     from_west = shift(east, "lon", 1, True)
     size = lax.axis_size("lon")
-    inner = [(i, i - 1) for i in range(size) if i % part]
-    seam = [(i, (i - 1) % size) for i in range(size) if i % part == 0]
+    inner = [(i, i - 1) for i in range(size) if 0 < i % part < part - 1]
+    seam = [(i, (i - 1) % size) for i in range(size) if i % part in (0, part - 1)]
     from_east = lax.ppermute(west, "lon", inner)
     before, west = lax.optimization_barrier((before, west))
     main, tail = pl.pallas_call(

time: 56.8 us -> 53.4 us (0.940)
  starting transfers between devices: 19.1 us -> 16.1 us
    ppermute x1, starting transfers between devices: 4.38 us -> 1.69 us  [shards(): from_seam = lax.ppermute(west, 'lon', seam)]
  transfers between devices with their start and end apart: 6 -> 6, of which waited for: 2 -> 2; matrix products, arithmetic and copies ran while one was open for 0% -> 0% of each run, Pallas kernels for 43% -> 46%
where the time goes in v7:
time: 53.4 us; the launch traced here: 53.1 us
  Pallas kernels  30.7 us (57%)
  starting transfers between devices  16.1 us (30%)
  waiting for transfers between devices  5.9 us (11%)
    ppermute x4, starting transfers between devices, shift(): return lax.ppermute(block, axis, route)  13.2 us
    pallas_call x1, Pallas kernels, shards(): pl.pallas_call(first_kernel, out_shape=(jax.ShapeDtypeStruct((288, D), BF...  12.5 us
    pallas_call x1, Pallas kernels, shards(): pl.pallas_call(early_kernel, out_shape=bias_shapes, in_specs=[SMEM, HBM,...  9.91 us
    pallas_call x1, Pallas kernels, shards(): pl.pallas_call(second_kernel, out_shape=jax.ShapeDtypeStruct((72, 4, D),...  5.61 us
    ppermute x4, waiting for transfers between devices, shift(): return lax.ppermute(block, axis, route)  4.55 us
    ppermute x1, starting transfers between devices, shards(): from_seam = lax.ppermute(west, 'lon', seam)  1.69 us
    pallas_call x1, Pallas kernels, shards(): pl.pallas_call(near_kernel, out_shape=(jax.ShapeDtypeStruct((320, D), F32...  1.4 us
    ppermute x1, waiting for transfers between devices, shards(): from_seam = lax.ppermute(west, 'lon', seam)  1.35 us
  transfers between devices with their start and end apart: 6, of which 2 were waited for; matrix products, arithmetic and copies ran while one was open for 0% of the time, Pallas kernels for 46%

profile of v7, /device:TPU:11, one launch (start us, length us, event | category | flops | bytes accessed | tf_op | source)
XLA Modules:
  0.0 53.1 jit_solution(3190845117742462435)
XLA Ops:
  0.0 3.6 %collective-permute-start = (bf16[12,2,3312]{2,1,0:T(2,128)(2,1)}, bf16[12,2,3312]{2,1,0:T(2,128)(2,1)S(1)}, u32[]{:S(2)}, u32[]{:S(2)}) collective-permute-start(bf16[12,2,3312]{2,1,0:T(2,128)(2,1)} %bitcast.17), channel_id=1, source_target_pairs={{0,32},{32,64},{64,96},{96,128},{128,160},{160,192},{192,224},{224... | collective-permute-start | bytes 476936 | tf_op jit(solution)/shard_map/ppermute | solution.py:432
  3.6 0.0 copy-start.3
  3.6 0.0 copy-start.4
  3.6 12.5 %first_block.1 = (bf16[288,384]{1,0:T(8,128)(2,1)}, bf16[2,72,384]{2,1,0:T(8,128)(2,1)}, bf16[2,72,384]{2,1,0:T(8,128)(2,1)}) custom-call(s32[144,144]{1,0:T(8,128)} %idx_in.5, bf16[12,2,3312]{2,1,0:T(2,128)(2,1)} %bitcast.21, bf16[72,4,384]{2,1,0:T(4,128)(2,1)} %bitcast.20, bf16[384,1152]{1,0:T(8,128)(2,1)} %wqkv_in.1, bf16[384,384]{1,0:T(8,128)(2,1)} %wo_in.1, ...), custom_call_target="tpu_custom_call" | custom-call | flops 1000000000 | bytes 3000000 | tf_op jit(solution)/shard_map/first_block/pallas_call | solution.py:454
  16.1 0.0 copy-start.5
  16.1 3.7 %collective-permute-start.1 = (bf16[2,72,384]{2,1,0:T(8,128)(2,1)}, bf16[2,72,384]{2,1,0:T(8,128)(2,1)S(1)}, u32[]{:S(2)}, u32[]{:S(2)}) collective-permute-start(bf16[2,72,384]{2,1,0:T(8,128)(2,1)} %get-tuple-element.28.east_ref), channel_id=1, source_target_pairs={{0,1},{1,2},{2,3},{3,4},{4,5},{5,6},{6,7},{7,8},{8,9},{9,10},{10,1... | collective-permute-start | bytes 331784 | tf_op jit(solution)/shard_map/ppermute | solution.py:432
  19.8 1.3 %collective-permute-start.2 = (bf16[2,72,384]{2,1,0:T(8,128)(2,1)}, bf16[2,72,384]{2,1,0:T(8,128)(2,1)S(1)}, u32[]{:S(2)}, u32[]{:S(2)}) collective-permute-start(bf16[2,72,384]{2,1,0:T(8,128)(2,1)} %get-tuple-element.27.west_ref), channel_id=1, source_target_pairs={{1,0},{2,1},{3,2},{4,3},{5,4},{6,5},{7,6},{8,7},{9,8},{10,9},{11,1... | collective-permute-start | bytes 331784 | tf_op jit(solution)/shard_map/ppermute | solution.py:509
  21.1 0.1 pad_add_fusion.where_ref
  21.2 0.0 collective-permute-done.before_in
  21.2 0.0 copy-done.3
  21.2 0.0 copy-done.4
  21.2 9.9 %early_bias.1 = (s32[2,8,80,128]{3,2,1,0:T(8,128)S(1)}, s32[2,8,128,128]{3,2,1,0:T(8,128)S(1)}) custom-call(s32[3]{0:T(128)S(1)} %pad_add_fusion.where_ref, s32[144,144]{1,0:T(8,128)S(1)} %copy-done.4, bf16[12,2,3312]{2,1,0:T(2,128)(2,1)S(1)} %bitcast.18, bf16[12,2,3312]{2,1,0:T(2,128)(2,1)S(1)} %collective-permute-done.before_in), custom_call_target="tpu_custom_call" | custom-call | flops 1000000 | bytes 100000 | tf_op jit(solution)/shard_map/early_bias/pallas_call | solution.py:511
  31.1 0.0 copy-done.5
  31.1 0.0 copy-start.6
  31.1 1.7 %collective-permute-start.3 = (bf16[2,72,384]{2,1,0:T(8,128)(2,1)S(1)}, bf16[2,72,384]{2,1,0:T(8,128)(2,1)S(1)}, u32[]{:S(2)}, u32[]{:S(2)}) collective-permute-start(bf16[2,72,384]{2,1,0:T(8,128)(2,1)S(1)} %copy-done.5), channel_id=1, source_target_pairs={{0,31},{15,14},{16,15},{31,30},{32,63},{47,46},{48,47},{63,62},{64... | collective-permute-start | bytes 331784 | tf_op jit(solution)/shard_map/ppermute | solution.py:522
  32.8 0.7 %late_bias.1 = (s32[2,8,80,128]{3,2,1,0:T(8,128)S(1)}, s32[2,8,128,128]{3,2,1,0:T(8,128)S(1)}) custom-call(s32[3]{0:T(128)S(1)} %pad_add_fusion.where_ref, s32[144,144]{1,0:T(8,128)S(1)} %copy-done.4, bf16[12,2,3312]{2,1,0:T(2,128)(2,1)S(1)} %bitcast.19, bf16[12,2,3312]{2,1,0:T(2,128)(2,1)S(1)} %collective-permute-done.before_in, ...), custom_call_target="tpu_custom_call" | custom-call | flops 1000000000 | bytes 10000000 | tf_op jit(solution)/shard_map/late_bias/pallas_call | solution.py:523
  33.5 0.0 copy-start
  33.6 0.0 collective-permute-done.1.from_west_ref
  33.6 0.0 collective-permute-done.2.from_east_ref
  33.6 1.4 %collective-permute-done.3.seam_ref = bf16[2,72,384]{2,1,0:T(8,128)(2,1)S(1)} collective-permute-done((bf16[2,72,384]{2,1,0:T(8,128)(2,1)S(1)}, bf16[2,72,384]{2,1,0:T(8,128)(2,1)S(1)}, u32[]{:S(2)}, u32[]{:S(2)}) %collective-permute-start.3) | collective-permute-done | bytes 110624 | tf_op jit(solution)/shard_map/ppermute | solution.py:522
  34.9 0.0 copy-done.6
  34.9 0.6 %stack_pieces.1 = (bf16[4,72,384]{2,1,0:T(8,128)(2,1)S(1)}, bf16[4,72,384]{2,1,0:T(8,128)(2,1)S(1)}) custom-call(s32[3]{0:T(128)S(1)} %pad_add_fusion.where_ref, bf16[2,72,384]{2,1,0:T(8,128)(2,1)S(1)} %copy-done.5, bf16[2,72,384]{2,1,0:T(8,128)(2,1)S(1)} %copy-done.6, bf16[2,72,384]{2,1,0:T(8,128)(2,1)S(1)} %collective-permute-done.1.from_west_ref, ...), custom_call_target="tpu_custom_call" | custom-call | flops 100000 | bytes 1000000 | tf_op jit(solution)/shard_map/stack_pieces/pallas_call | solution.py:535
  35.5 3.8 %collective-permute-start.4 = (bf16[4,72,384]{2,1,0:T(8,128)(2,1)S(1)}, bf16[4,72,384]{2,1,0:T(8,128)(2,1)S(1)}, u32[]{:S(2)}, u32[]{:S(2)}) collective-permute-start(bf16[4,72,384]{2,1,0:T(8,128)(2,1)S(1)} %get-tuple-element.33.down_ref), channel_id=1, source_target_pairs={{0,32},{32,64},{64,96},{96,128},{128,160},{160,192},{192,224},{224... | collective-permute-start | bytes 663560 | tf_op jit(solution)/shard_map/ppermute | solution.py:432
  39.3 2.1 %collective-permute-start.5 = (bf16[4,72,384]{2,1,0:T(8,128)(2,1)S(1)}, bf16[4,72,384]{2,1,0:T(8,128)(2,1)S(1)}, u32[]{:S(2)}, u32[]{:S(2)}) collective-permute-start(bf16[4,72,384]{2,1,0:T(8,128)(2,1)S(1)} %get-tuple-element.32.up_ref), channel_id=1, source_target_pairs={{32,0},{64,32},{96,64},{128,96},{160,128},{192,160},{224,192},{256... | collective-permute-start | bytes 663560 | tf_op jit(solution)/shard_map/ppermute | solution.py:432
  41.5 0.1 add_convert_fusion.edge_ref
  41.5 0.0 copy-done
  41.5 0.0 copy-start.1
  41.5 0.0 copy-start.2
  41.5 1.4 %near_half.1 = (f32[320,384]{1,0:T(8,128)S(1)}, f32[576,768]{1,0:T(8,128)S(1)}) custom-call(bf16[4,72,384]{2,1,0:T(8,128)(2,1)S(1)} %get-tuple-element.32.up_ref, bf16[4,72,384]{2,1,0:T(8,128)(2,1)S(1)} %get-tuple-element.33.down_ref, bf16[384,1152]{1,0:T(8,128)(2,1)S(1)} %copy-done), custom_call_target="tpu_custom_call" | custom-call | flops 1000000000 | bytes 10000000 | tf_op jit(solution)/shard_map/near_half/pallas_call | solution.py:547
  43.0 0.0 collective-permute-done.4.north_ref
  43.0 4.5 %collective-permute-done.5.south_ref = bf16[4,72,384]{2,1,0:T(8,128)(2,1)S(1)} collective-permute-done((bf16[4,72,384]{2,1,0:T(8,128)(2,1)S(1)}, bf16[4,72,384]{2,1,0:T(8,128)(2,1)S(1)}, u32[]{:S(2)}, u32[]{:S(2)}) %collective-permute-start.5) | collective-permute-done | bytes 221216 | tf_op jit(solution)/shard_map/ppermute | solution.py:432
  47.5 0.0 copy-done.1
  47.5 0.0 copy-done.2
  47.5 5.6 %second_block.1 = bf16[72,4,384]{2,1,0:T(4,128)(2,1)} custom-call(s32[2]{0:T(128)S(1)} %add_convert_fusion.edge_ref, bf16[288,384]{1,0:T(8,128)(2,1)S(1)} %copy-done.2, f32[320,384]{1,0:T(8,128)S(1)} %get-tuple-element.34.query_ref, f32[576,768]{1,0:T(8,128)S(1)} %get-tuple-element.35.near_ref, bf16[4,72,384]{2,1,0:T(8,128)(2,1)S(1)} %collective-permute-done.4.north_ref, ...), custom_call_target="tpu_custom_call" | custom-call | flops 1000000000 | bytes 5000000 | tf_op jit(solution)/shard_map/second_block/pallas_call | solution.py:559
Async XLA Ops:
  0.0 21.2 %collective-permute-start = (bf16[12,2,3312]{2,1,0:T(2,128)(2,1)}, bf16[12,2,3312]{2,1,0:T(2,128)(2,1)S(1)}, u32[]{:S(2)}, u32[]{:S(2)}) collective-permute-start(bf16[12,2,3312]{2,1,0:T(2,128)(2,1)} %bitcast.17), channel_id=1, source_target_pairs={{0,32},{32,64},{64,96},{96,128},{128,160},{160,192},{192,224},{224... | collective-permute-start | bytes 476936 | tf_op jit(solution)/shard_map/ppermute | solution.py:432
  3.6 17.6 %copy-start.3 = (bf16[1,2,12,3312]{3,1,2,0:T(2,128)(2,1)S(1)}, bf16[1,2,12,3312]{3,1,2,0:T(2,128)(2,1)}, u32[]{:S(2)}) copy-start(bf16[1,2,12,3312]{3,1,2,0:T(2,128)(2,1)} %param.19) | copy-start | bytes 476932
  3.6 17.6 %copy-start.4 = (s32[144,144]{1,0:T(8,128)S(1)}, s32[144,144]{1,0:T(8,128)}, u32[]{:S(2)}) copy-start(s32[144,144]{1,0:T(8,128)} %idx_in.5) | copy-start | bytes 248836
  16.1 15.0 %copy-start.5 = (bf16[2,72,384]{2,1,0:T(8,128)(2,1)S(1)}, bf16[2,72,384]{2,1,0:T(8,128)(2,1)}, u32[]{:S(2)}) copy-start(bf16[2,72,384]{2,1,0:T(8,128)(2,1)} %get-tuple-element.27.west_ref) | copy-start | bytes 331780
  16.1 17.4 %collective-permute-start.1 = (bf16[2,72,384]{2,1,0:T(8,128)(2,1)}, bf16[2,72,384]{2,1,0:T(8,128)(2,1)S(1)}, u32[]{:S(2)}, u32[]{:S(2)}) collective-permute-start(bf16[2,72,384]{2,1,0:T(8,128)(2,1)} %get-tuple-element.28.east_ref), channel_id=1, source_target_pairs={{0,1},{1,2},{2,3},{3,4},{4,5},{5,6},{6,7},{7,8},{8,9},{9,10},{10,1... | collective-permute-start | bytes 331784 | tf_op jit(solution)/shard_map/ppermute | solution.py:432
  19.8 13.8 %collective-permute-start.2 = (bf16[2,72,384]{2,1,0:T(8,128)(2,1)}, bf16[2,72,384]{2,1,0:T(8,128)(2,1)S(1)}, u32[]{:S(2)}, u32[]{:S(2)}) collective-permute-start(bf16[2,72,384]{2,1,0:T(8,128)(2,1)} %get-tuple-element.27.west_ref), channel_id=1, source_target_pairs={{1,0},{2,1},{3,2},{4,3},{5,4},{6,5},{7,6},{8,7},{9,8},{10,9},{11,1... | collective-permute-start | bytes 331784 | tf_op jit(solution)/shard_map/ppermute | solution.py:509
  31.1 3.8 %copy-start.6 = (bf16[2,72,384]{2,1,0:T(8,128)(2,1)S(1)}, bf16[2,72,384]{2,1,0:T(8,128)(2,1)}, u32[]{:S(2)}) copy-start(bf16[2,72,384]{2,1,0:T(8,128)(2,1)} %get-tuple-element.28.east_ref) | copy-start | bytes 331780
  31.1 3.8 %collective-permute-start.3 = (bf16[2,72,384]{2,1,0:T(8,128)(2,1)S(1)}, bf16[2,72,384]{2,1,0:T(8,128)(2,1)S(1)}, u32[]{:S(2)}, u32[]{:S(2)}) collective-permute-start(bf16[2,72,384]{2,1,0:T(8,128)(2,1)S(1)} %copy-done.5), channel_id=1, source_target_pairs={{0,31},{15,14},{16,15},{31,30},{32,63},{47,46},{48,47},{63,62},{64... | collective-permute-start | bytes 331784 | tf_op jit(solution)/shard_map/ppermute | solution.py:522
  33.5 8.0 %copy-start = (bf16[384,1152]{1,0:T(8,128)(2,1)S(1)}, bf16[384,1152]{1,0:T(8,128)(2,1)}, u32[]{:S(2)}) copy-start(bf16[384,1152]{1,0:T(8,128)(2,1)} %wqkv_ref.3) | copy-start | bytes 2654212
  35.5 7.4 %collective-permute-start.4 = (bf16[4,72,384]{2,1,0:T(8,128)(2,1)S(1)}, bf16[4,72,384]{2,1,0:T(8,128)(2,1)S(1)}, u32[]{:S(2)}, u32[]{:S(2)}) collective-permute-start(bf16[4,72,384]{2,1,0:T(8,128)(2,1)S(1)} %get-tuple-element.33.down_ref), channel_id=1, source_target_pairs={{0,32},{32,64},{64,96},{96,128},{128,160},{160,192},{192,224},{224... | collective-permute-start | bytes 663560 | tf_op jit(solution)/shard_map/ppermute | solution.py:432
  39.3 8.2 %collective-permute-start.5 = (bf16[4,72,384]{2,1,0:T(8,128)(2,1)S(1)}, bf16[4,72,384]{2,1,0:T(8,128)(2,1)S(1)}, u32[]{:S(2)}, u32[]{:S(2)}) collective-permute-start(bf16[4,72,384]{2,1,0:T(8,128)(2,1)S(1)} %get-tuple-element.32.up_ref), channel_id=1, source_target_pairs={{32,0},{64,32},{96,64},{128,96},{160,128},{192,160},{224,192},{256... | collective-permute-start | bytes 663560 | tf_op jit(solution)/shard_map/ppermute | solution.py:432
  41.5 6.0 %copy-start.1 = (bf16[384,384]{1,0:T(8,128)(2,1)S(1)}, bf16[384,384]{1,0:T(8,128)(2,1)}, u32[]{:S(2)}) copy-start(bf16[384,384]{1,0:T(8,128)(2,1)} %wo_ref.1) | copy-start | bytes 884740
  41.5 6.0 %copy-start.2 = (bf16[288,384]{1,0:T(8,128)(2,1)S(1)}, bf16[288,384]{1,0:T(8,128)(2,1)}, u32[]{:S(2)}) copy-start(bf16[288,384]{1,0:T(8,128)(2,1)} %get-tuple-element.21.first_ref) | copy-start | bytes 663556

commit v8 on v7

--- a/solution.py
+++ b/solution.py
@@ -149,34 +149,35 @@
 
 
 def expand(packed_ref, high_ref, low_ref, main_ref, tail_ref, tiles):
-    def picked(t):
-        rows = pl.ds(pl.multiple_of(t * 8, 8), 8)
-        low = low_ref[rows, :]
-        high = high_ref[rows, :]
-        words = [None] * 8
+    def picked(at):
+        low = [low_ref[pl.ds(r, 8), :] for r in at]
+        high = [high_ref[pl.ds(r, 8), :] for r in at]
+        words = [[None] * 8 for _ in at]
         for c in range(CHUNKS):
-            here = high == c
+            here = [x == c for x in high]
             for r in range(8):
                 entries = jnp.broadcast_to(packed_ref[r : r + 1, 128 * c : 128 * c + 128], (8, 128))
-                got = jnp.take_along_axis(entries, low, axis=1, mode="promise_in_bounds")
-                words[r] = got if c == 0 else jnp.where(here, got, words[r])
+                for k in range(len(at)):
+                    got = jnp.take_along_axis(entries, low[k], axis=1, mode="promise_in_bounds")
+                    words[k][r] = got if c == 0 else jnp.where(here[k], got, words[k][r])
         return words
 
     def main(t, carry):
-        for r, words in enumerate(picked(t)):
-            main_ref[r, pl.ds(pl.multiple_of(t * 8, 8), 8), :] = words
+        at = [pl.multiple_of(t * 16, 8), pl.multiple_of(t * 16 + 8, 8)]
+        for start, words in zip(at, picked(at)):
+            for r in range(8):
+                main_ref[r, pl.ds(start, 8), :] = words[r]
         return carry
 
-    def tail(v, carry):
-        for r, words in enumerate(picked(tiles + v)):
-            tail_ref[r, pl.ds(pl.multiple_of(v * 64, 64), 8), :] = words
-            for j in range(1, 8):
-                at = pl.multiple_of(v * 64 + 8 * j, 8)
-                tail_ref[r, pl.ds(at, 8), :] = pltpu.roll(words, 128 - 16 * j, 1)
-        return carry
-
-    lax.fori_loop(0, tiles, main, 0)
-    lax.fori_loop(0, -(-tiles // 8), tail, 0)
+    lax.fori_loop(0, tiles // 2, main, 0)
+    tails = list(range(-(-tiles // 8)))
+    for first in tails[::2]:
+        group = tails[first : first + 2]
+        for v, words in zip(group, picked([8 * (tiles + v) for v in group])):
+            for r in range(8):
+                for j in range(min(8, tiles - 8 * v)):
+                    rolled = words[r] if j == 0 else pltpu.roll(words[r], 128 - 16 * j, 1)
+                    tail_ref[r, 64 * v + 8 * j : 64 * v + 8 * j + 8, :] = rolled
 
 
 def layer_norm(values, gain):
@@ -270,21 +271,10 @@
 
 
 def fill_bias(
-    where_ref, idx_in, table_in, before_in, main_ref, tail_ref,
-    idx_ref, tables, packed, high_ref, low_ref, sems,
+    where_ref, idx_ref, table_ref, before_ref, main_ref, tail_ref, packed, high_ref, low_ref
 ):
-    copies = [
-        pltpu.make_async_copy(src, dst, sems.at[i])
-        for i, (src, dst) in enumerate(
-            ((idx_in, idx_ref), (before_in, tables.at[0]), (table_in, tables.at[1]))
-        )
-    ]
-    for copy in copies:
-        copy.start()
-    for copy in copies:
-        copy.wait()
-    pack_table(tables.at[0], packed.at[0])
-    pack_table(tables.at[1], packed.at[1])
+    pack_table(before_ref, packed.at[0])
+    pack_table(table_ref, packed.at[1])
 
     @pl.when(where_ref[0] == 0)
     def _():
@@ -495,12 +485,9 @@
         jax.ShapeDtypeStruct((2, 8, 128, 128), I32),
     )
     bias_scratch = [
-        pltpu.VMEM((WIN, WIN), I32),
-        pltpu.VMEM((2, HEADS, 2, POS), BF16),
         pltpu.VMEM((2, 8, CHUNKS * 128), I32),
         pltpu.VMEM((2, 96, 128), I32),
         pltpu.VMEM((2, 96, 128), I32),
-        pltpu.SemaphoreType.DMA((3,)),
     ]
     from_west = shift(east, "lon", 1, True)
     size = lax.axis_size("lon")
@@ -511,7 +498,7 @@
     main, tail = pl.pallas_call(
         early_kernel,
         out_shape=bias_shapes,
-        in_specs=[SMEM, HBM, HBM, ANY],
+        in_specs=[SMEM, VMEM, VMEM, VMEM],
         out_specs=(VMEM, VMEM),
         scratch_shapes=bias_scratch,
         compiler_params=params,
@@ -523,7 +510,7 @@
     main, tail = pl.pallas_call(
         late_kernel,
         out_shape=bias_shapes,
-        in_specs=[SMEM, HBM, HBM, ANY, VMEM, VMEM],
+        in_specs=[SMEM] + [VMEM] * 5,
         out_specs=(VMEM, VMEM),
         scratch_shapes=bias_scratch,
         compiler_params=params,

time: 53.4 us -> 52.4 us (0.981)
  Pallas kernels: 30.7 us -> 28.1 us
  starting transfers between devices: 16.1 us -> 17.9 us
    pallas_call x2, Pallas kernels: 10.6 us -> 8.86 us  [the longest x1 8.2 us: shards(): pl.pallas_call(early_kernel, out_shape=bias_shapes, in_specs=[SMEM, VMEM,...]
    ppermute x1, starting transfers between devices: 1.69 us -> 3.38 us  [shards(): from_seam = lax.ppermute(west, 'lon', seam)]
    pallas_call x1, Pallas kernels: 12.5 us -> 11.6 us  [shards(): pl.pallas_call(first_kernel, out_shape=(jax.ShapeDtypeStruct((288, D), BF...]
  transfers between devices with their start and end apart: 6 -> 6, of which waited for: 2 -> 2; matrix products, arithmetic and copies ran while one was open for 0% -> 0% of each run, Pallas kernels for 46% -> 42%
where the time goes in v8:
time: 52.4 us; the launch traced here: 52.2 us
  Pallas kernels  28.1 us (54%)
  starting transfers between devices  17.9 us (34%)
  waiting for transfers between devices  5.89 us (11%)
    ppermute x4, starting transfers between devices, shift(): return lax.ppermute(block, axis, route)  13.2 us
    pallas_call x1, Pallas kernels, shards(): pl.pallas_call(first_kernel, out_shape=(jax.ShapeDtypeStruct((288, D), BF...  11.6 us
    pallas_call x1, Pallas kernels, shards(): pl.pallas_call(early_kernel, out_shape=bias_shapes, in_specs=[SMEM, VMEM,...  8.2 us
    pallas_call x1, Pallas kernels, shards(): pl.pallas_call(second_kernel, out_shape=jax.ShapeDtypeStruct((72, 4, D),...  5.61 us
    ppermute x4, waiting for transfers between devices, shift(): return lax.ppermute(block, axis, route)  4.55 us
    ppermute x1, starting transfers between devices, shards(): from_seam = lax.ppermute(west, 'lon', seam)  3.38 us
    pallas_call x1, Pallas kernels, shards(): pl.pallas_call(near_kernel, out_shape=(jax.ShapeDtypeStruct((320, D), F32...  1.4 us
    ppermute x1, waiting for transfers between devices, shards(): from_seam = lax.ppermute(west, 'lon', seam)  1.35 us
  transfers between devices with their start and end apart: 6, of which 2 were waited for; matrix products, arithmetic and copies ran while one was open for 0% of the time, Pallas kernels for 42%

profile of v8, /device:TPU:11, one launch (start us, length us, event | category | flops | bytes accessed | tf_op | source)
XLA Modules:
  0.0 52.2 jit_solution(286338592108605988)
XLA Ops:
  0.0 3.6 %collective-permute-start = (bf16[12,2,3312]{2,1,0:T(2,128)(2,1)}, bf16[12,2,3312]{2,1,0:T(2,128)(2,1)S(1)}, u32[]{:S(2)}, u32[]{:S(2)}) collective-permute-start(bf16[12,2,3312]{2,1,0:T(2,128)(2,1)} %bitcast.17), channel_id=1, source_target_pairs={{0,32},{32,64},{64,96},{96,128},{128,160},{160,192},{192,224},{224... | collective-permute-start | bytes 476936 | tf_op jit(solution)/shard_map/ppermute | solution.py:422
  3.6 0.0 copy-start.3
  3.6 0.0 copy-start.4
  3.6 11.6 %first_block.1 = (bf16[288,384]{1,0:T(8,128)(2,1)}, bf16[2,72,384]{2,1,0:T(8,128)(2,1)}, bf16[2,72,384]{2,1,0:T(8,128)(2,1)}) custom-call(s32[144,144]{1,0:T(8,128)} %idx_in.5, bf16[12,2,3312]{2,1,0:T(2,128)(2,1)} %bitcast.21, bf16[72,4,384]{2,1,0:T(4,128)(2,1)} %bitcast.20, bf16[384,1152]{1,0:T(8,128)(2,1)} %wqkv_in.1, bf16[384,384]{1,0:T(8,128)(2,1)} %wo_in.1, ...), custom_call_target="tpu_custom_call" | custom-call | flops 1000000000 | bytes 3000000 | tf_op jit(solution)/shard_map/first_block/pallas_call | solution.py:444
  15.2 0.0 copy-start.5
  15.2 3.7 %collective-permute-start.1 = (bf16[2,72,384]{2,1,0:T(8,128)(2,1)}, bf16[2,72,384]{2,1,0:T(8,128)(2,1)S(1)}, u32[]{:S(2)}, u32[]{:S(2)}) collective-permute-start(bf16[2,72,384]{2,1,0:T(8,128)(2,1)} %get-tuple-element.28.east_ref), channel_id=1, source_target_pairs={{0,1},{1,2},{2,3},{3,4},{4,5},{5,6},{6,7},{7,8},{8,9},{9,10},{10,1... | collective-permute-start | bytes 331784 | tf_op jit(solution)/shard_map/ppermute | solution.py:422
  18.9 1.3 %collective-permute-start.2 = (bf16[2,72,384]{2,1,0:T(8,128)(2,1)}, bf16[2,72,384]{2,1,0:T(8,128)(2,1)S(1)}, u32[]{:S(2)}, u32[]{:S(2)}) collective-permute-start(bf16[2,72,384]{2,1,0:T(8,128)(2,1)} %get-tuple-element.27.west_ref), channel_id=1, source_target_pairs={{1,0},{2,1},{3,2},{4,3},{5,4},{6,5},{7,6},{8,7},{9,8},{10,9},{11,1... | collective-permute-start | bytes 331784 | tf_op jit(solution)/shard_map/ppermute | solution.py:496
  20.2 0.1 pad_add_fusion.where_ref
  20.3 0.0 collective-permute-done.before_in
  20.3 0.0 copy-done.3
  20.3 0.0 copy-done.4
  20.3 8.2 %early_bias.1 = (s32[2,8,80,128]{3,2,1,0:T(8,128)S(1)}, s32[2,8,128,128]{3,2,1,0:T(8,128)S(1)}) custom-call(s32[3]{0:T(128)S(1)} %pad_add_fusion.where_ref, s32[144,144]{1,0:T(8,128)S(1)} %copy-done.4, bf16[12,2,3312]{2,1,0:T(2,128)(2,1)S(1)} %bitcast.18, bf16[12,2,3312]{2,1,0:T(2,128)(2,1)S(1)} %collective-permute-done.before_in), custom_call_target="tpu_custom_call" | custom-call | flops 1000000 | bytes 100000 | tf_op jit(solution)/shard_map/early_bias/pallas_call | solution.py:498
  28.5 0.0 copy-done.5
  28.5 0.0 copy-start.6
  28.5 3.4 %collective-permute-start.3 = (bf16[2,72,384]{2,1,0:T(8,128)(2,1)S(1)}, bf16[2,72,384]{2,1,0:T(8,128)(2,1)S(1)}, u32[]{:S(2)}, u32[]{:S(2)}) collective-permute-start(bf16[2,72,384]{2,1,0:T(8,128)(2,1)S(1)} %copy-done.5), channel_id=1, source_target_pairs={{0,31},{15,14},{16,15},{31,30},{32,63},{47,46},{48,47},{63,62},{64... | collective-permute-start | bytes 331784 | tf_op jit(solution)/shard_map/ppermute | solution.py:509
  31.9 0.7 %late_bias.1 = (s32[2,8,80,128]{3,2,1,0:T(8,128)S(1)}, s32[2,8,128,128]{3,2,1,0:T(8,128)S(1)}) custom-call(s32[3]{0:T(128)S(1)} %pad_add_fusion.where_ref, s32[144,144]{1,0:T(8,128)S(1)} %copy-done.4, bf16[12,2,3312]{2,1,0:T(2,128)(2,1)S(1)} %bitcast.19, bf16[12,2,3312]{2,1,0:T(2,128)(2,1)S(1)} %collective-permute-done.before_in, ...), custom_call_target="tpu_custom_call" | custom-call | flops 1000000000 | bytes 10000000 | tf_op jit(solution)/shard_map/late_bias/pallas_call | solution.py:510
  32.6 0.0 copy-start
  32.6 0.0 collective-permute-done.1.from_west_ref
  32.6 0.0 collective-permute-done.2.from_east_ref
  32.6 1.3 %collective-permute-done.3.seam_ref = bf16[2,72,384]{2,1,0:T(8,128)(2,1)S(1)} collective-permute-done((bf16[2,72,384]{2,1,0:T(8,128)(2,1)S(1)}, bf16[2,72,384]{2,1,0:T(8,128)(2,1)S(1)}, u32[]{:S(2)}, u32[]{:S(2)}) %collective-permute-start.3) | collective-permute-done | bytes 110624 | tf_op jit(solution)/shard_map/ppermute | solution.py:509
  34.0 0.0 copy-done.6
  34.0 0.6 %stack_pieces.1 = (bf16[4,72,384]{2,1,0:T(8,128)(2,1)S(1)}, bf16[4,72,384]{2,1,0:T(8,128)(2,1)S(1)}) custom-call(s32[3]{0:T(128)S(1)} %pad_add_fusion.where_ref, bf16[2,72,384]{2,1,0:T(8,128)(2,1)S(1)} %copy-done.5, bf16[2,72,384]{2,1,0:T(8,128)(2,1)S(1)} %copy-done.6, bf16[2,72,384]{2,1,0:T(8,128)(2,1)S(1)} %collective-permute-done.1.from_west_ref, ...), custom_call_target="tpu_custom_call" | custom-call | flops 100000 | bytes 1000000 | tf_op jit(solution)/shard_map/stack_pieces/pallas_call | solution.py:522
  34.6 3.9 %collective-permute-start.4 = (bf16[4,72,384]{2,1,0:T(8,128)(2,1)S(1)}, bf16[4,72,384]{2,1,0:T(8,128)(2,1)S(1)}, u32[]{:S(2)}, u32[]{:S(2)}) collective-permute-start(bf16[4,72,384]{2,1,0:T(8,128)(2,1)S(1)} %get-tuple-element.33.down_ref), channel_id=1, source_target_pairs={{0,32},{32,64},{64,96},{96,128},{128,160},{160,192},{192,224},{224... | collective-permute-start | bytes 663560 | tf_op jit(solution)/shard_map/ppermute | solution.py:422
  38.4 2.1 %collective-permute-start.5 = (bf16[4,72,384]{2,1,0:T(8,128)(2,1)S(1)}, bf16[4,72,384]{2,1,0:T(8,128)(2,1)S(1)}, u32[]{:S(2)}, u32[]{:S(2)}) collective-permute-start(bf16[4,72,384]{2,1,0:T(8,128)(2,1)S(1)} %get-tuple-element.32.up_ref), channel_id=1, source_target_pairs={{32,0},{64,32},{96,64},{128,96},{160,128},{192,160},{224,192},{256... | collective-permute-start | bytes 663560 | tf_op jit(solution)/shard_map/ppermute | solution.py:422
  40.5 0.1 add_convert_fusion.edge_ref
  40.6 0.0 copy-done
  40.6 0.0 copy-start.1
  40.6 0.0 copy-start.2
  40.6 1.4 %near_half.1 = (f32[320,384]{1,0:T(8,128)S(1)}, f32[576,768]{1,0:T(8,128)S(1)}) custom-call(bf16[4,72,384]{2,1,0:T(8,128)(2,1)S(1)} %get-tuple-element.32.up_ref, bf16[4,72,384]{2,1,0:T(8,128)(2,1)S(1)} %get-tuple-element.33.down_ref, bf16[384,1152]{1,0:T(8,128)(2,1)S(1)} %copy-done), custom_call_target="tpu_custom_call" | custom-call | flops 1000000000 | bytes 10000000 | tf_op jit(solution)/shard_map/near_half/pallas_call | solution.py:534
  42.0 0.0 collective-permute-done.4.north_ref
  42.0 4.5 %collective-permute-done.5.south_ref = bf16[4,72,384]{2,1,0:T(8,128)(2,1)S(1)} collective-permute-done((bf16[4,72,384]{2,1,0:T(8,128)(2,1)S(1)}, bf16[4,72,384]{2,1,0:T(8,128)(2,1)S(1)}, u32[]{:S(2)}, u32[]{:S(2)}) %collective-permute-start.5) | collective-permute-done | bytes 221216 | tf_op jit(solution)/shard_map/ppermute | solution.py:422
  46.6 0.0 copy-done.1
  46.6 0.0 copy-done.2
  46.6 5.6 %second_block.1 = bf16[72,4,384]{2,1,0:T(4,128)(2,1)} custom-call(s32[2]{0:T(128)S(1)} %add_convert_fusion.edge_ref, bf16[288,384]{1,0:T(8,128)(2,1)S(1)} %copy-done.2, f32[320,384]{1,0:T(8,128)S(1)} %get-tuple-element.34.query_ref, f32[576,768]{1,0:T(8,128)S(1)} %get-tuple-element.35.near_ref, bf16[4,72,384]{2,1,0:T(8,128)(2,1)S(1)} %collective-permute-done.4.north_ref, ...), custom_call_target="tpu_custom_call" | custom-call | flops 1000000000 | bytes 5000000 | tf_op jit(solution)/shard_map/second_block/pallas_call | solution.py:546
Async XLA Ops:
  0.0 20.3 %collective-permute-start = (bf16[12,2,3312]{2,1,0:T(2,128)(2,1)}, bf16[12,2,3312]{2,1,0:T(2,128)(2,1)S(1)}, u32[]{:S(2)}, u32[]{:S(2)}) collective-permute-start(bf16[12,2,3312]{2,1,0:T(2,128)(2,1)} %bitcast.17), channel_id=1, source_target_pairs={{0,32},{32,64},{64,96},{96,128},{128,160},{160,192},{192,224},{224... | collective-permute-start | bytes 476936 | tf_op jit(solution)/shard_map/ppermute | solution.py:422
  3.6 16.7 %copy-start.3 = (bf16[1,2,12,3312]{3,1,2,0:T(2,128)(2,1)S(1)}, bf16[1,2,12,3312]{3,1,2,0:T(2,128)(2,1)}, u32[]{:S(2)}) copy-start(bf16[1,2,12,3312]{3,1,2,0:T(2,128)(2,1)} %param.19) | copy-start | bytes 476932
  3.6 16.7 %copy-start.4 = (s32[144,144]{1,0:T(8,128)S(1)}, s32[144,144]{1,0:T(8,128)}, u32[]{:S(2)}) copy-start(s32[144,144]{1,0:T(8,128)} %idx_in.5) | copy-start | bytes 248836
  15.2 13.3 %copy-start.5 = (bf16[2,72,384]{2,1,0:T(8,128)(2,1)S(1)}, bf16[2,72,384]{2,1,0:T(8,128)(2,1)}, u32[]{:S(2)}) copy-start(bf16[2,72,384]{2,1,0:T(8,128)(2,1)} %get-tuple-element.27.west_ref) | copy-start | bytes 331780
  15.2 17.4 %collective-permute-start.1 = (bf16[2,72,384]{2,1,0:T(8,128)(2,1)}, bf16[2,72,384]{2,1,0:T(8,128)(2,1)S(1)}, u32[]{:S(2)}, u32[]{:S(2)}) collective-permute-start(bf16[2,72,384]{2,1,0:T(8,128)(2,1)} %get-tuple-element.28.east_ref), channel_id=1, source_target_pairs={{0,1},{1,2},{2,3},{3,4},{4,5},{5,6},{6,7},{7,8},{8,9},{9,10},{10,1... | collective-permute-start | bytes 331784 | tf_op jit(solution)/shard_map/ppermute | solution.py:422
  18.9 13.7 %collective-permute-start.2 = (bf16[2,72,384]{2,1,0:T(8,128)(2,1)}, bf16[2,72,384]{2,1,0:T(8,128)(2,1)S(1)}, u32[]{:S(2)}, u32[]{:S(2)}) collective-permute-start(bf16[2,72,384]{2,1,0:T(8,128)(2,1)} %get-tuple-element.27.west_ref), channel_id=1, source_target_pairs={{1,0},{2,1},{3,2},{4,3},{5,4},{6,5},{7,6},{8,7},{9,8},{10,9},{11,1... | collective-permute-start | bytes 331784 | tf_op jit(solution)/shard_map/ppermute | solution.py:496
  28.5 5.4 %copy-start.6 = (bf16[2,72,384]{2,1,0:T(8,128)(2,1)S(1)}, bf16[2,72,384]{2,1,0:T(8,128)(2,1)}, u32[]{:S(2)}) copy-start(bf16[2,72,384]{2,1,0:T(8,128)(2,1)} %get-tuple-element.28.east_ref) | copy-start | bytes 331780
  28.5 5.4 %collective-permute-start.3 = (bf16[2,72,384]{2,1,0:T(8,128)(2,1)S(1)}, bf16[2,72,384]{2,1,0:T(8,128)(2,1)S(1)}, u32[]{:S(2)}, u32[]{:S(2)}) collective-permute-start(bf16[2,72,384]{2,1,0:T(8,128)(2,1)S(1)} %copy-done.5), channel_id=1, source_target_pairs={{0,31},{15,14},{16,15},{31,30},{32,63},{47,46},{48,47},{63,62},{64... | collective-permute-start | bytes 331784 | tf_op jit(solution)/shard_map/ppermute | solution.py:509
  32.6 8.0 %copy-start = (bf16[384,1152]{1,0:T(8,128)(2,1)S(1)}, bf16[384,1152]{1,0:T(8,128)(2,1)}, u32[]{:S(2)}) copy-start(bf16[384,1152]{1,0:T(8,128)(2,1)} %wqkv_ref.3) | copy-start | bytes 2654212
  34.6 7.5 %collective-permute-start.4 = (bf16[4,72,384]{2,1,0:T(8,128)(2,1)S(1)}, bf16[4,72,384]{2,1,0:T(8,128)(2,1)S(1)}, u32[]{:S(2)}, u32[]{:S(2)}) collective-permute-start(bf16[4,72,384]{2,1,0:T(8,128)(2,1)S(1)} %get-tuple-element.33.down_ref), channel_id=1, source_target_pairs={{0,32},{32,64},{64,96},{96,128},{128,160},{160,192},{192,224},{224... | collective-permute-start | bytes 663560 | tf_op jit(solution)/shard_map/ppermute | solution.py:422
  38.4 8.2 %collective-permute-start.5 = (bf16[4,72,384]{2,1,0:T(8,128)(2,1)S(1)}, bf16[4,72,384]{2,1,0:T(8,128)(2,1)S(1)}, u32[]{:S(2)}, u32[]{:S(2)}) collective-permute-start(bf16[4,72,384]{2,1,0:T(8,128)(2,1)S(1)} %get-tuple-element.32.up_ref), channel_id=1, source_target_pairs={{32,0},{64,32},{96,64},{128,96},{160,128},{192,160},{224,192},{256... | collective-permute-start | bytes 663560 | tf_op jit(solution)/shard_map/ppermute | solution.py:422
  40.6 6.0 %copy-start.1 = (bf16[384,384]{1,0:T(8,128)(2,1)S(1)}, bf16[384,384]{1,0:T(8,128)(2,1)}, u32[]{:S(2)}) copy-start(bf16[384,384]{1,0:T(8,128)(2,1)} %wo_ref.1) | copy-start | bytes 884740
  40.6 6.0 %copy-start.2 = (bf16[288,384]{1,0:T(8,128)(2,1)S(1)}, bf16[288,384]{1,0:T(8,128)(2,1)}, u32[]{:S(2)}) copy-start(bf16[288,384]{1,0:T(8,128)(2,1)} %get-tuple-element.21.first_ref) | copy-start | bytes 663556
